TPU v7x, 32 devices: a whole 2x2x4 slice. The times are simulated.
32 devices in a mesh: tm: 8 (over y, x, core), space: 4 (over z).
Axes of the slice: x: 2, y: 2, z: 4, core: 2. Of those that a mesh axis runs over, the one named last changes fastest.
Arguments:
- frames_in: bfloat16 [8, 128, 128, 256], P('tm', 'space'), may hold values from -6 to 6
- w_input: bfloat16 [3, 3, 256, 256], replicated, may hold values from -0.125 to 0.125
- decay_rate: float32 [128], replicated, may hold values from 0.001 to 0.2
- phase: float32 [128], replicated, may hold values from -3.140625 to 3.140625
- w_output: bfloat16 [3, 3, 256, 256], replicated, may hold values from -0.125 to 0.125
Outputs:
- frames_out: bfloat16 [8, 128, 128, 256], P('tm', 'space')
All inputs are finite; a program needn't handle non-finite values.
Results may differ from a plain program's by a relative error of at most 0.0029.
Values may be sent and summed in bfloat16 or wider, within the bound.
No kernel may reach another device: no remote copies, remote signals or barrier semaphores. Data moves between devices by JAX's collectives and lax.ppermute only.
A program may use at most 192 MiB of HBM per device.

v0:
```python
import jax
import jax.numpy as jnp
from jax import lax
from jax.sharding import PartitionSpec as P


def with_halo(block, sides, width):
    for axis, dim in sides:
        count = lax.axis_size(axis)
        forward = [(i, i + 1) for i in range(count - 1)]
        backward = [(target, source) for source, target in forward]
        low = lax.ppermute(
            lax.slice_in_dim(block, block.shape[dim] - width, None, axis=dim), axis, forward
        )
        high = lax.ppermute(lax.slice_in_dim(block, 0, width, axis=dim), axis, backward)
        block = jnp.concatenate([low, block, high], axis=dim)
    return block


def convolve_valid(padded, kernel):
    return lax.conv_general_dilated(
        padded,
        kernel,
        (1, 1),
        ((0, 0), (0, 0)),
        dimension_numbers=("NHWC", "HWIO", "NHWC"),
        preferred_element_type=jnp.float32,
    )


def local_recurrence(drive, decay_rate, phase):
    states_n = decay_rate.shape[0]
    magnitude = jnp.exp(-decay_rate)
    lam_re = magnitude * jnp.cos(phase)
    lam_im = magnitude * jnp.sin(phase)
    factor = jnp.sqrt(1.0 - magnitude * magnitude)
    feed = drive * jnp.concatenate([factor, factor])

    def advance(carry, item):
        prev_re, prev_im = carry
        new_re = lam_re * prev_re - lam_im * prev_im + item[..., :states_n]
        new_im = lam_re * prev_im + lam_im * prev_re + item[..., states_n:]
        return ((new_re, new_im), (new_re, new_im))

    start = jnp.zeros(feed.shape[1:3] + (states_n,), jnp.float32)
    return lax.scan(advance, (start, start), feed)


def on_device(frames_in, w_input, decay_rate, phase, w_output):
    strips = lax.all_to_all(frames_in, "tm", split_axis=2, concat_axis=0, tiled=True)
    padded = with_halo(strips, (("tm", 2), ("space", 1)), 1)
    drive = convolve_valid(padded, w_input)
    ends, locals_all = local_recurrence(drive, decay_rate, phase)
    state_b = jnp.concatenate([locals_all[0], locals_all[1]], axis=-1).astype(jnp.bfloat16)
    padded_state = with_halo(state_b, (("tm", 2), ("space", 1)), 1)
    mixed = convolve_valid(padded_state, w_output)
    result = (strips.astype(jnp.float32) + jax.nn.gelu(mixed, approximate=False)).astype(
        jnp.bfloat16
    )
    return lax.all_to_all(result, "tm", split_axis=0, concat_axis=2, tiled=True)


def solution(mesh):
    in_specs = (P("tm", "space", None, None), P(), P(), P(), P())
    out_specs = P("tm", "space", None, None)
    return jax.shard_map(
        on_device, mesh=mesh, in_specs=in_specs, out_specs=out_specs, check_vma=False
    )
```

profile of v0, /device:TPU:0, one launch (start us, length us, event | category | flops | bytes accessed | tf_op | source)
XLA Modules:
  0.0 255.6 jit_solution(5553172015022559004)
XLA Ops:
  4.2 5.3 %all-to-all-start = ((bf16[1,32,128,256]{3,1,0,2:T(8,128)(2,1)}), bf16[1,32,128,256]{3,1,0,2:T(8,128)(2,1)}, u32[]{:S(2)}, u32[]{:S(2)}) async-start(bf16[1,32,128,256]{3,1,0,2:T(8,128)(2,1)} %copy.14), calls=%async_computation | async-start | bytes 4194304 | tf_op jit(solution)/shard_map/all_to_all | solution.py:50
  9.5 26.7 %all-to-all-done = bf16[1,32,128,256]{3,1,0,2:T(8,128)(2,1)} async-done(((bf16[1,32,128,256]{3,1,0,2:T(8,128)(2,1)}), bf16[1,32,128,256]{3,1,0,2:T(8,128)(2,1)}, u32[]{:S(2)}, u32[]{:S(2)}) %all-to-all-start) | async-done | bytes 2097184 | tf_op jit(solution)/shard_map/all_to_all | solution.py:50
  50.4 4.3 %collective-permute-done.3 = bf16[8,1,18,256]{3,0,2,1:T(8,128)(2,1)S(1)} collective-permute-done((bf16[8,1,18,256]{3,0,2,1:T(8,128)(2,1)S(1)}, bf16[8,1,18,256]{3,0,2,1:T(8,128)(2,1)S(1)}, u32[]{:S(2)}, u32[]{:S(2)}) %collective-permute-start.3) | collective-permute-done | bytes 73760 | tf_op jit(solution)/shard_map/ppermute | solution.py:15
  54.6 6.6 %fusion.35 = f32[8,32,16,256]{3,0,2,1:T(8,128)} fusion(bf16[3,3,256,256]{3,2,1,0:T(8,128)(2,1)S(1)} %copy-done, bf16[8,1,18,256]{3,0,2,1:T(8,128)(2,1)S(1)} %collective-permute-done.3, bf16[8,32,1,256]{3,0,2,1:T(8,128)(2,1)S(1)} %collective-permute-done.1, bf16[8,32,16,256]{3,0,2,1:T(8,128)(2,1)S(1)} %bitcast.35, ...), kind=kOutput, calls=%fused_computation.46 | convolution fusion | flops 4837900288 | bytes 7881728 | tf_op jit(solution)/shard_map/conv_general_dilated | solution.py:21
  61.3 124.0 %while.17 = (s32[]{:T(128)}, f32[32,16,128]{2,1,0:T(8,128)S(1)}, f32[32,16,128]{2,1,0:T(8,128)S(1)}, bf16[8,32,16,128]{3,0,2,1:T(8,128)(2,1)}, bf16[8,32,16,128]...) while((s32[]{:T(128)}, f32[32,16,128]{2,1,0:T(8,128)S(1)}, ...), condition=%wide.region_1.2_spmd.clone, body=%wide.region_0.1_spmd.clone.sunk | while | flops 655363 | bytes 4719747 | solution.py:46
  64.2 5.1 %dynamic_update_slice.12 = bf16[8,32,16,128]{3,0,2,1:T(8,128)(2,1)S(1)} dynamic-update-slice(bf16[8,32,16,128]{3,0,2,1:T(8,128)(2,1)S(1)} %get-tuple-element.197, f32[1,32,16,128]{3,0,2,1:T(1,128)S(1)} %bitcast.31, s32[]{:T(128)S(6)} %copy.44, s32[]{:T(128)} %constant.37.clone.1..sunk, s32[]{:T(128)} %constant.37.clone.1..sunk, s32[]{:T(128)} %constant.37.clone.1..sunk) | dynamic-update-slice | bytes 524292 | tf_op jit(solution)/shard_map/while/body/jit(dynamic_update_index_in_dim)/dynamic_update_slice | solution.py:46
  69.3 7.5 %dynamic_update_slice.11 = bf16[8,32,16,128]{3,0,2,1:T(8,128)(2,1)} dynamic-update-slice(bf16[8,32,16,128]{3,0,2,1:T(8,128)(2,1)} %get-tuple-element.196, f32[1,32,16,128]{3,0,2,1:T(1,128)S(1)} %bitcast.32, s32[]{:T(128)S(6)} %copy.44, s32[]{:T(128)} %constant.37.clone.1..sunk, s32[]{:T(128)} %constant.37.clone.1..sunk, s32[]{:T(128)} %constant.37.clone.1..sunk) | dynamic-update-slice | bytes 524292 | tf_op jit(solution)/shard_map/while/body/jit(dynamic_update_index_in_dim)/dynamic_update_slice | solution.py:46
  79.7 5.1 %dynamic_update_slice.12 = bf16[8,32,16,128]{3,0,2,1:T(8,128)(2,1)S(1)} dynamic-update-slice(bf16[8,32,16,128]{3,0,2,1:T(8,128)(2,1)S(1)} %get-tuple-element.197, f32[1,32,16,128]{3,0,2,1:T(1,128)S(1)} %bitcast.31, s32[]{:T(128)S(6)} %copy.44, s32[]{:T(128)} %constant.37.clone.1..sunk, s32[]{:T(128)} %constant.37.clone.1..sunk, s32[]{:T(128)} %constant.37.clone.1..sunk) | dynamic-update-slice | bytes 524292 | tf_op jit(solution)/shard_map/while/body/jit(dynamic_update_index_in_dim)/dynamic_update_slice | solution.py:46
  84.8 7.5 %dynamic_update_slice.11 = bf16[8,32,16,128]{3,0,2,1:T(8,128)(2,1)} dynamic-update-slice(bf16[8,32,16,128]{3,0,2,1:T(8,128)(2,1)} %get-tuple-element.196, f32[1,32,16,128]{3,0,2,1:T(1,128)S(1)} %bitcast.32, s32[]{:T(128)S(6)} %copy.44, s32[]{:T(128)} %constant.37.clone.1..sunk, s32[]{:T(128)} %constant.37.clone.1..sunk, s32[]{:T(128)} %constant.37.clone.1..sunk) | dynamic-update-slice | bytes 524292 | tf_op jit(solution)/shard_map/while/body/jit(dynamic_update_index_in_dim)/dynamic_update_slice | solution.py:46
  95.2 5.1 %dynamic_update_slice.12 = bf16[8,32,16,128]{3,0,2,1:T(8,128)(2,1)S(1)} dynamic-update-slice(bf16[8,32,16,128]{3,0,2,1:T(8,128)(2,1)S(1)} %get-tuple-element.197, f32[1,32,16,128]{3,0,2,1:T(1,128)S(1)} %bitcast.31, s32[]{:T(128)S(6)} %copy.44, s32[]{:T(128)} %constant.37.clone.1..sunk, s32[]{:T(128)} %constant.37.clone.1..sunk, s32[]{:T(128)} %constant.37.clone.1..sunk) | dynamic-update-slice | bytes 524292 | tf_op jit(solution)/shard_map/while/body/jit(dynamic_update_index_in_dim)/dynamic_update_slice | solution.py:46
  100.3 7.5 %dynamic_update_slice.11 = bf16[8,32,16,128]{3,0,2,1:T(8,128)(2,1)} dynamic-update-slice(bf16[8,32,16,128]{3,0,2,1:T(8,128)(2,1)} %get-tuple-element.196, f32[1,32,16,128]{3,0,2,1:T(1,128)S(1)} %bitcast.32, s32[]{:T(128)S(6)} %copy.44, s32[]{:T(128)} %constant.37.clone.1..sunk, s32[]{:T(128)} %constant.37.clone.1..sunk, s32[]{:T(128)} %constant.37.clone.1..sunk) | dynamic-update-slice | bytes 524292 | tf_op jit(solution)/shard_map/while/body/jit(dynamic_update_index_in_dim)/dynamic_update_slice | solution.py:46
  110.7 5.1 %dynamic_update_slice.12 = bf16[8,32,16,128]{3,0,2,1:T(8,128)(2,1)S(1)} dynamic-update-slice(bf16[8,32,16,128]{3,0,2,1:T(8,128)(2,1)S(1)} %get-tuple-element.197, f32[1,32,16,128]{3,0,2,1:T(1,128)S(1)} %bitcast.31, s32[]{:T(128)S(6)} %copy.44, s32[]{:T(128)} %constant.37.clone.1..sunk, s32[]{:T(128)} %constant.37.clone.1..sunk, s32[]{:T(128)} %constant.37.clone.1..sunk) | dynamic-update-slice | bytes 524292 | tf_op jit(solution)/shard_map/while/body/jit(dynamic_update_index_in_dim)/dynamic_update_slice | solution.py:46
  115.8 7.5 %dynamic_update_slice.11 = bf16[8,32,16,128]{3,0,2,1:T(8,128)(2,1)} dynamic-update-slice(bf16[8,32,16,128]{3,0,2,1:T(8,128)(2,1)} %get-tuple-element.196, f32[1,32,16,128]{3,0,2,1:T(1,128)S(1)} %bitcast.32, s32[]{:T(128)S(6)} %copy.44, s32[]{:T(128)} %constant.37.clone.1..sunk, s32[]{:T(128)} %constant.37.clone.1..sunk, s32[]{:T(128)} %constant.37.clone.1..sunk) | dynamic-update-slice | bytes 524292 | tf_op jit(solution)/shard_map/while/body/jit(dynamic_update_index_in_dim)/dynamic_update_slice | solution.py:46
  126.2 5.1 %dynamic_update_slice.12 = bf16[8,32,16,128]{3,0,2,1:T(8,128)(2,1)S(1)} dynamic-update-slice(bf16[8,32,16,128]{3,0,2,1:T(8,128)(2,1)S(1)} %get-tuple-element.197, f32[1,32,16,128]{3,0,2,1:T(1,128)S(1)} %bitcast.31, s32[]{:T(128)S(6)} %copy.44, s32[]{:T(128)} %constant.37.clone.1..sunk, s32[]{:T(128)} %constant.37.clone.1..sunk, s32[]{:T(128)} %constant.37.clone.1..sunk) | dynamic-update-slice | bytes 524292 | tf_op jit(solution)/shard_map/while/body/jit(dynamic_update_index_in_dim)/dynamic_update_slice | solution.py:46
  131.3 7.5 %dynamic_update_slice.11 = bf16[8,32,16,128]{3,0,2,1:T(8,128)(2,1)} dynamic-update-slice(bf16[8,32,16,128]{3,0,2,1:T(8,128)(2,1)} %get-tuple-element.196, f32[1,32,16,128]{3,0,2,1:T(1,128)S(1)} %bitcast.32, s32[]{:T(128)S(6)} %copy.44, s32[]{:T(128)} %constant.37.clone.1..sunk, s32[]{:T(128)} %constant.37.clone.1..sunk, s32[]{:T(128)} %constant.37.clone.1..sunk) | dynamic-update-slice | bytes 524292 | tf_op jit(solution)/shard_map/while/body/jit(dynamic_update_index_in_dim)/dynamic_update_slice | solution.py:46
  141.7 5.1 %dynamic_update_slice.12 = bf16[8,32,16,128]{3,0,2,1:T(8,128)(2,1)S(1)} dynamic-update-slice(bf16[8,32,16,128]{3,0,2,1:T(8,128)(2,1)S(1)} %get-tuple-element.197, f32[1,32,16,128]{3,0,2,1:T(1,128)S(1)} %bitcast.31, s32[]{:T(128)S(6)} %copy.44, s32[]{:T(128)} %constant.37.clone.1..sunk, s32[]{:T(128)} %constant.37.clone.1..sunk, s32[]{:T(128)} %constant.37.clone.1..sunk) | dynamic-update-slice | bytes 524292 | tf_op jit(solution)/shard_map/while/body/jit(dynamic_update_index_in_dim)/dynamic_update_slice | solution.py:46
  146.8 7.5 %dynamic_update_slice.11 = bf16[8,32,16,128]{3,0,2,1:T(8,128)(2,1)} dynamic-update-slice(bf16[8,32,16,128]{3,0,2,1:T(8,128)(2,1)} %get-tuple-element.196, f32[1,32,16,128]{3,0,2,1:T(1,128)S(1)} %bitcast.32, s32[]{:T(128)S(6)} %copy.44, s32[]{:T(128)} %constant.37.clone.1..sunk, s32[]{:T(128)} %constant.37.clone.1..sunk, s32[]{:T(128)} %constant.37.clone.1..sunk) | dynamic-update-slice | bytes 524292 | tf_op jit(solution)/shard_map/while/body/jit(dynamic_update_index_in_dim)/dynamic_update_slice | solution.py:46
  157.2 5.1 %dynamic_update_slice.12 = bf16[8,32,16,128]{3,0,2,1:T(8,128)(2,1)S(1)} dynamic-update-slice(bf16[8,32,16,128]{3,0,2,1:T(8,128)(2,1)S(1)} %get-tuple-element.197, f32[1,32,16,128]{3,0,2,1:T(1,128)S(1)} %bitcast.31, s32[]{:T(128)S(6)} %copy.44, s32[]{:T(128)} %constant.37.clone.1..sunk, s32[]{:T(128)} %constant.37.clone.1..sunk, s32[]{:T(128)} %constant.37.clone.1..sunk) | dynamic-update-slice | bytes 524292 | tf_op jit(solution)/shard_map/while/body/jit(dynamic_update_index_in_dim)/dynamic_update_slice | solution.py:46
  162.3 7.5 %dynamic_update_slice.11 = bf16[8,32,16,128]{3,0,2,1:T(8,128)(2,1)} dynamic-update-slice(bf16[8,32,16,128]{3,0,2,1:T(8,128)(2,1)} %get-tuple-element.196, f32[1,32,16,128]{3,0,2,1:T(1,128)S(1)} %bitcast.32, s32[]{:T(128)S(6)} %copy.44, s32[]{:T(128)} %constant.37.clone.1..sunk, s32[]{:T(128)} %constant.37.clone.1..sunk, s32[]{:T(128)} %constant.37.clone.1..sunk) | dynamic-update-slice | bytes 524292 | tf_op jit(solution)/shard_map/while/body/jit(dynamic_update_index_in_dim)/dynamic_update_slice | solution.py:46
  172.7 5.1 %dynamic_update_slice.12 = bf16[8,32,16,128]{3,0,2,1:T(8,128)(2,1)S(1)} dynamic-update-slice(bf16[8,32,16,128]{3,0,2,1:T(8,128)(2,1)S(1)} %get-tuple-element.197, f32[1,32,16,128]{3,0,2,1:T(1,128)S(1)} %bitcast.31, s32[]{:T(128)S(6)} %copy.44, s32[]{:T(128)} %constant.37.clone.1..sunk, s32[]{:T(128)} %constant.37.clone.1..sunk, s32[]{:T(128)} %constant.37.clone.1..sunk) | dynamic-update-slice | bytes 524292 | tf_op jit(solution)/shard_map/while/body/jit(dynamic_update_index_in_dim)/dynamic_update_slice | solution.py:46
  177.8 7.5 %dynamic_update_slice.11 = bf16[8,32,16,128]{3,0,2,1:T(8,128)(2,1)} dynamic-update-slice(bf16[8,32,16,128]{3,0,2,1:T(8,128)(2,1)} %get-tuple-element.196, f32[1,32,16,128]{3,0,2,1:T(1,128)S(1)} %bitcast.32, s32[]{:T(128)S(6)} %copy.44, s32[]{:T(128)} %constant.37.clone.1..sunk, s32[]{:T(128)} %constant.37.clone.1..sunk, s32[]{:T(128)} %constant.37.clone.1..sunk) | dynamic-update-slice | bytes 524292 | tf_op jit(solution)/shard_map/while/body/jit(dynamic_update_index_in_dim)/dynamic_update_slice | solution.py:46
  200.7 4.3 %collective-permute-done.7 = bf16[8,1,18,256]{3,0,2,1:T(8,128)(2,1)S(1)} collective-permute-done((bf16[8,1,18,256]{3,0,2,1:T(8,128)(2,1)S(1)}, bf16[8,1,18,256]{3,0,2,1:T(8,128)(2,1)S(1)}, u32[]{:S(2)}, u32[]{:S(2)}) %collective-permute-start.7) | collective-permute-done | bytes 73760 | tf_op jit(solution)/shard_map/ppermute | solution.py:15
  204.9 15.8 %fusion.3 = bf16[8,32,16,256]{3,0,2,1:T(8,128)(2,1)S(1)} fusion(bf16[3,3,256,256]{3,2,1,0:T(8,128)(2,1)S(1)} %copy-done.4, bf16[8,1,18,256]{3,0,2,1:T(8,128)(2,1)S(1)} %collective-permute-done.7, bf16[8,32,1,256]{3,0,2,1:T(8,128)(2,1)S(1)} %collective-permute-done.5, bf16[8,32,16,128]{3,0,2,1:T(8,128)(2,1)S(1)} %get-tuple-element.49, ...), kind=kOutput, calls=%fused_computation.8 | convolution fusion | flops 4917133312 | bytes 7880704 | tf_op jit(solution)/shard_map/conv_general_dilated | solution.py:21
  221.2 32.8 %all_to_all.36 = bf16[8,32,16,256]{3,2,1,0:T(8,128)(2,1)S(1)} all-to-all(bf16[8,32,16,256]{3,2,1,0:T(8,128)(2,1)S(1)} %copy.20), channel_id=1, replica_groups=mesh['tm'=8,'space'=4] {'tm'}, dimensions={0} | all-to-all | bytes 4194304 | tf_op jit(solution)/shard_map/all_to_all | solution.py:60
  (62 shorter events, 58.9 us)
Async XLA Ops:
  0.0 54.6 %copy-start = (bf16[3,3,256,256]{3,2,1,0:T(8,128)(2,1)S(1)}, bf16[3,3,256,256]{3,2,1,0:T(8,128)(2,1)}, u32[]{:S(2)}) copy-start(bf16[3,3,256,256]{3,2,1,0:T(8,128)(2,1)} %param.8) | copy-start | bytes 3538948
  4.2 37.5 %copy-start.2 = (f32[128]{0:T(128)S(1)}, f32[128]{0:T(128)}, u32[]{:S(2)}) copy-start(f32[128]{0:T(128)} %param.10) | copy-start | bytes 1540
  4.2 37.5 %copy-start.3 = (f32[128]{0:T(128)S(1)}, f32[128]{0:T(128)}, u32[]{:S(2)}) copy-start(f32[128]{0:T(128)} %param.9) | copy-start | bytes 1540
  4.2 32.1 %all-to-all-start = ((bf16[1,32,128,256]{3,1,0,2:T(8,128)(2,1)}), bf16[1,32,128,256]{3,1,0,2:T(8,128)(2,1)}, u32[]{:S(2)}, u32[]{:S(2)}) async-start(bf16[1,32,128,256]{3,1,0,2:T(8,128)(2,1)} %copy.14), calls=%async_computation | async-start | bytes 4194304 | tf_op jit(solution)/shard_map/all_to_all | solution.py:50
  39.0 2.7 %collective-permute-start = (bf16[8,32,1,256]{3,0,2,1:T(8,128)(2,1)S(1)}, bf16[8,32,1,256]{3,0,2,1:T(8,128)(2,1)S(1)}, u32[]{:S(2)}, u32[]{:S(2)}) collective-permute-start(bf16[8,32,1,256]{3,0,2,1:T(8,128)(2,1)S(1)} %get-tuple-element.125), channel_id=1, source_target_pairs={{0,4},{4,8},{8,12},{12,16},{16,20},{20,24},{24,28},{1,5},{5,9},{9,... | collective-permute-start | bytes 393224 | tf_op jit(solution)/shard_map/ppermute | solution.py:12
  40.3 4.0 %collective-permute-start.1 = (bf16[8,32,1,256]{3,0,2,1:T(8,128)(2,1)S(1)}, bf16[8,32,1,256]{3,0,2,1:T(8,128)(2,1)S(1)}, u32[]{:S(2)}, u32[]{:S(2)}) collective-permute-start(bf16[8,32,1,256]{3,0,2,1:T(8,128)(2,1)S(1)} %get-tuple-element.126), channel_id=1, source_target_pairs={{4,0},{8,4},{12,8},{16,12},{20,16},{24,20},{28,24},{5,1},{9,5},{13... | collective-permute-start | bytes 393224 | tf_op jit(solution)/shard_map/ppermute | solution.py:15
  44.4 6.0 %collective-permute-start.2 = (bf16[8,1,18,256]{3,0,2,1:T(8,128)(2,1)S(1)}, bf16[8,1,18,256]{3,0,2,1:T(8,128)(2,1)S(1)}, u32[]{:S(2)}, u32[]{:S(2)}) collective-permute-start(bf16[8,1,18,256]{3,0,2,1:T(8,128)(2,1)S(1)} %get-tuple-element.121), channel_id=1, source_target_pairs={{0,1},{1,2},{2,3},{4,5},{5,6},{6,7},{8,9},{9,10},{10,11},{12,13},{... | collective-permute-start | bytes 221192 | tf_op jit(solution)/shard_map/ppermute | solution.py:12
  48.4 6.2 %collective-permute-start.3 = (bf16[8,1,18,256]{3,0,2,1:T(8,128)(2,1)S(1)}, bf16[8,1,18,256]{3,0,2,1:T(8,128)(2,1)S(1)}, u32[]{:S(2)}, u32[]{:S(2)}) collective-permute-start(bf16[8,1,18,256]{3,0,2,1:T(8,128)(2,1)S(1)} %get-tuple-element.122), channel_id=1, source_target_pairs={{1,0},{2,1},{3,2},{5,4},{6,5},{7,6},{9,8},{10,9},{11,10},{13,12},{... | collective-permute-start | bytes 221192 | tf_op jit(solution)/shard_map/ppermute | solution.py:15
  185.3 19.7 %copy-start.1 = (bf16[8,32,16,128]{3,0,2,1:T(8,128)(2,1)S(1)}, bf16[8,32,16,128]{3,0,2,1:T(8,128)(2,1)}, u32[]{:S(2)}) copy-start(bf16[8,32,16,128]{3,0,2,1:T(8,128)(2,1)} %get-tuple-element.48) | copy-start | bytes 3145732
  185.3 19.7 %copy-start.4 = (bf16[3,3,256,256]{3,2,1,0:T(8,128)(2,1)S(1)}, bf16[3,3,256,256]{3,2,1,0:T(8,128)(2,1)}, u32[]{:S(2)}) copy-start(bf16[3,3,256,256]{3,2,1,0:T(8,128)(2,1)} %param.11) | copy-start | bytes 3538948
  186.3 5.3 %collective-permute-start.4 = (bf16[8,32,1,256]{3,0,2,1:T(8,128)(2,1)S(1)}, bf16[8,32,1,256]{3,0,2,1:T(8,128)(2,1)S(1)}, u32[]{:S(2)}, u32[]{:S(2)}) collective-permute-start(bf16[8,32,1,256]{3,0,2,1:T(8,128)(2,1)S(1)} %get-tuple-element.123), channel_id=1, source_target_pairs={{0,4},{4,8},{8,12},{12,16},{16,20},{20,24},{24,28},{1,5},{5,9},{9,... | collective-permute-start | bytes 393224 | tf_op jit(solution)/shard_map/ppermute | solution.py:12
  190.4 4.0 %collective-permute-start.5 = (bf16[8,32,1,256]{3,0,2,1:T(8,128)(2,1)S(1)}, bf16[8,32,1,256]{3,0,2,1:T(8,128)(2,1)S(1)}, u32[]{:S(2)}, u32[]{:S(2)}) collective-permute-start(bf16[8,32,1,256]{3,0,2,1:T(8,128)(2,1)S(1)} %get-tuple-element.124), channel_id=1, source_target_pairs={{4,0},{8,4},{12,8},{16,12},{20,16},{24,20},{28,24},{5,1},{9,5},{13... | collective-permute-start | bytes 393224 | tf_op jit(solution)/shard_map/ppermute | solution.py:15
  195.2 5.5 %collective-permute-start.6 = (bf16[8,1,18,256]{3,0,2,1:T(8,128)(2,1)S(1)}, bf16[8,1,18,256]{3,0,2,1:T(8,128)(2,1)S(1)}, u32[]{:S(2)}, u32[]{:S(2)}) collective-permute-start(bf16[8,1,18,256]{3,0,2,1:T(8,128)(2,1)S(1)} %get-tuple-element.119), channel_id=1, source_target_pairs={{0,1},{1,2},{2,3},{4,5},{5,6},{6,7},{8,9},{9,10},{10,11},{12,13},{... | collective-permute-start | bytes 221192 | tf_op jit(solution)/shard_map/ppermute | solution.py:12
  198.7 6.2 %collective-permute-start.7 = (bf16[8,1,18,256]{3,0,2,1:T(8,128)(2,1)S(1)}, bf16[8,1,18,256]{3,0,2,1:T(8,128)(2,1)S(1)}, u32[]{:S(2)}, u32[]{:S(2)}) collective-permute-start(bf16[8,1,18,256]{3,0,2,1:T(8,128)(2,1)S(1)} %get-tuple-element.120), channel_id=1, source_target_pairs={{1,0},{2,1},{3,2},{5,4},{6,5},{7,6},{9,8},{10,9},{11,10},{13,12},{... | collective-permute-start | bytes 221192 | tf_op jit(solution)/shard_map/ppermute | solution.py:15
where the time goes:
time: 258 us; the launch traced here: 256 us
  local copies, waits for them, and re-layouts  131 us (51%)
  waiting for transfers between devices  41.8 us (16%)
  blocking collectives  32.8 us (13%)
  starting transfers between devices  23.5 us (9%)
  matrix products  22.5 us (9%)
  other arithmetic  3.54 us (1%)
    dynamic_update_slice x16, local copies, waits for them, and re-layouts, local_recurrence(): return lax.scan(advance, (start, start), feed)  101 us
    all_to_all x1, blocking collectives, on_device(): return lax.all_to_all(result, 'tm', split_axis=0, concat_axis=2, tiled=True)  32.8 us
    all_to_all x1, waiting for transfers between devices, on_device(): lax.all_to_all(frames_in, 'tm', split_axis=2, concat_axis=0, tiled=True)  26.7 us
    conv_general_dilated x2, matrix products, convolve_valid(): lax.conv_general_dilated(padded, kernel, (1, 1), ((0, 0), (0, 0)), dimens...  22.5 us
    dynamic_slice x16, local copies, waits for them, and re-layouts, local_recurrence(): return lax.scan(advance, (start, start), feed)  21.7 us
    ppermute x4, waiting for transfers between devices, with_halo(): lax.ppermute(lax.slice_in_dim(block, 0, width, axis=dim), axis, backward)  13.9 us
    ppermute x4, starting transfers between devices, with_halo(): lax.ppermute(lax.slice_in_dim(block, block.shape[dim] - width, None, axis...  12.8 us
    ppermute x4, starting transfers between devices, with_halo(): lax.ppermute(lax.slice_in_dim(block, 0, width, axis=dim), axis, backward)  5.35 us
  transfers between devices with their start and end apart: 9, of which 7 were waited for; matrix products, arithmetic and copies ran while one was open for 0% of the time, Pallas kernels for 0%

commit v1 on v0

v1 whole, which is shorter than its diff:
```python
import functools

import numpy as np
import jax
import jax.numpy as jnp
from jax import lax
from jax.experimental import pallas as pl
from jax.experimental.pallas import tpu as pltpu
from jax.sharding import PartitionSpec as P

F32 = jnp.float32
BF16 = jnp.bfloat16
VMEM = pl.BlockSpec(memory_space=pltpu.VMEM)
SMEM = pl.BlockSpec(memory_space=pltpu.SMEM)
PARAMS = pltpu.CompilerParams(vmem_limit_bytes=48 * 1024 * 1024)


def cmul(coef, z):
    n = z.shape[-1] // 2
    re, im = z[..., :n], z[..., n:]
    cr, ci = coef
    return jnp.concatenate([cr * re - ci * im, cr * im + ci * re], axis=-1)


def widen(row):
    w = row.shape[0]
    col = lax.broadcasted_iota(jnp.int32, row.shape, 0)
    left = jnp.where(col == 0, 0.0, pltpu.roll(row, 1, 0))
    right = jnp.where(col == w - 1, 0.0, pltpu.roll(row, w - 1, 0))
    return jnp.concatenate([left, row, right], axis=-1).astype(BF16)


def conv_block(wide, w_ref, start, count):
    w, k = wide.shape[1], wide.shape[2]
    lhs = jnp.concatenate(
        [wide[start + d : start + d + count].reshape(count * w, k) for d in range(3)], axis=-1
    )
    return jnp.dot(lhs, w_ref[...], preferred_element_type=F32)


def blocks(total, size):
    return [(s, min(size, total - s)) for s in range(0, total, size)]


def coefficient(tab_ref, i):
    return tab_ref[2 * i : 2 * i + 1, :], tab_ref[2 * i + 1 : 2 * i + 2, :]


def drive_kernel(pieces, segments, step, *refs):
    idx, edge, decay, w_ref = refs[:4]
    xs = refs[4 : 4 + len(pieces)]
    feed, send, wide = refs[4 + len(pieces) :]
    n_states = decay.shape[1]
    mag = jnp.exp(-decay[...])
    factor = jnp.sqrt(1.0 - mag * mag)
    factor = jnp.concatenate([factor, factor], axis=-1)
    at = 0
    for ref, (lo, hi) in zip(xs, pieces):
        for r in range(lo, hi):
            wide[at] = widen(ref[r].astype(F32))
            at += 1
    quarters = feed.shape[1]
    half = quarters // 2
    other = (1 - idx[0]) * half
    out = 0
    for first, count, mask in segments:
        for s, size in blocks(count, step):
            acc = conv_block(wide, w_ref, first + s, size) * factor
            acc = acc.reshape((size,) + feed.shape[1:])
            for r in range(size):
                row = acc[r]
                if mask is not None and mask[0] == s + r:
                    row = row * edge[mask[1]]
                feed[out + r] = row
            out += size
    send[...] = feed[:, pl.ds(other, half)].astype(BF16)


def drive(xs, pieces, segments, rows, idx, edge, decay, w_in, quarters, step):
    w, c = xs[0].shape[1:]
    n_wide = sum(hi - lo for lo, hi in pieces)
    flops = 2 * rows * w * w_in.shape[0] * w_in.shape[1]
    return pl.pallas_call(
        functools.partial(drive_kernel, pieces, segments, step),
        out_shape=(
            jax.ShapeDtypeStruct((rows, quarters, w // quarters, c), F32),
            jax.ShapeDtypeStruct((rows, quarters // 2, w // quarters, c), BF16),
        ),
        in_specs=[SMEM, SMEM, VMEM, VMEM] + [VMEM] * len(xs),
        out_specs=(VMEM, VMEM),
        scratch_shapes=[pltpu.VMEM((n_wide, w, 3 * c), BF16)],
        compiler_params=PARAMS,
        cost_estimate=pl.CostEstimate(flops=flops, bytes_accessed=rows * w * c * 8, transcendentals=0),
        name="drive",
    )(idx, edge, decay, w_in, *xs)


def mix_kernel(terms, outs, *refs):
    idx, tab = refs[:2]
    srcs = refs[2 : 2 + len(terms)]
    dsts = refs[2 + len(terms) :]
    rows = srcs[0].shape[0]
    picks = []
    for plan in outs:
        picks.append([(coefficient(tab, k), srcs[s], idx[p] if isinstance(p, int) else None, p) for k, s, p in plan])

    def one(r, _):
        for dst, plan in zip(dsts, picks):
            total = None
            for coef, src, where, p in plan:
                if p == "all":
                    z = src[r]
                elif isinstance(p, tuple):
                    z = src[r, p[0] : p[0] + p[1]]
                else:
                    z = src[r, pl.ds(where, dst.shape[1])]
                part = cmul(coef, z.astype(F32))
                total = part if total is None else total + part
            dst[r] = total.astype(dst.dtype)
        return 0

    lax.fori_loop(0, rows, one, 0, unroll=False)


def mix(idx, tab, srcs, outs, name):
    size = sum(int(np.prod(s.shape)) for s in srcs)
    return pl.pallas_call(
        functools.partial(mix_kernel, srcs, [plan for _, _, plan in outs]),
        out_shape=tuple(jax.ShapeDtypeStruct(shape, dtype) for shape, dtype, _ in outs),
        in_specs=[SMEM, VMEM] + [VMEM] * len(srcs),
        out_specs=tuple(VMEM for _ in outs),
        compiler_params=PARAMS,
        cost_estimate=pl.CostEstimate(flops=8 * size, bytes_accessed=2 * size, transcendentals=0),
        name=name,
    )(idx, tab, *srcs)


def carry_kernel(half, idx, tab, r1, r2, r3, feed, got, pay, own):
    a2, a3, b1, b2, b3 = (coefficient(tab, k) for k in range(6, 11))
    pc, pf, qc, qg = (coefficient(tab, k) for k in range(11, 15))
    mine = idx[0] * half

    def one(r, _):
        x1, x2, x3 = (ref[r].astype(F32) for ref in (r1, r2, r3))
        first = cmul(a2, x2) + cmul(a3, x3)
        second = cmul(b1, x1) + cmul(b2, x2) + cmul(b3, x3)
        carry = jnp.stack([first, second])
        f = feed[r, pl.ds(mine, half)]
        g = got[r].astype(F32)
        pay[r] = (cmul(pc, carry) + cmul(pf, f)).astype(BF16)
        own[r] = (cmul(qc, carry) + cmul(qg, g)).astype(BF16)
        return 0

    lax.fori_loop(0, r1.shape[0], one, 0)


def carry_mix(idx, tab, r1, r2, r3, feed, got):
    shape = got.shape
    return pl.pallas_call(
        functools.partial(carry_kernel, shape[1]),
        out_shape=(jax.ShapeDtypeStruct(shape, BF16), jax.ShapeDtypeStruct(shape, BF16)),
        in_specs=[SMEM] + [VMEM] * 6,
        out_specs=(VMEM, VMEM),
        compiler_params=PARAMS,
        cost_estimate=pl.CostEstimate(flops=40 * got.size, bytes_accessed=12 * got.size, transcendentals=0),
        name="carry",
    )(idx, tab, r1, r2, r3, feed, got)


def output_kernel(plan, step, *refs):
    keep_rows, strips, aliased = plan
    idx, tab, w_ref, feed, own, other, frames = refs[:7]
    refs = refs[7:]
    if aliased:
        kept, _, out = refs[:3]
        refs = refs[3:]
    else:
        out, kept_out = refs[:2]
        refs = refs[2:]
    prev, wide, block, sem = refs
    rows, quarters = prev.shape[0], prev.shape[1]
    half = quarters // 2
    w, c = frames.shape[1:]
    lam = coefficient(tab, 15)
    prev[:, pl.ds(idx[0] * half, half)] = own[...]
    prev[:, pl.ds((1 - idx[0]) * half, half)] = other[...]

    def state(i):
        z = cmul(lam, prev[i].astype(F32)) + feed[i]
        return z.reshape(w, c)

    at = 0
    jobs = []
    for sources, first, count in strips:
        base = at
        for kind, i in sources:
            if kind == "new":
                row = state(i)
                if not aliased and i in keep_rows:
                    kept_out[keep_rows.index(i)] = row.astype(BF16)
                wide[at] = widen(row)
            else:
                wide[at] = widen(kept[i].astype(F32))
            at += 1
        jobs += [(base + s, first + s, size) for s, size in blocks(count, step)]
    copies = []
    for j, (base, first, size) in enumerate(jobs):
        mixed = conv_block(wide, w_ref, base, size).reshape(size, w, c)
        act = 0.5 * mixed * (1.0 + lax.erf(mixed * np.float32(0.5**0.5)))
        lo = sum(s for _, _, s in jobs[:j])
        block[lo : lo + size] = (frames[first : first + size].astype(F32) + act).astype(BF16)
        copy = pltpu.make_async_copy(block.at[pl.ds(lo, size)], out.at[pl.ds(first, size)], sem.at[j])
        copy.start()
        copies.append(copy)
    for copy in copies:
        copy.wait()


def output(idx, tab, w_out, feed, own, other, frames, plan, step, previous=None, kept=None):
    keep_rows, strips, aliased = plan
    rows, quarters = feed.shape[:2]
    w, c = frames.shape[1:]
    n_wide = sum(len(s) for s, _, _ in strips)
    n_out = sum(n for _, _, n in strips)
    n_jobs = sum(len(blocks(n, step)) for _, _, n in strips)
    hbm = pl.BlockSpec(memory_space=pl.ANY)
    whole = jax.ShapeDtypeStruct(frames.shape, BF16)
    args = [idx, tab, w_out, feed, own, other, frames]
    specs = [SMEM] + [VMEM] * 6
    if aliased:
        args += [kept, previous]
        specs += [VMEM, hbm]
        out_shape, out_specs, alias = whole, hbm, {8: 0}
    else:
        out_shape = (whole, jax.ShapeDtypeStruct((len(keep_rows), w, c), BF16))
        out_specs, alias = (hbm, VMEM), {}
    return pl.pallas_call(
        functools.partial(output_kernel, plan, step),
        out_shape=out_shape,
        in_specs=specs,
        out_specs=out_specs,
        input_output_aliases=alias,
        scratch_shapes=[
            pltpu.VMEM((rows, quarters, w // quarters, c), BF16),
            pltpu.VMEM((n_wide, w, 3 * c), BF16),
            pltpu.VMEM((n_out, w, c), BF16),
            pltpu.SemaphoreType.DMA((n_jobs,)),
        ],
        compiler_params=PARAMS,
        cost_estimate=pl.CostEstimate(
            flops=2 * n_out * w * w_out.shape[0] * w_out.shape[1], bytes_accessed=n_out * w * c * 8, transcendentals=0
        ),
        name="output",
    )(*args)


def role_table(n):
    expo, gate = np.zeros((n, 16)), np.zeros((n, 16))

    def put(dev, k, e):
        expo[dev, k], gate[dev, k] = e, 1.0

    for dev in range(n):
        q, core = divmod(dev, 2)
        put(dev, 0, 1 - core)
        put(dev, 1, core)
        if n == 8:
            if q == 0:
                put(dev, 2, 2), put(dev, 3, 0), put(dev, 4, 0)
            if q == 1:
                put(dev, 2, 0), put(dev, 3, 2), put(dev, 7, 0), put(dev, 8, 0)
            if q == 2:
                put(dev, 4, 0), put(dev, 5, 2), put(dev, 6, 0), put(dev, 10, 0)
            if q == 3:
                put(dev, 5, 0), put(dev, 7, 0), put(dev, 8, 0), put(dev, 9, 2)
        else:
            put(dev, 7, 0), put(dev, 8, 0)
        put(dev, 11, 1 - core)
        if core == 0:
            put(dev, 12, 0)
        put(dev, 13, core)
        if core == 1:
            put(dev, 14, 0)
        put(dev, 15, 1)
    return expo.astype(np.float32), gate.astype(np.float32)


def powers(expo, gate, decay, phase):
    size = gate[:, None] * jnp.exp(-expo[:, None] * decay)
    angle = expo[:, None] * phase
    return jnp.stack([size * jnp.cos(angle), size * jnp.sin(angle)], axis=1).reshape(2 * expo.shape[0], -1)


def both_cores(pairs):
    return [(2 * a + k, 2 * b + k) for a, b in pairs for k in range(2)]


def on_device(n, n_space, frames_in, w_input, decay_rate, phase, w_output):
    frames = frames_in[0]
    rows, w, c = frames.shape
    quarters = 4
    me = lax.axis_index("tm")
    core = me % 2
    chip = me // 2
    expo, gate = role_table(n)
    tab = powers(jnp.asarray(expo)[me], jnp.asarray(gate)[me], decay_rate, phase)
    idx = jnp.stack([core, jnp.where(chip == 1, 0, 1), jnp.where(chip == 0, 0, 1)]).astype(jnp.int32)
    space = lax.axis_index("space")
    edge = jnp.stack([space > 0, space < n_space - 1]).astype(F32)
    decay = decay_rate[None]
    w_in = w_input.reshape(-1, w_input.shape[-1])
    w_out = w_output.reshape(-1, w_output.shape[-1])
    swap = [(i, i ^ 1) for i in range(n)]

    up = [(i, i + 1) for i in range(n_space - 1)]
    down = [(b, a) for a, b in up]
    above = lax.ppermute(frames[rows - 2 :], "space", up)
    below = lax.ppermute(frames[:2], "space", down)

    m = rows // 4
    inner = rows - 2 * m
    feeds, gots = [], []
    first = drive(
        [frames], [(m - 1, rows - m + 1)], [(0, inner, None)], inner, idx, edge, decay, w_in, quarters, 8
    )
    second = drive(
        [above, frames, frames, below],
        [(0, 2), (0, m + 1), (rows - m - 1, rows), (0, 2)],
        [(0, m + 1, (0, 0)), (m + 3, m + 1, (m, 1))],
        2 * (m + 1), idx, edge, decay, w_in, quarters, 9,
    )

    def exchange(feed, send):
        got = lax.ppermute(send, "tm", swap)
        n_rows, half = got.shape[:2]
        quarter = (n_rows, 1) + got.shape[2:]
        if n == 8:
            pair, pay = pair_sum(idx, tab, feed, got)
            r1 = lax.ppermute(pay, "tm", both_cores([(0, 1), (1, 0), (2, 3)]))
            (pay,) = mix(idx, tab, [pair, r1], [(quarter, BF16, [(2, 0, 2), (3, 1, "all")])], "second")
            r2 = lax.ppermute(pay, "tm", both_cores([(0, 2), (1, 3)]))
            (pay,) = mix(idx, tab, [pair, r2], [(quarter, BF16, [(4, 0, (0, 1)), (5, 1, "all")])], "third")
            r3 = lax.ppermute(pay, "tm", both_cores([(0, 1), (2, 3), (3, 2)]))
        else:
            pair, _ = pair_sum(idx, tab, feed, got)
            chips = n // 2
            stride = 1
            while stride < chips:
                moved = lax.ppermute(
                    pair.astype(BF16), "tm", both_cores([(i, i + stride) for i in range(chips - stride)])
                ).astype(F32)
                power = powers(jnp.asarray([2.0 * stride], F32), jnp.ones((1,), F32), decay_rate, phase)
                pair = pair + cmul((power[0], power[1]), moved)
                stride *= 2
            carry = lax.ppermute(pair.astype(BF16), "tm", both_cores([(i, i + 1) for i in range(chips - 1)]))
            r1, r3 = carry[:, 1:], carry[:, :1]
            r2 = jnp.zeros_like(r1)
        pay, own = carry_mix(idx, tab, r1[:, 0], r2[:, 0], r3[:, 0], feed, got)
        return own, lax.ppermute(pay, "tm", swap)

    own1, other1 = exchange(*first)
    own2, other2 = exchange(*second)
    top = [("new", i) for i in range(m + 1)] + [("kept", 0), ("kept", 1)]
    bottom = [("kept", 2), ("kept", 3)] + [("new", i) for i in range(m + 1, 2 * (m + 1))]
    keep = [0, 1, inner - 2, inner - 1]
    result, kept = output(
        idx, tab, w_out, first[0], own1, other1, frames,
        (keep, [([("new", i) for i in range(inner)], m + 1, inner - 2)], False), 7,
    )
    result = output(
        idx, tab, w_out, second[0], own2, other2, frames,
        (keep, [(top, 0, m + 1), (bottom, rows - m - 1, m + 1)], True), 9,
        previous=result, kept=kept,
    )
    return result[None]


def pair_kernel(half, idx, tab, feed, got, pair, pay):
    cm, cr = coefficient(tab, 0), coefficient(tab, 1)
    mine = idx[0] * half

    def one(r, _):
        pair[r] = cmul(cm, feed[r, pl.ds(mine, half)]) + cmul(cr, got[r].astype(F32))
        pay[r] = pair[r, pl.ds(idx[1], 1)].astype(BF16)
        return 0

    lax.fori_loop(0, got.shape[0], one, 0)


def pair_sum(idx, tab, feed, got):
    n_rows, half, w, c = got.shape
    return pl.pallas_call(
        functools.partial(pair_kernel, half),
        out_shape=(jax.ShapeDtypeStruct(got.shape, F32), jax.ShapeDtypeStruct((n_rows, 1, w, c), BF16)),
        in_specs=[SMEM, VMEM, VMEM, VMEM],
        out_specs=(VMEM, VMEM),
        compiler_params=PARAMS,
        cost_estimate=pl.CostEstimate(flops=16 * got.size, bytes_accessed=10 * got.size, transcendentals=0),
        name="pair",
    )(idx, tab, feed, got)


def solution(mesh):
    in_specs = (P("tm", "space", None, None), P(), P(), P(), P())
    out_specs = P("tm", "space", None, None)
    body = functools.partial(on_device, mesh.shape["tm"], mesh.shape["space"])
    return jax.shard_map(body, mesh=mesh, in_specs=in_specs, out_specs=out_specs, check_vma=False)
```

time: 258 us -> 77.3 us (0.30)
  the two profiles are of different devices: /device:TPU:0 before, /device:TPU:15 now
where the time goes in v1:
time: 77.3 us; the launch traced here: 76.8 us
  Pallas kernels  28.4 us (37%)
  starting transfers between devices  21.3 us (28%)
  waiting for transfers between devices  16.9 us (22%)
  local copies, waits for them, and re-layouts  8.75 us (11%)
  other arithmetic  1.12 us (1%)
    pallas_call x2, Pallas kernels, output(): pl.pallas_call(functools.partial(output_kernel, plan, step), out_shape=ou...  11.8 us
    ppermute x2, waiting for transfers between devices, exchange(): r1 = lax.ppermute(pay, 'tm', both_cores([(0, 1), (1, 0), (2, 3)]))  9.77 us
    pallas_call x2, Pallas kernels, drive(): pl.pallas_call(functools.partial(drive_kernel, pieces, segments, step), o...  8.12 us
    unnamed x20, local copies, waits for them, and re-layouts  6.39 us
    ppermute x2, starting transfers between devices, exchange(): return (own, lax.ppermute(pay, 'tm', swap))  5.69 us
    ppermute x2, waiting for transfers between devices, exchange(): r2 = lax.ppermute(pay, 'tm', both_cores([(0, 2), (1, 3)]))  4.98 us
    ppermute x2, starting transfers between devices, exchange(): r3 = lax.ppermute(pay, 'tm', both_cores([(0, 1), (2, 3), (3, 2)]))  3.84 us
    pallas_call x2, Pallas kernels, carry_mix(): pl.pallas_call(functools.partial(carry_kernel, shape[1]), out_shape=(jax....  3.26 us
  transfers between devices with their start and end apart: 12, of which 4 were waited for; matrix products, arithmetic and copies ran while one was open for 2% of the time, Pallas kernels for 29%

profile of v1, /device:TPU:15, one launch (start us, length us, event | category | flops | bytes accessed | tf_op | source)
XLA Modules:
  0.0 76.8 jit_solution(6846577123467711321)
XLA Ops:
  0.0 1.6 %slice_bitcast_fusion = (bf16[2,128,256]{2,1,0:T(8,128)(2,1)}, bf16[2,128,256]{2,1,0:T(8,128)(2,1)S(1)}) fusion(bf16[1,32,128,256]{3,2,1,0:T(8,128)(2,1)} %param.7), kind=kLoop, calls=%fused_computation | loop fusion | bytes 524288 | tf_op jit(solution)/shard_map/slice | solution.py:318
  1.6 2.1 %collective-permute-start.1 = (bf16[2,128,256]{2,1,0:T(8,128)(2,1)}, bf16[2,128,256]{2,1,0:T(8,128)(2,1)S(1)}, u32[]{:S(2)}, u32[]{:S(2)}) collective-permute-start(bf16[2,128,256]{2,1,0:T(8,128)(2,1)} %get-tuple-element.33), channel_id=1, source_target_pairs={{1,0},{2,1},{3,2},{5,4},{6,5},{7,6},{9,8},{10,9},{11,10},{13,12},{... | collective-permute-start | bytes 393224 | tf_op jit(solution)/shard_map/ppermute | solution.py:318
  3.7 3.2 %collective-permute-start = (bf16[2,128,256]{2,1,0:T(8,128)(2,1)S(1)}, bf16[2,128,256]{2,1,0:T(8,128)(2,1)S(1)}, u32[]{:S(2)}, u32[]{:S(2)}) collective-permute-start(bf16[2,128,256]{2,1,0:T(8,128)(2,1)S(1)} %get-tuple-element.34), channel_id=1, source_target_pairs={{0,1},{1,2},{2,3},{4,5},{5,6},{6,7},{8,9},{9,10},{10,11},{12,13},{... | collective-permute-start | bytes 393224 | tf_op jit(solution)/shard_map/ppermute | solution.py:317
  7.1 1.6 %copy-done.1 = bf16[1,32,128,256]{3,2,1,0:T(8,128)(2,1)S(1)} copy-done((bf16[1,32,128,256]{3,2,1,0:T(8,128)(2,1)S(1)}, bf16[1,32,128,256]{3,2,1,0:T(8,128)(2,1)}, u32[]{:S(2)}) %copy-start.1) | copy-done | bytes 2097176
  10.6 3.2 %drive.3 = (f32[16,4,32,256]{3,2,1,0:T(8,128)S(1)}, bf16[16,2,32,256]{3,2,1,0:T(8,128)(2,1)S(1)}) custom-call(s32[3]{0:T(128)S(1)} %pad_add_fusion.refs_0_.idx, f32[2]{0:T(128)S(1)} %add_convert_fusion.refs_1_, f32[1,128]{1,0:T(1,128)S(1)} %bitcast.68, bf16[2304,256]{1,0:T(8,128)(2,1)S(1)} %bitcast.70, bf16[32,128,256]{2,1,0:T(8,128)(2,1)S(1)} %bitcast.38), custom_call_target="tpu_custom_call" | custom-call | flops 2415919104 | bytes 4194304 | tf_op jit(solution)/shard_map/drive/pallas_call | solution.py:83
  13.9 1.3 %collective-permute-start.7 = (bf16[16,2,32,256]{3,2,1,0:T(8,128)(2,1)S(1)}, bf16[16,2,32,256]{3,2,1,0:T(8,128)(2,1)S(1)}, u32[]{:S(2)}, u32[]{:S(2)}) collective-permute-start(bf16[16,2,32,256]{3,2,1,0:T(8,128)(2,1)S(1)} %get-tuple-element.26), channel_id=1, source_target_pairs={{0,4},{4,0},{8,12},{12,8},{16,20},{20,16},{24,28},{28,24},{1,5},{5... | collective-permute-start | bytes 1572872 | tf_op jit(solution)/shard_map/ppermute | solution.py:334
  15.2 1.6 %copy-done.2 = bf16[1,32,128,256]{3,2,1,0:T(8,128)(2,1)S(1)} copy-done((bf16[1,32,128,256]{3,2,1,0:T(8,128)(2,1)S(1)}, bf16[1,32,128,256]{3,2,1,0:T(8,128)(2,1)}, u32[]{:S(2)}) %copy-start.2) | copy-done | bytes 2097176
  18.0 4.9 %drive.2 = (f32[18,4,32,256]{3,2,1,0:T(8,128)}, bf16[18,2,32,256]{3,2,1,0:T(8,128)(2,1)S(1)}) custom-call(s32[3]{0:T(128)S(1)} %pad_add_fusion.refs_0_.idx, f32[2]{0:T(128)S(1)} %add_convert_fusion.refs_1_, f32[1,128]{1,0:T(1,128)S(1)} %bitcast.69, bf16[2304,256]{1,0:T(8,128)(2,1)S(1)} %bitcast.71, bf16[2,128,256]{2,1,0:T(8,128)(2,1)S(1)} %collective-permute-done.refs_4_, ...), custom_call_target="tpu_custom_call" | custom-call | flops 2717908992 | bytes 4718592 | tf_op jit(solution)/shard_map/drive/pallas_call | solution.py:83
  25.7 1.3 %collective-permute-start.8 = (bf16[16,1,32,256]{3,2,0,1:T(8,128)(2,1)S(1)}, bf16[16,1,32,256]{3,2,0,1:T(8,128)(2,1)S(1)}, u32[]{:S(2)}, u32[]{:S(2)}) collective-permute-start(bf16[16,1,32,256]{3,2,0,1:T(8,128)(2,1)S(1)} %bitcast.73), channel_id=1, source_target_pairs={{0,8},{4,12},{8,0},{12,4},{16,24},{20,28},{1,9},{5,13},{9,1},{13,5... | collective-permute-start | bytes 786440 | tf_op jit(solution)/shard_map/ppermute | solution.py:339
  28.1 1.3 %collective-permute-start.3 = (bf16[18,1,32,256]{3,2,0,1:T(8,128)(2,1)S(1)}, bf16[18,1,32,256]{3,2,0,1:T(8,128)(2,1)S(1)}, u32[]{:S(2)}, u32[]{:S(2)}) collective-permute-start(bf16[18,1,32,256]{3,2,0,1:T(8,128)(2,1)S(1)} %bitcast.72), channel_id=1, source_target_pairs={{0,8},{4,12},{8,0},{12,4},{16,24},{20,28},{1,9},{5,13},{9,1},{13,5... | collective-permute-start | bytes 884744 | tf_op jit(solution)/shard_map/ppermute | solution.py:339
  29.4 5.5 %collective-permute-done.8 = bf16[16,1,32,256]{3,2,0,1:T(8,128)(2,1)S(1)} collective-permute-done((bf16[16,1,32,256]{3,2,0,1:T(8,128)(2,1)S(1)}, bf16[16,1,32,256]{3,2,0,1:T(8,128)(2,1)S(1)}, u32[]{:S(2)}, u32[]{:S(2)}) %collective-permute-start.8) | collective-permute-done | bytes 262176 | tf_op jit(solution)/shard_map/ppermute | solution.py:339
  35.7 1.3 %collective-permute-start.9 = (bf16[16,1,32,256]{3,2,0,1:T(8,128)(2,1)S(1)}, bf16[16,1,32,256]{3,2,0,1:T(8,128)(2,1)S(1)}, u32[]{:S(2)}, u32[]{:S(2)}) collective-permute-start(bf16[16,1,32,256]{3,2,0,1:T(8,128)(2,1)S(1)} %bitcast.67), channel_id=1, source_target_pairs={{0,16},{4,20},{8,24},{12,28},{1,17},{5,21},{9,25},{13,29},{2,18},{... | collective-permute-start | bytes 786440 | tf_op jit(solution)/shard_map/ppermute | solution.py:341
  37.0 4.2 %collective-permute-done.3 = bf16[18,1,32,256]{3,2,0,1:T(8,128)(2,1)S(1)} collective-permute-done((bf16[18,1,32,256]{3,2,0,1:T(8,128)(2,1)S(1)}, bf16[18,1,32,256]{3,2,0,1:T(8,128)(2,1)S(1)}, u32[]{:S(2)}, u32[]{:S(2)}) %collective-permute-start.3) | collective-permute-done | bytes 294944 | tf_op jit(solution)/shard_map/ppermute | solution.py:339
  42.1 1.3 %collective-permute-start.4 = (bf16[18,1,32,256]{3,2,0,1:T(8,128)(2,1)S(1)}, bf16[18,1,32,256]{3,2,0,1:T(8,128)(2,1)S(1)}, u32[]{:S(2)}, u32[]{:S(2)}) collective-permute-start(bf16[18,1,32,256]{3,2,0,1:T(8,128)(2,1)S(1)} %bitcast.64), channel_id=1, source_target_pairs={{0,16},{4,20},{8,24},{12,28},{1,17},{5,21},{9,25},{13,29},{2,18},{... | collective-permute-start | bytes 884744 | tf_op jit(solution)/shard_map/ppermute | solution.py:341
  44.2 1.9 %collective-permute-start.10 = (bf16[16,1,32,256]{3,2,0,1:T(8,128)(2,1)S(1)}, bf16[16,1,32,256]{3,2,0,1:T(8,128)(2,1)S(1)}, u32[]{:S(2)}, u32[]{:S(2)}) collective-permute-start(bf16[16,1,32,256]{3,2,0,1:T(8,128)(2,1)S(1)} %bitcast.66), channel_id=1, source_target_pairs={{0,8},{4,12},{16,24},{20,28},{24,16},{28,20},{1,9},{5,13},{17,25},... | collective-permute-start | bytes 786440 | tf_op jit(solution)/shard_map/ppermute | solution.py:343
  46.1 5.0 %collective-permute-done.4 = bf16[18,1,32,256]{3,2,0,1:T(8,128)(2,1)S(1)} collective-permute-done((bf16[18,1,32,256]{3,2,0,1:T(8,128)(2,1)S(1)}, bf16[18,1,32,256]{3,2,0,1:T(8,128)(2,1)S(1)}, u32[]{:S(2)}, u32[]{:S(2)}) %collective-permute-start.4) | collective-permute-done | bytes 294944 | tf_op jit(solution)/shard_map/ppermute | solution.py:341
  51.9 1.9 %collective-permute-start.5 = (bf16[18,1,32,256]{3,2,0,1:T(8,128)(2,1)S(1)}, bf16[18,1,32,256]{3,2,0,1:T(8,128)(2,1)S(1)}, u32[]{:S(2)}, u32[]{:S(2)}) collective-permute-start(bf16[18,1,32,256]{3,2,0,1:T(8,128)(2,1)S(1)} %bitcast.63), channel_id=1, source_target_pairs={{0,8},{4,12},{16,24},{20,28},{24,16},{28,20},{1,9},{5,13},{17,25},... | collective-permute-start | bytes 884744 | tf_op jit(solution)/shard_map/ppermute | solution.py:343
  53.8 1.6 %carry.3 = (bf16[16,2,32,256]{3,2,1,0:T(8,128)(2,1)S(1)}, bf16[16,2,32,256]{3,2,1,0:T(8,128)(2,1)S(1)}) custom-call(s32[3]{0:T(128)S(1)} %pad_add_fusion.refs_0_.idx, f32[32,128]{1,0:T(8,128)S(1)} %bitcast.48, bf16[16,32,256]{2,1,0:T(8,128)(2,1)S(1)} %bitcast.59, bf16[16,32,256]{2,1,0:T(8,128)(2,1)S(1)} %bitcast.61, bf16[16,32,256]{2,1,0:T(8,128)(2,1)S(1)} %bitcast.65, ...), custom_call_target="tpu_custom_call" | custom-call | flops 10485760 | bytes 3145728 | tf_op jit(solution)/shard_map/carry/pallas_call | solution.py:159
  55.4 2.4 %collective-permute-start.11 = (bf16[16,2,32,256]{3,2,1,0:T(8,128)(2,1)S(1)}, bf16[16,2,32,256]{3,2,1,0:T(8,128)(2,1)S(1)}, u32[]{:S(2)}, u32[]{:S(2)}) collective-permute-start(bf16[16,2,32,256]{3,2,1,0:T(8,128)(2,1)S(1)} %get-tuple-element.30), channel_id=1, source_target_pairs={{0,4},{4,0},{8,12},{12,8},{16,20},{20,16},{24,28},{28,24},{1,5},{5... | collective-permute-start | bytes 1572872 | tf_op jit(solution)/shard_map/ppermute | solution.py:359
  57.8 2.2 %collective-permute-done.5 = bf16[18,1,32,256]{3,2,0,1:T(8,128)(2,1)S(1)} collective-permute-done((bf16[18,1,32,256]{3,2,0,1:T(8,128)(2,1)S(1)}, bf16[18,1,32,256]{3,2,0,1:T(8,128)(2,1)S(1)}, u32[]{:S(2)}, u32[]{:S(2)}) %collective-permute-start.5) | collective-permute-done | bytes 294944 | tf_op jit(solution)/shard_map/ppermute | solution.py:343
  60.0 1.7 %carry.2 = (bf16[18,2,32,256]{3,2,1,0:T(8,128)(2,1)S(1)}, bf16[18,2,32,256]{3,2,1,0:T(8,128)(2,1)S(1)}) custom-call(s32[3]{0:T(128)S(1)} %pad_add_fusion.refs_0_.idx, f32[32,128]{1,0:T(8,128)S(1)} %bitcast.49, bf16[18,32,256]{2,1,0:T(8,128)(2,1)S(1)} %bitcast.53, bf16[18,32,256]{2,1,0:T(8,128)(2,1)S(1)} %bitcast.55, bf16[18,32,256]{2,1,0:T(8,128)(2,1)S(1)} %bitcast.62, ...), custom_call_target="tpu_custom_call" | custom-call | flops 11796480 | bytes 3538944 | tf_op jit(solution)/shard_map/carry/pallas_call | solution.py:159
  61.7 3.3 %collective-permute-start.6 = (bf16[18,2,32,256]{3,2,1,0:T(8,128)(2,1)S(1)}, bf16[18,2,32,256]{3,2,1,0:T(8,128)(2,1)S(1)}, u32[]{:S(2)}, u32[]{:S(2)}) collective-permute-start(bf16[18,2,32,256]{3,2,1,0:T(8,128)(2,1)S(1)} %get-tuple-element.24), channel_id=1, source_target_pairs={{0,4},{4,0},{8,12},{12,8},{16,20},{20,16},{24,28},{28,24},{1,5},{5... | collective-permute-start | bytes 1769480 | tf_op jit(solution)/shard_map/ppermute | solution.py:359
  65.0 5.5 %output.2 = (bf16[32,128,256]{2,1,0:T(8,128)(2,1)}, bf16[4,128,256]{2,1,0:T(8,128)(2,1)S(1)}) custom-call(s32[3]{0:T(128)S(1)} %pad_add_fusion.refs_0_.idx, f32[32,128]{1,0:T(8,128)S(1)} %bitcast.50, bf16[2304,256]{1,0:T(8,128)(2,1)S(1)} %bitcast.56, f32[16,4,32,256]{3,2,1,0:T(8,128)S(1)} %get-tuple-element.25.feed.refs_3_, ...), custom_call_target="tpu_custom_call" | custom-call | flops 2113929216 | bytes 3670016 | tf_op jit(solution)/shard_map/output/pallas_call | solution.py:237
  70.5 6.3 %output.3 = bf16[32,128,256]{2,1,0:T(8,128)(2,1)} custom-call(s32[3]{0:T(128)S(1)} %pad_add_fusion.refs_0_.idx, f32[32,128]{1,0:T(8,128)S(1)} %bitcast.51, bf16[2304,256]{1,0:T(8,128)(2,1)S(1)} %bitcast.57, f32[18,4,32,256]{3,2,1,0:T(8,128)} %get-tuple-element.19.feed.refs_3_, ...), custom_call_target="tpu_custom_call", output_to_operand_aliasing={{}: (8, {})} | custom-call | flops 2717908992 | bytes 4718592 | tf_op jit(solution)/shard_map/output/pallas_call | solution.py:237
  (40 shorter events, 10.4 us)
Async XLA Ops:
  1.6 13.5 %collective-permute-start.1 = (bf16[2,128,256]{2,1,0:T(8,128)(2,1)}, bf16[2,128,256]{2,1,0:T(8,128)(2,1)S(1)}, u32[]{:S(2)}, u32[]{:S(2)}) collective-permute-start(bf16[2,128,256]{2,1,0:T(8,128)(2,1)} %get-tuple-element.33), channel_id=1, source_target_pairs={{1,0},{2,1},{3,2},{5,4},{6,5},{7,6},{9,8},{10,9},{11,10},{13,12},{... | collective-permute-start | bytes 393224 | tf_op jit(solution)/shard_map/ppermute | solution.py:318
  3.7 11.5 %collective-permute-start = (bf16[2,128,256]{2,1,0:T(8,128)(2,1)S(1)}, bf16[2,128,256]{2,1,0:T(8,128)(2,1)S(1)}, u32[]{:S(2)}, u32[]{:S(2)}) collective-permute-start(bf16[2,128,256]{2,1,0:T(8,128)(2,1)S(1)} %get-tuple-element.34), channel_id=1, source_target_pairs={{0,1},{1,2},{2,3},{4,5},{5,6},{6,7},{8,9},{9,10},{10,11},{12,13},{... | collective-permute-start | bytes 393224 | tf_op jit(solution)/shard_map/ppermute | solution.py:317
  7.1 1.6 %copy-start.1 = (bf16[1,32,128,256]{3,2,1,0:T(8,128)(2,1)S(1)}, bf16[1,32,128,256]{3,2,1,0:T(8,128)(2,1)}, u32[]{:S(2)}) copy-start(bf16[1,32,128,256]{3,2,1,0:T(8,128)(2,1)} %param.7) | copy-start | bytes 6291460
  8.7 0.7 copy-start.5
  9.4 1.3 %copy-start.7 = (bf16[3,3,256,256]{3,2,1,0:T(8,128)(2,1)S(1)}, bf16[3,3,256,256]{3,2,1,0:T(8,128)(2,1)}, u32[]{:S(2)}) copy-start(bf16[3,3,256,256]{3,2,1,0:T(8,128)(2,1)} %param.8) | copy-start | bytes 3538948
  10.6 4.5 %copy-start.6 = (f32[128]{0:T(128)S(1)}, f32[128]{0:T(128)}, u32[]{:S(2)}) copy-start(f32[128]{0:T(128)} %param.9) | copy-start | bytes 1540
  13.9 10.9 %collective-permute-start.7 = (bf16[16,2,32,256]{3,2,1,0:T(8,128)(2,1)S(1)}, bf16[16,2,32,256]{3,2,1,0:T(8,128)(2,1)S(1)}, u32[]{:S(2)}, u32[]{:S(2)}) collective-permute-start(bf16[16,2,32,256]{3,2,1,0:T(8,128)(2,1)S(1)} %get-tuple-element.26), channel_id=1, source_target_pairs={{0,4},{4,0},{8,12},{12,8},{16,20},{20,16},{24,28},{28,24},{1,5},{5... | collective-permute-start | bytes 1572872 | tf_op jit(solution)/shard_map/ppermute | solution.py:334
  15.2 9.4 %copy-start.9 = (f32[128]{0:T(128)S(1)}, f32[128]{0:T(128)}, u32[]{:S(2)}) copy-start(f32[128]{0:T(128)} %param.10) | copy-start | bytes 1540
  15.2 1.6 %copy-start.2 = (bf16[1,32,128,256]{3,2,1,0:T(8,128)(2,1)S(1)}, bf16[1,32,128,256]{3,2,1,0:T(8,128)(2,1)}, u32[]{:S(2)}) copy-start(bf16[1,32,128,256]{3,2,1,0:T(8,128)(2,1)} %param.7) | copy-start | bytes 6291460
  16.8 1.3 %copy-start.8 = (bf16[3,3,256,256]{3,2,1,0:T(8,128)(2,1)S(1)}, bf16[3,3,256,256]{3,2,1,0:T(8,128)(2,1)}, u32[]{:S(2)}) copy-start(bf16[3,3,256,256]{3,2,1,0:T(8,128)(2,1)} %param.8) | copy-start | bytes 3538948
  23.0 4.1 %copy-start = (f32[18,4,32,256]{3,2,1,0:T(8,128)S(1)}, f32[18,4,32,256]{3,2,1,0:T(8,128)}, u32[]{:S(2)}) copy-start(f32[18,4,32,256]{3,2,1,0:T(8,128)} %get-tuple-element.19.feed.refs_3_) | copy-start | bytes 7077892
  23.0 4.1 %collective-permute-start.2 = (bf16[18,2,32,256]{3,2,1,0:T(8,128)(2,1)S(1)}, bf16[18,2,32,256]{3,2,1,0:T(8,128)(2,1)S(1)}, u32[]{:S(2)}, u32[]{:S(2)}) collective-permute-start(bf16[18,2,32,256]{3,2,1,0:T(8,128)(2,1)S(1)} %get-tuple-element.20), channel_id=1, source_target_pairs={{0,4},{4,0},{8,12},{12,8},{16,20},{20,16},{24,28},{28,24},{1,5},{5... | collective-permute-start | bytes 1769480 | tf_op jit(solution)/shard_map/ppermute | solution.py:334
  25.7 9.2 %collective-permute-start.8 = (bf16[16,1,32,256]{3,2,0,1:T(8,128)(2,1)S(1)}, bf16[16,1,32,256]{3,2,0,1:T(8,128)(2,1)S(1)}, u32[]{:S(2)}, u32[]{:S(2)}) collective-permute-start(bf16[16,1,32,256]{3,2,0,1:T(8,128)(2,1)S(1)} %bitcast.73), channel_id=1, source_target_pairs={{0,8},{4,12},{8,0},{12,4},{16,24},{20,28},{1,9},{5,13},{9,1},{13,5... | collective-permute-start | bytes 786440 | tf_op jit(solution)/shard_map/ppermute | solution.py:339
  28.1 13.1 %collective-permute-start.3 = (bf16[18,1,32,256]{3,2,0,1:T(8,128)(2,1)S(1)}, bf16[18,1,32,256]{3,2,0,1:T(8,128)(2,1)S(1)}, u32[]{:S(2)}, u32[]{:S(2)}) collective-permute-start(bf16[18,1,32,256]{3,2,0,1:T(8,128)(2,1)S(1)} %bitcast.72), channel_id=1, source_target_pairs={{0,8},{4,12},{8,0},{12,4},{16,24},{20,28},{1,9},{5,13},{9,1},{13,5... | collective-permute-start | bytes 884744 | tf_op jit(solution)/shard_map/ppermute | solution.py:339
  35.7 7.7 %collective-permute-start.9 = (bf16[16,1,32,256]{3,2,0,1:T(8,128)(2,1)S(1)}, bf16[16,1,32,256]{3,2,0,1:T(8,128)(2,1)S(1)}, u32[]{:S(2)}, u32[]{:S(2)}) collective-permute-start(bf16[16,1,32,256]{3,2,0,1:T(8,128)(2,1)S(1)} %bitcast.67), channel_id=1, source_target_pairs={{0,16},{4,20},{8,24},{12,28},{1,17},{5,21},{9,25},{13,29},{2,18},{... | collective-permute-start | bytes 786440 | tf_op jit(solution)/shard_map/ppermute | solution.py:341
  42.1 9.0 %collective-permute-start.4 = (bf16[18,1,32,256]{3,2,0,1:T(8,128)(2,1)S(1)}, bf16[18,1,32,256]{3,2,0,1:T(8,128)(2,1)S(1)}, u32[]{:S(2)}, u32[]{:S(2)}) collective-permute-start(bf16[18,1,32,256]{3,2,0,1:T(8,128)(2,1)S(1)} %bitcast.64), channel_id=1, source_target_pairs={{0,16},{4,20},{8,24},{12,28},{1,17},{5,21},{9,25},{13,29},{2,18},{... | collective-permute-start | bytes 884744 | tf_op jit(solution)/shard_map/ppermute | solution.py:341
  44.2 9.6 %collective-permute-start.10 = (bf16[16,1,32,256]{3,2,0,1:T(8,128)(2,1)S(1)}, bf16[16,1,32,256]{3,2,0,1:T(8,128)(2,1)S(1)}, u32[]{:S(2)}, u32[]{:S(2)}) collective-permute-start(bf16[16,1,32,256]{3,2,0,1:T(8,128)(2,1)S(1)} %bitcast.66), channel_id=1, source_target_pairs={{0,8},{4,12},{16,24},{20,28},{24,16},{28,20},{1,9},{5,13},{17,25},... | collective-permute-start | bytes 786440 | tf_op jit(solution)/shard_map/ppermute | solution.py:343
  51.9 8.1 %collective-permute-start.5 = (bf16[18,1,32,256]{3,2,0,1:T(8,128)(2,1)S(1)}, bf16[18,1,32,256]{3,2,0,1:T(8,128)(2,1)S(1)}, u32[]{:S(2)}, u32[]{:S(2)}) collective-permute-start(bf16[18,1,32,256]{3,2,0,1:T(8,128)(2,1)S(1)} %bitcast.63), channel_id=1, source_target_pairs={{0,8},{4,12},{16,24},{20,28},{24,16},{28,20},{1,9},{5,13},{17,25},... | collective-permute-start | bytes 884744 | tf_op jit(solution)/shard_map/ppermute | solution.py:343
  55.4 9.6 %copy-start.4 = (bf16[3,3,256,256]{3,2,1,0:T(8,128)(2,1)S(1)}, bf16[3,3,256,256]{3,2,1,0:T(8,128)(2,1)}, u32[]{:S(2)}) copy-start(bf16[3,3,256,256]{3,2,1,0:T(8,128)(2,1)} %param.11) | copy-start | bytes 3538948
  55.4 9.6 %collective-permute-start.11 = (bf16[16,2,32,256]{3,2,1,0:T(8,128)(2,1)S(1)}, bf16[16,2,32,256]{3,2,1,0:T(8,128)(2,1)S(1)}, u32[]{:S(2)}, u32[]{:S(2)}) collective-permute-start(bf16[16,2,32,256]{3,2,1,0:T(8,128)(2,1)S(1)} %get-tuple-element.30), channel_id=1, source_target_pairs={{0,4},{4,0},{8,12},{12,8},{16,20},{20,16},{24,28},{28,24},{1,5},{5... | collective-permute-start | bytes 1572872 | tf_op jit(solution)/shard_map/ppermute | solution.py:359
  61.7 8.8 %collective-permute-start.6 = (bf16[18,2,32,256]{3,2,1,0:T(8,128)(2,1)S(1)}, bf16[18,2,32,256]{3,2,1,0:T(8,128)(2,1)S(1)}, u32[]{:S(2)}, u32[]{:S(2)}) collective-permute-start(bf16[18,2,32,256]{3,2,1,0:T(8,128)(2,1)S(1)} %get-tuple-element.24), channel_id=1, source_target_pairs={{0,4},{4,0},{8,12},{12,8},{16,20},{20,16},{24,28},{28,24},{1,5},{5... | collective-permute-start | bytes 1769480 | tf_op jit(solution)/shard_map/ppermute | solution.py:359
  65.0 5.5 %copy-start.3 = (bf16[1,32,128,256]{3,2,1,0:T(8,128)(2,1)S(1)}, bf16[1,32,128,256]{3,2,1,0:T(8,128)(2,1)}, u32[]{:S(2)}) copy-start(bf16[1,32,128,256]{3,2,1,0:T(8,128)(2,1)} %param.7) | copy-start | bytes 6291460

commit v2 on v0

v2 whole, which is shorter than its diff:
```python
import functools

import numpy as np
import jax
import jax.numpy as jnp
from jax import lax
from jax.experimental import pallas as pl
from jax.experimental.pallas import tpu as pltpu
from jax.sharding import PartitionSpec as P

F32 = jnp.float32
BF16 = jnp.bfloat16
VMEM = pl.BlockSpec(memory_space=pltpu.VMEM)
HBM = pl.BlockSpec(memory_space=pltpu.HBM)
PARAMS = pltpu.CompilerParams(vmem_limit_bytes=24 * 1024 * 1024)
SLOTS = 16


def cmul(coef, z):
    n = z.shape[-1] // 2
    re, im = z[..., :n], z[..., n:]
    cr, ci = coef
    return jnp.concatenate([cr * re - ci * im, cr * im + ci * re], axis=-1)


def coefficient(tab, i):
    return tab[i : i + 1, :], tab[SLOTS + i : SLOTS + i + 1, :]


def widen(row):
    w = row.shape[0]
    col = lax.broadcasted_iota(jnp.int32, row.shape, 0)
    left = jnp.where(col == 0, 0.0, pltpu.roll(row, 1, 0))
    right = jnp.where(col == w - 1, 0.0, pltpu.roll(row, w - 1, 0))
    return jnp.concatenate([left, row, right], axis=-1).astype(BF16)


def conv_block(wide, weights, start, count):
    w, k = wide.shape[1], wide.shape[2]
    lhs = jnp.concatenate(
        [wide[start + d : start + d + count].reshape(count * w, k) for d in range(3)], axis=-1
    )
    return jnp.dot(lhs, weights[...].reshape(3 * k, -1), preferred_element_type=F32)


def load_weights(core, hbm, vmem, sem):
    copies = []
    for d in range(3):
        source = jnp.where(core == 1, 2 - d, d)
        copies.append(pltpu.make_async_copy(hbm.at[source], vmem.at[d], sem.at[d]))
        copies[-1].start()
    return copies


def my_core():
    return lax.rem(lax.axis_index("tm"), 2)


def convolve(weights, wide, row_of, n, step, finish):
    ready = 0
    for s in range(0, n, step):
        size = min(step, n - s)
        while ready < s + size + 2:
            wide[ready] = widen(row_of(ready))
            ready += 1
        finish(s, size, conv_block(wide, weights, s, size))


def lead_kernel(entries, lo, hi, step, own, w_hbm, decay, phase, feed, frame, weights, tab, factor, wide, dvec, sem):
    core, chip = my_core(), lax.div(lax.axis_index("tm"), 2)
    rows = own.shape[0]
    n = hi - lo
    vectors = [pltpu.make_async_copy(ref, dvec.at[pl.ds(k, 1)], sem.at[3 + k]) for k, ref in enumerate((decay, phase))]
    for copy in vectors:
        copy.start()
    source = jnp.where(core == 1, rows - 1 - hi, lo - 1)
    near = pltpu.make_async_copy(own.at[pl.ds(source, n + 2)], frame.at[pl.ds(source, n + 2)], sem.at[5])
    near.start()
    wcopies = load_weights(core, w_hbm, weights, sem)
    rest = []
    for k, (begin, end) in enumerate(((0, lo - 1), (hi + 1, rows))):
        at = jnp.where(core == 1, rows - end, begin)
        rest.append(
            pltpu.make_async_copy(own.at[pl.ds(at, end - begin)], frame.at[pl.ds(at, end - begin)], sem.at[6 + k])
        )
        rest[-1].start()
    for copy in vectors:
        copy.wait()
    expo, gate = [jnp.float32(0.0)] * SLOTS, [jnp.float32(0.0)] * SLOTS
    for q, slot, power in entries:
        expo[slot] = jnp.where(chip == q, jnp.float32(power), expo[slot])
        gate[slot] = jnp.where(chip == q, jnp.float32(1.0), gate[slot])
    for slot, power in ((8, 1), (9, 1 - core), (10, core)):
        expo[slot], gate[slot] = jnp.asarray(power).astype(F32), jnp.float32(1.0)
    spread = lambda values: jnp.concatenate([jnp.full((1, dvec.shape[1]), v, F32) for v in values], axis=0)
    expo = spread(expo)
    size = spread(gate) * jnp.exp(-expo * dvec[0:1])
    angle = expo * dvec[1:2]
    tab[...] = jnp.concatenate([size * jnp.cos(angle), size * jnp.sin(angle)], axis=0)
    mag = jnp.exp(-dvec[0:1])
    scale = jnp.sqrt(1.0 - mag * mag)
    factor[...] = jnp.concatenate([scale, scale], axis=-1)
    near.wait()
    for copy in wcopies:
        copy.wait()

    def row_of(p):
        return frame[source + jnp.where(core == 1, n + 1 - p, p)].astype(F32)

    def finish(s, count, acc):
        feed[s : s + count] = (acc * factor[...]).reshape((count,) + feed.shape[1:])

    convolve(weights, wide, row_of, n, step, finish)
    for copy in rest:
        copy.wait()


def lead(entries, own, w_in, decay, phase, lo, hi, step):
    rows, w, c = own.shape
    n = hi - lo
    return pl.pallas_call(
        functools.partial(lead_kernel, entries, lo, hi, step),
        out_shape=[
            jax.ShapeDtypeStruct((n, w, c), F32),
            jax.ShapeDtypeStruct(own.shape, BF16),
            jax.ShapeDtypeStruct(w_in.shape, BF16),
            jax.ShapeDtypeStruct((2 * SLOTS, decay.shape[1]), F32),
            jax.ShapeDtypeStruct((1, 2 * decay.shape[1]), F32),
        ],
        in_specs=[HBM] * 4,
        out_specs=[VMEM] * 5,
        scratch_shapes=[
            pltpu.VMEM((n + 2, w, 3 * c), BF16),
            pltpu.VMEM((2, decay.shape[1]), F32),
            pltpu.SemaphoreType.DMA((8,)),
        ],
        compiler_params=PARAMS,
        cost_estimate=pl.CostEstimate(flops=18 * n * w * c * c, bytes_accessed=2 * own.size, transcendentals=0),
        name="lead",
    )(own, w_in, decay, phase)


def pair_kernel(lo, hi, step, frame, oth, weights, tab, factor, feed_own, feed, pay, border, wide):
    core = my_core()
    rows = frame.shape[0]
    n = hi - lo
    source = jnp.where(core == 1, rows - 1 - hi, lo - 1)
    for r in range(2):
        border[0, r] = frame[core * (rows - 2) + r]
        border[1, r] = oth[core * (rows - 2) + r]

    def row_of(p):
        return oth[source + jnp.where(core == 1, n + 1 - p, p)].astype(F32)

    def finish(s, count, acc):
        value = (acc * factor[...]).reshape((count,) + feed.shape[1:])
        feed[s : s + count] = value
        for r in range(count):
            pair = cmul(coefficient(tab, 9), feed_own[s + r]) + cmul(coefficient(tab, 10), value[r])
            pay[s + r] = pair.astype(BF16)

    convolve(weights, wide, row_of, n, step, finish)


def pair_up(frame, oth, weights, tab, factor, feed_own, lo, hi, step):
    rows, w, c = frame.shape
    n = hi - lo
    return pl.pallas_call(
        functools.partial(pair_kernel, lo, hi, step),
        out_shape=[
            jax.ShapeDtypeStruct((n, w, c), F32),
            jax.ShapeDtypeStruct((n, w, c), BF16),
            jax.ShapeDtypeStruct((2, 2, w, c), BF16),
        ],
        in_specs=[VMEM] * 6,
        out_specs=[VMEM] * 3,
        scratch_shapes=[pltpu.VMEM((n + 2, w, 3 * c), BF16)],
        compiler_params=PARAMS,
        cost_estimate=pl.CostEstimate(flops=18 * n * w * c * c, bytes_accessed=2 * oth.size, transcendentals=0),
        name="pair",
    )(frame, oth, weights, tab, factor, feed_own)


def drive_kernel(lo, hi, step, edge, last, *refs):
    refs = list(refs)
    take = lambda k: [refs.pop(0) for _ in range(k)]
    frame, oth, weights, tab, factor = take(5)
    if edge:
        (halo,) = take(1)
    if last:
        (w_hbm,) = take(1)
    feed_own, feed_oth, pay = take(3)
    if last:
        (w_next,) = take(1)
    (wide,) = take(1)
    core = my_core()
    rows = frame.shape[0]
    n = hi - lo
    copies = load_weights(core, w_hbm, w_next, take(1)[0]) if last else []
    if edge:
        space = lax.axis_index("space")
        outer = jnp.where(core == 1, lax.axis_size("space") - 1, 0)
        inside = jnp.where(space == outer, 0.0, 1.0)
    for f, (ref, feed) in enumerate(((frame, feed_own), (oth, feed_oth))):

        def row_of(p):
            depth = lo - 1 + p
            if depth < 0:
                return halo[1 - f, jnp.where(core == 1, -1 - depth, 2 + depth)].astype(F32)
            return ref[jnp.where(core == 1, rows - 1 - depth, depth)].astype(F32)

        def finish(s, count, acc):
            value = (acc * factor[...]).reshape((count,) + feed.shape[1:])
            for r in range(count):
                row = value[r]
                if edge and s + r == 0:
                    row = row * inside
                feed[s + r] = row
                if f == 1:
                    pair = cmul(coefficient(tab, 9), feed_own[s + r]) + cmul(coefficient(tab, 10), row)
                    pay[s + r] = pair.astype(BF16)

        convolve(weights, wide.at[f], row_of, n, step, finish)
    for copy in copies:
        copy.wait()


def drive(frame, oth, weights, tab, factor, lo, hi, step, halo=None, w_out=None):
    rows, w, c = frame.shape
    n = hi - lo
    edge, last = halo is not None, w_out is not None
    args, specs = [frame, oth, weights, tab, factor], [VMEM] * 5
    if edge:
        args, specs = args + [halo], specs + [VMEM]
    if last:
        args, specs = args + [w_out], specs + [HBM]
    shapes = [jax.ShapeDtypeStruct((n, w, c), F32)] * 2 + [jax.ShapeDtypeStruct((n, w, c), BF16)]
    scratch = [pltpu.VMEM((2, n + 2, w, 3 * c), BF16)]
    if last:
        shapes += [jax.ShapeDtypeStruct(w_out.shape, BF16)]
        scratch += [pltpu.SemaphoreType.DMA((3,))]
    return pl.pallas_call(
        functools.partial(drive_kernel, lo, hi, step, edge, last),
        out_shape=shapes,
        in_specs=specs,
        out_specs=[VMEM] * len(shapes),
        scratch_shapes=scratch,
        compiler_params=PARAMS,
        cost_estimate=pl.CostEstimate(flops=36 * n * w * c * c, bytes_accessed=20 * n * w * c, transcendentals=0),
        name="drive",
    )(*args)


def relay_kernel(slot, tab, pair, got, pay):
    cp, cr = coefficient(tab, slot), coefficient(tab, slot + 1)
    for r in range(pair.shape[0]):
        pay[r] = (cmul(cp, pair[r].astype(F32)) + cmul(cr, got[r].astype(F32))).astype(BF16)


def relay(slot, tab, pair, got):
    return pl.pallas_call(
        functools.partial(relay_kernel, slot),
        out_shape=jax.ShapeDtypeStruct(pair.shape, BF16),
        in_specs=[VMEM] * 3,
        out_specs=VMEM,
        compiler_params=PARAMS,
        cost_estimate=pl.CostEstimate(flops=16 * pair.size, bytes_accessed=6 * pair.size, transcendentals=0),
        name="relay",
    )(tab, pair, got)


def output_kernel(lo, hi, begin, end, slot, step, keep, *refs):
    refs = list(refs)
    take = lambda k: [refs.pop(0) for _ in range(k)]
    tab, weights, feed_own, feed_oth, r1, r2, own, oth = take(8)
    kept = None
    if hi < end + 1:
        kept, _ = take(2)
    out, pay = take(2)
    if keep:
        (kept_out,) = take(1)
    wide, block, sem = take(3)
    core = my_core()
    first_core = core == 0
    n, n_out = hi - lo, end - begin
    w, c = own.shape[1:]
    rows = own.shape[0]
    lam = coefficient(tab, 8)
    e1, e2 = coefficient(tab, slot + 2), coefficient(tab, slot + 3)

    def states(r):
        f_own, f_oth = feed_own[r], feed_oth[r]
        carry = cmul(e1, r1[r].astype(F32)) + cmul(e2, r2[r].astype(F32))
        s0 = cmul(lam, carry) + jnp.where(first_core, f_own, f_oth)
        s1 = cmul(lam, s0) + jnp.where(first_core, f_oth, f_own)
        return jnp.where(first_core, s1, s0), jnp.where(first_core, s0, s1)

    ready = 0
    copies = []
    for s in range(0, n_out, step):
        size = min(step, n_out - s)
        while ready < s + size + 2:
            if ready < n:
                pair = states(ready)
                if keep and ready < 2:
                    for f in range(2):
                        kept_out[f, ready] = pair[f].astype(BF16)
            else:
                pair = [kept[f, ready - n].astype(F32) for f in range(2)]
            for f in range(2):
                wide[f, ready] = widen(pair[f])
            ready += 1
        for f, (frame, dst) in enumerate(((oth, pay), (own, block))):
            mixed = conv_block(wide.at[f], weights, s, size).reshape(size, w, c)
            act = 0.5 * mixed * (1.0 + lax.erf(mixed * np.float32(0.5**0.5)))
            for r in range(s, s + size):
                depth = begin + r
                at = jnp.where(core == 1, rows - 1 - depth, depth)
                dst[r] = (frame[at].astype(F32) + act[r - s]).astype(BF16)
                if f == 1:
                    copies.append(pltpu.make_async_copy(block.at[r], out.at[at], sem.at[r]))
                    copies[-1].start()
    for copy in copies:
        copy.wait()


def output(tab, weights, feeds, arrived, own, oth, lo, hi, begin, end, slot, step, keep, kept=None, result=None):
    rows, w, c = own.shape
    n, n_out = hi - lo, end - begin
    args = [tab, weights, *feeds, *arrived, own, oth]
    specs = [VMEM] * len(args)
    alias = {}
    if kept is not None:
        args += [kept, result]
        specs += [VMEM, HBM]
        alias = {len(args) - 1: 0}
    shapes = [jax.ShapeDtypeStruct(own.shape, BF16), jax.ShapeDtypeStruct((n_out, w, c), BF16)]
    out_specs = [HBM, VMEM]
    if keep:
        shapes.append(jax.ShapeDtypeStruct((2, 2, w, c), BF16))
        out_specs.append(VMEM)
    return pl.pallas_call(
        functools.partial(output_kernel, lo, hi, begin, end, slot, step, keep),
        out_shape=shapes,
        in_specs=specs,
        out_specs=out_specs,
        input_output_aliases=alias,
        scratch_shapes=[
            pltpu.VMEM((2, n_out + 2, w, 3 * c), BF16),
            pltpu.VMEM((n_out, w, c), BF16),
            pltpu.SemaphoreType.DMA((n_out,)),
        ],
        compiler_params=PARAMS,
        cost_estimate=pl.CostEstimate(flops=36 * n_out * w * c * c, bytes_accessed=20 * n * w * c, transcendentals=0),
        name="output",
    )(*args)


def place_kernel(spans, *refs):
    parts, out, sem = refs[: len(spans)], refs[-2], refs[-1]
    core = my_core()
    rows = out.shape[0]
    copies = []
    for part, (begin, end) in zip(parts, spans):
        for r in range(end - begin):
            at = jnp.where(core == 1, begin + r, rows - 1 - begin - r)
            copies.append(pltpu.make_async_copy(part.at[r], out.at[at], sem.at[len(copies)]))
            copies[-1].start()
    for copy in copies:
        copy.wait()


def place(parts, spans, result):
    return pl.pallas_call(
        functools.partial(place_kernel, spans),
        out_shape=jax.ShapeDtypeStruct(result.shape, result.dtype),
        in_specs=[VMEM] * len(parts) + [HBM],
        out_specs=HBM,
        input_output_aliases={len(parts): 0},
        scratch_shapes=[pltpu.SemaphoreType.DMA((sum(end - begin for begin, end in spans),))],
        compiler_params=PARAMS,
        name="place",
    )(*parts, result)


ALONG_X = [(0, 1), (1, 0), (2, 3)], [(0, 2), (1, 3)]
ALONG_Y = [(0, 2), (1, 3)], [(0, 1), (2, 3), (3, 2)]


def roles(n):
    if n != 8:
        return [(q, slot, 0) for q in range(n // 2) for slot in (2, 6)]
    along_x = [(0, 0, 2), (0, 1, 0), (1, 0, 0), (1, 1, 2), (1, 2, 0), (2, 3, 0), (3, 2, 0), (3, 3, 2)]
    along_y = [(0, 4, 0), (2, 4, 0), (2, 5, 4), (3, 5, 0), (1, 7, 0), (2, 6, 2), (2, 7, 0), (3, 6, 2), (3, 7, 0)]
    return along_x + along_y


def both_cores(pairs):
    return [(2 * a + k, 2 * b + k) for a, b in pairs for k in range(2)]


def exchange(n, slot, tab, pair, decay, phase):
    if n == 8:
        one, two = ALONG_X if slot == 0 else ALONG_Y
        r1 = lax.ppermute(pair, "tm", both_cores(one))
        r2 = lax.ppermute(relay(slot, tab, pair, r1), "tm", both_cores(two))
        return r1, r2
    chips, stride, total = n // 2, 1, pair.astype(F32)
    while stride < chips:
        steps = both_cores([(i, i + stride) for i in range(chips - stride)])
        moved = lax.ppermute(total.astype(BF16), "tm", steps).astype(F32)
        size, angle = jnp.exp(-2.0 * stride * decay), 2.0 * stride * phase
        total = total + cmul((size * jnp.cos(angle), size * jnp.sin(angle)), moved)
        stride *= 2
    carry = lax.ppermute(total.astype(BF16), "tm", both_cores([(i, i + 1) for i in range(chips - 1)]))
    return carry, jnp.zeros_like(carry)


def on_device(n, n_space, frames_in, w_input, decay_rate, phase, w_output):
    own = frames_in[0]
    rows, w, c = own.shape
    decay, phase = decay_rate[None], phase[None]
    w_in = w_input.reshape(3, 3 * c, -1)
    w_out = w_output.reshape(3, -1, c)
    swap = [(i, i ^ 1) for i in range(n)]
    step = 3
    oth = lax.ppermute(own, "tm", swap)

    half = rows // 2
    cut = half // 2
    own1, frame, weights, tab, factor = lead(roles(n), own, w_in, decay, phase, cut, half + 1, step)
    oth1, pair1, border = pair_up(frame, oth, weights, tab, factor, own1, cut, half + 1, step)
    links = [
        ((t ^ 1) * n_space + s, t * n_space + s + 1) if t % 2 == 0 else ((t ^ 1) * n_space + s + 1, t * n_space + s)
        for t in range(n)
        for s in range(n_space - 1)
    ]
    halo = lax.ppermute(border, ("tm", "space"), links)
    arrived1 = exchange(n, 0, tab, pair1, decay, phase)
    own2, oth2, pair2, weights = drive(frame, oth, weights, tab, factor, -1, cut, step, halo=halo, w_out=w_out)
    arrived2 = exchange(n, 4, tab, pair2, decay, phase)
    result, pay1, kept = output(
        tab, weights, (own1, oth1), arrived1, frame, oth, cut, half + 1, cut + 1, half, 0, step, True
    )
    got1 = lax.ppermute(pay1, "tm", swap)
    result, pay2 = output(
        tab, weights, (own2, oth2), arrived2, frame, oth, -1, cut, 0, cut + 1, 4, step, False, kept=kept, result=result
    )
    got2 = lax.ppermute(pay2, "tm", swap)
    return place([got1, got2], [(cut + 1, half), (0, cut + 1)], result)[None]


def solution(mesh):
    in_specs = (P("tm", "space", None, None), P(), P(), P(), P())
    out_specs = P("tm", "space", None, None)
    body = functools.partial(on_device, mesh.shape["tm"], mesh.shape["space"])
    return jax.shard_map(body, mesh=mesh, in_specs=in_specs, out_specs=out_specs, check_vma=False)
```

time: 258 us -> 64.9 us (0.25)
  the two profiles are of different devices: /device:TPU:0 before, /device:TPU:15 now
where the time goes in v2:
time: 64.9 us; the launch traced here: 64.6 us
  waiting for transfers between devices  30.1 us (46%)
  Pallas kernels  18.6 us (29%)
  starting transfers between devices  11.5 us (18%)
  local copies, waits for them, and re-layouts  4.18 us (6%)
    ppermute x2, waiting for transfers between devices, exchange(): r1 = lax.ppermute(pair, 'tm', both_cores(one))  14.1 us
    ppermute x2, waiting for transfers between devices, exchange(): r2 = lax.ppermute(relay(slot, tab, pair, r1), 'tm', both_cores(two))  10.2 us
    pallas_call x2, Pallas kernels, output(): pl.pallas_call(functools.partial(output_kernel, lo, hi, begin, end, slot,...  8.34 us
    unnamed x10, local copies, waits for them, and re-layouts  4.18 us
    pallas_call x1, Pallas kernels, drive(): pl.pallas_call(functools.partial(drive_kernel, lo, hi, step, edge, last),...  3.68 us
    ppermute x1, waiting for transfers between devices, on_device(): halo = lax.ppermute(border, ('tm', 'space'), links)  3.58 us
    ppermute x2, starting transfers between devices, exchange(): r2 = lax.ppermute(relay(slot, tab, pair, r1), 'tm', both_cores(two))  3.39 us
    ppermute x1, starting transfers between devices, on_device(): halo = lax.ppermute(border, ('tm', 'space'), links)  3.1 us
  transfers between devices with their start and end apart: 8, of which 5 were waited for; matrix products, arithmetic and copies ran while one was open for 0% of the time, Pallas kernels for 17%

profile of v2, /device:TPU:15, one launch (start us, length us, event | category | flops | bytes accessed | tf_op | source)
XLA Modules:
  0.0 64.6 jit_solution(12984294363224936694)
XLA Ops:
  0.0 0.7 %collective-permute-start = (bf16[32,128,256]{2,1,0:T(8,128)(2,1)}, bf16[32,128,256]{2,1,0:T(8,128)(2,1)S(1)}, u32[]{:S(2)}, u32[]{:S(2)}) collective-permute-start(bf16[32,128,256]{2,1,0:T(8,128)(2,1)} %bitcast.6), channel_id=1, source_target_pairs={{0,4},{4,0},{8,12},{12,8},{16,20},{20,16},{24,28},{28,24},{1,5},{5... | collective-permute-start | bytes 6291464 | tf_op jit(solution)/shard_map/ppermute | solution.py:427
  0.7 1.6 %copy-done = bf16[1,32,128,256]{3,2,1,0:T(8,128)(2,1)S(1)} copy-done((bf16[1,32,128,256]{3,2,1,0:T(8,128)(2,1)S(1)}, bf16[1,32,128,256]{3,2,1,0:T(8,128)(2,1)}, u32[]{:S(2)}) %copy-start) | copy-done | bytes 2097176
  2.3 1.3 %copy-done.1 = bf16[3,3,256,256]{3,2,1,0:T(8,128)(2,1)S(1)} copy-done((bf16[3,3,256,256]{3,2,1,0:T(8,128)(2,1)S(1)}, bf16[3,3,256,256]{3,2,1,0:T(8,128)(2,1)}, u32[]{:S(2)}) %copy-start.1) | copy-done | bytes 1179672
  3.5 0.7 %copy-done.3 = f32[128]{0:T(128)S(1)} copy-done((f32[128]{0:T(128)S(1)}, f32[128]{0:T(128)}, u32[]{:S(2)}) %copy-start.3) | copy-done | bytes 536
  4.2 0.7 %copy-done.4 = f32[128]{0:T(128)S(1)} copy-done((f32[128]{0:T(128)S(1)}, f32[128]{0:T(128)}, u32[]{:S(2)}) %copy-start.4) | copy-done | bytes 536
  4.9 3.1 %lead.1 = (f32[9,128,256]{2,1,0:T(8,128)S(1)}, bf16[32,128,256]{2,1,0:T(8,128)(2,1)S(1)}, bf16[3,768,256]{2,1,0:T(8,128)(2,1)S(1)}, f32[32,128]{1,0:T(8,128)S(1)}, f32[1,256]{1,0:T(1,128)S(1)}) custom-call(bf16[32,128,256]{2,1,0:T(8,128)(2,1)S(1)} %bitcast.7, bf16[3,768,256]{2,1,0:T(8,128)(2,1)S(1)} %bitcast.8, f32[1,128]{1,0:T(1,128)S(1)} %bitcast.10, ...), custom_call_target="tpu_custom_call" | custom-call | flops 1358954496 | bytes 2097152 | tf_op jit(solution)/shard_map/lead/pallas_call | solution.py:121
  7.9 1.7 %pair.1 = (f32[9,128,256]{2,1,0:T(8,128)S(1)}, bf16[9,128,256]{2,1,0:T(8,128)(2,1)S(1)}, bf16[2,2,128,256]{3,2,1,0:T(8,128)(2,1)S(1)}) custom-call(bf16[32,128,256]{2,1,0:T(8,128)(2,1)S(1)} %get-tuple-element.23.frame.refs_0_.refs_6_, bf16[32,128,256]{2,1,0:T(8,128)(2,1)S(1)} %collective-permute-done.oth.refs_1_.refs_7_, ...), custom_call_target="tpu_custom_call" | custom-call | flops 1358954496 | bytes 2097152 | tf_op jit(solution)/shard_map/pair/pallas_call | solution.py:168
  9.7 3.1 %collective-permute-start.1 = (bf16[2,2,128,256]{3,2,1,0:T(8,128)(2,1)S(1)}, bf16[2,2,128,256]{3,2,1,0:T(8,128)(2,1)S(1)}, u32[]{:S(2)}, u32[]{:S(2)}) collective-permute-start(bf16[2,2,128,256]{3,2,1,0:T(8,128)(2,1)S(1)} %get-tuple-element.27), channel_id=1, source_target_pairs={{4,1},{5,2},{6,3},{1,4},{2,5},{3,6},{12,9},{13,10},{14,11},{9,12},... | collective-permute-start | bytes 786440 | tf_op jit(solution)/shard_map/ppermute | solution.py:438
  12.8 1.3 %collective-permute-start.2 = (bf16[9,128,256]{2,1,0:T(8,128)(2,1)S(1)}, bf16[9,128,256]{2,1,0:T(8,128)(2,1)S(1)}, u32[]{:S(2)}, u32[]{:S(2)}) collective-permute-start(bf16[9,128,256]{2,1,0:T(8,128)(2,1)S(1)} %get-tuple-element.30.pair), channel_id=1, source_target_pairs={{0,8},{4,12},{8,0},{12,4},{16,24},{20,28},{1,9},{5,13},{9,1},{13,5... | collective-permute-start | bytes 1769480 | tf_op jit(solution)/shard_map/ppermute | solution.py:405
  14.1 3.6 %collective-permute-done.1.refs_5_ = bf16[2,2,128,256]{3,2,1,0:T(8,128)(2,1)S(1)} collective-permute-done((bf16[2,2,128,256]{3,2,1,0:T(8,128)(2,1)S(1)}, bf16[2,2,128,256]{3,2,1,0:T(8,128)(2,1)S(1)}, u32[]{:S(2)}, u32[]{:S(2)}) %collective-permute-start.1) | collective-permute-done | bytes 262176 | tf_op jit(solution)/shard_map/ppermute | solution.py:438
  17.6 3.7 %drive.1 = (f32[9,128,256]{2,1,0:T(8,128)S(1)}, f32[9,128,256]{2,1,0:T(8,128)S(1)}, bf16[9,128,256]{2,1,0:T(8,128)(2,1)S(1)}, bf16[3,768,256]{2,1,0:T(8,128)(2,1)S(1)}) custom-call(bf16[32,128,256]{2,1,0:T(8,128)(2,1)S(1)} %get-tuple-element.23.frame.refs_0_.refs_6_, bf16[32,128,256]{2,1,0:T(8,128)(2,1)S(1)} %collective-permute-done.oth.refs_1_.refs_7_, ...), custom_call_target="tpu_custom_call" | custom-call | flops 2717908992 | bytes 5898240 | tf_op jit(solution)/shard_map/drive/pallas_call | solution.py:242
  21.3 1.3 %collective-permute-start.5 = (bf16[9,128,256]{2,1,0:T(8,128)(2,1)S(1)}, bf16[9,128,256]{2,1,0:T(8,128)(2,1)S(1)}, u32[]{:S(2)}, u32[]{:S(2)}) collective-permute-start(bf16[9,128,256]{2,1,0:T(8,128)(2,1)S(1)} %get-tuple-element.34.pair), channel_id=1, source_target_pairs={{0,16},{4,20},{8,24},{12,28},{1,17},{5,21},{9,25},{13,29},{2,18},{... | collective-permute-start | bytes 1769480 | tf_op jit(solution)/shard_map/ppermute | solution.py:405
  22.6 7.2 %collective-permute-done.2.got.refs_4_ = bf16[9,128,256]{2,1,0:T(8,128)(2,1)S(1)} collective-permute-done((bf16[9,128,256]{2,1,0:T(8,128)(2,1)S(1)}, bf16[9,128,256]{2,1,0:T(8,128)(2,1)S(1)}, u32[]{:S(2)}, u32[]{:S(2)}) %collective-permute-start.2) | collective-permute-done | bytes 589856 | tf_op jit(solution)/shard_map/ppermute | solution.py:405
  29.8 0.4 relay.2
  30.2 1.3 %collective-permute-start.3 = (bf16[9,128,256]{2,1,0:T(8,128)(2,1)S(1)}, bf16[9,128,256]{2,1,0:T(8,128)(2,1)S(1)}, u32[]{:S(2)}, u32[]{:S(2)}) collective-permute-start(bf16[9,128,256]{2,1,0:T(8,128)(2,1)S(1)} %relay.2), channel_id=1, source_target_pairs={{0,16},{4,20},{8,24},{12,28},{1,17},{5,21},{9,25},{13,29},{2,18},{... | collective-permute-start | bytes 1769480 | tf_op jit(solution)/shard_map/ppermute | solution.py:406
  31.5 6.9 %collective-permute-done.5.got.refs_4_ = bf16[9,128,256]{2,1,0:T(8,128)(2,1)S(1)} collective-permute-done((bf16[9,128,256]{2,1,0:T(8,128)(2,1)S(1)}, bf16[9,128,256]{2,1,0:T(8,128)(2,1)S(1)}, u32[]{:S(2)}, u32[]{:S(2)}) %collective-permute-start.5) | collective-permute-done | bytes 589856 | tf_op jit(solution)/shard_map/ppermute | solution.py:405
  38.4 0.4 relay.3
  38.8 2.1 %collective-permute-start.6 = (bf16[9,128,256]{2,1,0:T(8,128)(2,1)S(1)}, bf16[9,128,256]{2,1,0:T(8,128)(2,1)S(1)}, u32[]{:S(2)}, u32[]{:S(2)}) collective-permute-start(bf16[9,128,256]{2,1,0:T(8,128)(2,1)S(1)} %relay.3), channel_id=1, source_target_pairs={{0,8},{4,12},{16,24},{20,28},{24,16},{28,20},{1,9},{5,13},{17,25},... | collective-permute-start | bytes 1769480 | tf_op jit(solution)/shard_map/ppermute | solution.py:406
  40.9 10.2 %collective-permute-done.3.refs_5_ = bf16[9,128,256]{2,1,0:T(8,128)(2,1)S(1)} collective-permute-done((bf16[9,128,256]{2,1,0:T(8,128)(2,1)S(1)}, bf16[9,128,256]{2,1,0:T(8,128)(2,1)S(1)}, u32[]{:S(2)}, u32[]{:S(2)}) %collective-permute-start.3) | collective-permute-done | bytes 589856 | tf_op jit(solution)/shard_map/ppermute | solution.py:406
  51.0 3.8 %output.2 = (bf16[32,128,256]{2,1,0:T(8,128)(2,1)}, bf16[7,128,256]{2,1,0:T(8,128)(2,1)S(1)}, bf16[2,2,128,256]{3,2,1,0:T(8,128)(2,1)S(1)}) custom-call(f32[32,128]{1,0:T(8,128)S(1)} %get-tuple-element.22.tab.refs_3_.refs_0_, bf16[3,768,256]{2,1,0:T(8,128)(2,1)S(1)} %get-tuple-element.28.refs_1_, f32[9,128,256]{2,1,0:T(8,128)S(1)} %get-tuple-element.26.feed_own.refs_2_, ...), custom_call_target="tpu_custom_call" | custom-call | flops 2113929216 | bytes 5898240 | tf_op jit(solution)/shard_map/output/pallas_call | solution.py:342
  54.8 4.6 %output.3 = (bf16[32,128,256]{2,1,0:T(8,128)(2,1)}, bf16[9,128,256]{2,1,0:T(8,128)(2,1)S(1)}) custom-call(f32[32,128]{1,0:T(8,128)S(1)} %get-tuple-element.22.tab.refs_3_.refs_0_, bf16[3,768,256]{2,1,0:T(8,128)(2,1)S(1)} %get-tuple-element.28.refs_1_, f32[9,128,256]{2,1,0:T(8,128)S(1)} %get-tuple-element.32.refs_2_, ...), custom_call_target="tpu_custom_call", output_to_operand_aliasing={{0}: (9, {})} | custom-call | flops 2717908992 | bytes 5898240 | tf_op jit(solution)/shard_map/output/pallas_call | solution.py:342
  59.4 1.6 %collective-permute-start.7 = (bf16[9,128,256]{2,1,0:T(8,128)(2,1)S(1)}, bf16[9,128,256]{2,1,0:T(8,128)(2,1)S(1)}, u32[]{:S(2)}, u32[]{:S(2)}) collective-permute-start(bf16[9,128,256]{2,1,0:T(8,128)(2,1)S(1)} %get-tuple-element.37), channel_id=1, source_target_pairs={{0,4},{4,0},{8,12},{12,8},{16,20},{20,16},{24,28},{28,24},{1,5},{5... | collective-permute-start | bytes 1769480 | tf_op jit(solution)/shard_map/ppermute | solution.py:449
  61.1 2.2 %collective-permute-done.4.refs_0_ = bf16[7,128,256]{2,1,0:T(8,128)(2,1)S(1)} collective-permute-done((bf16[7,128,256]{2,1,0:T(8,128)(2,1)S(1)}, bf16[7,128,256]{2,1,0:T(8,128)(2,1)S(1)}, u32[]{:S(2)}, u32[]{:S(2)}) %collective-permute-start.4) | collective-permute-done | bytes 458784 | tf_op jit(solution)/shard_map/ppermute | solution.py:445
  63.3 1.1 %place.1 = bf16[32,128,256]{2,1,0:T(8,128)(2,1)} custom-call(bf16[7,128,256]{2,1,0:T(8,128)(2,1)S(1)} %collective-permute-done.4.refs_0_, bf16[9,128,256]{2,1,0:T(8,128)(2,1)S(1)} %collective-permute-done.7.refs_1_, bf16[32,128,256]{2,1,0:T(8,128)(2,1)} %get-tuple-element.38.refs_2_), custom_call_target="tpu_custom_call", output_to_operand_aliasing={{}: (2, {})} | custom-call | tf_op jit(solution)/shard_map/place/pallas_call | solution.py:374
  (10 shorter events, 0.1 us)
Async XLA Ops:
  0.0 7.9 %collective-permute-start = (bf16[32,128,256]{2,1,0:T(8,128)(2,1)}, bf16[32,128,256]{2,1,0:T(8,128)(2,1)S(1)}, u32[]{:S(2)}, u32[]{:S(2)}) collective-permute-start(bf16[32,128,256]{2,1,0:T(8,128)(2,1)} %bitcast.6), channel_id=1, source_target_pairs={{0,4},{4,0},{8,12},{12,8},{16,20},{20,16},{24,28},{28,24},{1,5},{5... | collective-permute-start | bytes 6291464 | tf_op jit(solution)/shard_map/ppermute | solution.py:427
  0.7 1.6 %copy-start = (bf16[1,32,128,256]{3,2,1,0:T(8,128)(2,1)S(1)}, bf16[1,32,128,256]{3,2,1,0:T(8,128)(2,1)}, u32[]{:S(2)}) copy-start(bf16[1,32,128,256]{3,2,1,0:T(8,128)(2,1)} %param.5) | copy-start | bytes 6291460
  2.3 1.3 %copy-start.1 = (bf16[3,3,256,256]{3,2,1,0:T(8,128)(2,1)S(1)}, bf16[3,3,256,256]{3,2,1,0:T(8,128)(2,1)}, u32[]{:S(2)}) copy-start(bf16[3,3,256,256]{3,2,1,0:T(8,128)(2,1)} %param.6) | copy-start | bytes 3538948
  3.5 0.7 %copy-start.3 = (f32[128]{0:T(128)S(1)}, f32[128]{0:T(128)}, u32[]{:S(2)}) copy-start(f32[128]{0:T(128)} %param.7) | copy-start | bytes 1540
  4.2 0.7 %copy-start.4 = (f32[128]{0:T(128)S(1)}, f32[128]{0:T(128)}, u32[]{:S(2)}) copy-start(f32[128]{0:T(128)} %param.8) | copy-start | bytes 1540
  7.9 9.7 %copy-start.2 = (bf16[3,3,256,256]{3,2,1,0:T(8,128)(2,1)S(1)}, bf16[3,3,256,256]{3,2,1,0:T(8,128)(2,1)}, u32[]{:S(2)}) copy-start(bf16[3,3,256,256]{3,2,1,0:T(8,128)(2,1)} %param.9) | copy-start | bytes 3538948
  9.7 8.0 %collective-permute-start.1 = (bf16[2,2,128,256]{3,2,1,0:T(8,128)(2,1)S(1)}, bf16[2,2,128,256]{3,2,1,0:T(8,128)(2,1)S(1)}, u32[]{:S(2)}, u32[]{:S(2)}) collective-permute-start(bf16[2,2,128,256]{3,2,1,0:T(8,128)(2,1)S(1)} %get-tuple-element.27), channel_id=1, source_target_pairs={{4,1},{5,2},{6,3},{1,4},{2,5},{3,6},{12,9},{13,10},{14,11},{9,12},... | collective-permute-start | bytes 786440 | tf_op jit(solution)/shard_map/ppermute | solution.py:438
  12.8 17.1 %collective-permute-start.2 = (bf16[9,128,256]{2,1,0:T(8,128)(2,1)S(1)}, bf16[9,128,256]{2,1,0:T(8,128)(2,1)S(1)}, u32[]{:S(2)}, u32[]{:S(2)}) collective-permute-start(bf16[9,128,256]{2,1,0:T(8,128)(2,1)S(1)} %get-tuple-element.30.pair), channel_id=1, source_target_pairs={{0,8},{4,12},{8,0},{12,4},{16,24},{20,28},{1,9},{5,13},{9,1},{13,5... | collective-permute-start | bytes 1769480 | tf_op jit(solution)/shard_map/ppermute | solution.py:405
  21.3 17.1 %collective-permute-start.5 = (bf16[9,128,256]{2,1,0:T(8,128)(2,1)S(1)}, bf16[9,128,256]{2,1,0:T(8,128)(2,1)S(1)}, u32[]{:S(2)}, u32[]{:S(2)}) collective-permute-start(bf16[9,128,256]{2,1,0:T(8,128)(2,1)S(1)} %get-tuple-element.34.pair), channel_id=1, source_target_pairs={{0,16},{4,20},{8,24},{12,28},{1,17},{5,21},{9,25},{13,29},{2,18},{... | collective-permute-start | bytes 1769480 | tf_op jit(solution)/shard_map/ppermute | solution.py:405
  30.2 20.8 %collective-permute-start.3 = (bf16[9,128,256]{2,1,0:T(8,128)(2,1)S(1)}, bf16[9,128,256]{2,1,0:T(8,128)(2,1)S(1)}, u32[]{:S(2)}, u32[]{:S(2)}) collective-permute-start(bf16[9,128,256]{2,1,0:T(8,128)(2,1)S(1)} %relay.2), channel_id=1, source_target_pairs={{0,16},{4,20},{8,24},{12,28},{1,17},{5,21},{9,25},{13,29},{2,18},{... | collective-permute-start | bytes 1769480 | tf_op jit(solution)/shard_map/ppermute | solution.py:406
  38.8 16.1 %collective-permute-start.6 = (bf16[9,128,256]{2,1,0:T(8,128)(2,1)S(1)}, bf16[9,128,256]{2,1,0:T(8,128)(2,1)S(1)}, u32[]{:S(2)}, u32[]{:S(2)}) collective-permute-start(bf16[9,128,256]{2,1,0:T(8,128)(2,1)S(1)} %relay.3), channel_id=1, source_target_pairs={{0,8},{4,12},{16,24},{20,28},{24,16},{28,20},{1,9},{5,13},{17,25},... | collective-permute-start | bytes 1769480 | tf_op jit(solution)/shard_map/ppermute | solution.py:406
  59.4 3.9 %collective-permute-start.7 = (bf16[9,128,256]{2,1,0:T(8,128)(2,1)S(1)}, bf16[9,128,256]{2,1,0:T(8,128)(2,1)S(1)}, u32[]{:S(2)}, u32[]{:S(2)}) collective-permute-start(bf16[9,128,256]{2,1,0:T(8,128)(2,1)S(1)} %get-tuple-element.37), channel_id=1, source_target_pairs={{0,4},{4,0},{8,12},{12,8},{16,20},{20,16},{24,28},{28,24},{1,5},{5... | collective-permute-start | bytes 1769480 | tf_op jit(solution)/shard_map/ppermute | solution.py:449
  61.0 2.3 %collective-permute-start.4 = (bf16[7,128,256]{2,1,0:T(8,128)(2,1)S(1)}, bf16[7,128,256]{2,1,0:T(8,128)(2,1)S(1)}, u32[]{:S(2)}, u32[]{:S(2)}) collective-permute-start(bf16[7,128,256]{2,1,0:T(8,128)(2,1)S(1)} %get-tuple-element.31), channel_id=1, source_target_pairs={{0,4},{4,0},{8,12},{12,8},{16,20},{20,16},{24,28},{28,24},{1,5},{5... | collective-permute-start | bytes 1376264 | tf_op jit(solution)/shard_map/ppermute | solution.py:445

commit v3 on v2

--- a/solution.py
+++ b/solution.py
@@ -137,17 +137,14 @@
         compiler_params=PARAMS,
         cost_estimate=pl.CostEstimate(flops=18 * n * w * c * c, bytes_accessed=2 * own.size, transcendentals=0),
         name="lead",
-    )(own, w_in, decay, phase)
-
-
-def pair_kernel(lo, hi, step, frame, oth, weights, tab, factor, feed_own, feed, pay, border, wide):
+    )(*(pltpu.with_memory_space_constraint(x, pltpu.HBM) for x in (own, w_in, decay, phase)))
+
+
+def pair_kernel(lo, hi, step, frame, oth, weights, tab, factor, feed_own, feed, pay, wide):
     core = my_core()
     rows = frame.shape[0]
     n = hi - lo
     source = jnp.where(core == 1, rows - 1 - hi, lo - 1)
-    for r in range(2):
-        border[0, r] = frame[core * (rows - 2) + r]
-        border[1, r] = oth[core * (rows - 2) + r]
 
     def row_of(p):
         return oth[source + jnp.where(core == 1, n + 1 - p, p)].astype(F32)
@@ -170,10 +167,9 @@
         out_shape=[
             jax.ShapeDtypeStruct((n, w, c), F32),
             jax.ShapeDtypeStruct((n, w, c), BF16),
-            jax.ShapeDtypeStruct((2, 2, w, c), BF16),
         ],
         in_specs=[VMEM] * 6,
-        out_specs=[VMEM] * 3,
+        out_specs=[VMEM] * 2,
         scratch_shapes=[pltpu.VMEM((n + 2, w, 3 * c), BF16)],
         compiler_params=PARAMS,
         cost_estimate=pl.CostEstimate(flops=18 * n * w * c * c, bytes_accessed=2 * oth.size, transcendentals=0),
@@ -181,22 +177,27 @@
     )(frame, oth, weights, tab, factor, feed_own)
 
 
-def drive_kernel(lo, hi, step, edge, last, *refs):
+def drive_kernel(lo, hi, step, edge, second, *refs):
     refs = list(refs)
     take = lambda k: [refs.pop(0) for _ in range(k)]
     frame, oth, weights, tab, factor = take(5)
     if edge:
         (halo,) = take(1)
-    if last:
+    if second:
         (w_hbm,) = take(1)
     feed_own, feed_oth, pay = take(3)
-    if last:
-        (w_next,) = take(1)
+    if second:
+        w_next, border = take(2)
     (wide,) = take(1)
     core = my_core()
     rows = frame.shape[0]
     n = hi - lo
-    copies = load_weights(core, w_hbm, w_next, take(1)[0]) if last else []
+    copies = []
+    if second:
+        copies = load_weights(core, w_hbm, w_next, take(1)[0])
+        for f, ref in enumerate((frame, oth)):
+            for r in range(2):
+                border[f, r] = ref[core * (rows - 2) + r]
     if edge:
         space = lax.axis_index("space")
         outer = jnp.where(core == 1, lax.axis_size("space") - 1, 0)
@@ -228,19 +229,19 @@
 def drive(frame, oth, weights, tab, factor, lo, hi, step, halo=None, w_out=None):
     rows, w, c = frame.shape
     n = hi - lo
-    edge, last = halo is not None, w_out is not None
+    edge, second = halo is not None, w_out is not None
     args, specs = [frame, oth, weights, tab, factor], [VMEM] * 5
     if edge:
         args, specs = args + [halo], specs + [VMEM]
-    if last:
+    if second:
         args, specs = args + [w_out], specs + [HBM]
     shapes = [jax.ShapeDtypeStruct((n, w, c), F32)] * 2 + [jax.ShapeDtypeStruct((n, w, c), BF16)]
     scratch = [pltpu.VMEM((2, n + 2, w, 3 * c), BF16)]
-    if last:
-        shapes += [jax.ShapeDtypeStruct(w_out.shape, BF16)]
+    if second:
+        shapes += [jax.ShapeDtypeStruct(w_out.shape, BF16), jax.ShapeDtypeStruct((2, 2, w, c), BF16)]
         scratch += [pltpu.SemaphoreType.DMA((3,))]
     return pl.pallas_call(
-        functools.partial(drive_kernel, lo, hi, step, edge, last),
+        functools.partial(drive_kernel, lo, hi, step, edge, second),
         out_shape=shapes,
         in_specs=specs,
         out_specs=[VMEM] * len(shapes),
@@ -269,17 +270,24 @@
     )(tab, pair, got)
 
 
-def output_kernel(lo, hi, begin, end, slot, step, keep, *refs):
+def output_kernel(lo, hi, begin, end, slot, step, keep, which, *refs):
     refs = list(refs)
     take = lambda k: [refs.pop(0) for _ in range(k)]
     tab, weights, feed_own, feed_oth, r1, r2, own, oth = take(8)
-    kept = None
+    kept = out = pay = block = None
     if hi < end + 1:
-        kept, _ = take(2)
-    out, pay = take(2)
+        (kept,) = take(1)
+        if 1 in which:
+            take(1)
+    if 1 in which:
+        (out,) = take(1)
+    if 0 in which:
+        (pay,) = take(1)
     if keep:
         (kept_out,) = take(1)
-    wide, block, sem = take(3)
+    (wide,) = take(1)
+    if 1 in which:
+        block, sem = take(2)
     core = my_core()
     first_core = core == 0
     n, n_out = hi - lo, end - begin
@@ -307,10 +315,11 @@
                         kept_out[f, ready] = pair[f].astype(BF16)
             else:
                 pair = [kept[f, ready - n].astype(F32) for f in range(2)]
-            for f in range(2):
+            for f in which:
                 wide[f, ready] = widen(pair[f])
             ready += 1
-        for f, (frame, dst) in enumerate(((oth, pay), (own, block))):
+        for f in which:
+            frame, dst = ((oth, pay), (own, block))[f]
             mixed = conv_block(wide.at[f], weights, s, size).reshape(size, w, c)
             act = 0.5 * mixed * (1.0 + lax.erf(mixed * np.float32(0.5**0.5)))
             for r in range(s, s + size):
@@ -324,34 +333,42 @@
         copy.wait()
 
 
-def output(tab, weights, feeds, arrived, own, oth, lo, hi, begin, end, slot, step, keep, kept=None, result=None):
+def output(tab, weights, feeds, arrived, own, oth, lo, hi, begin, end, slot, step, keep, which=(0, 1), kept=None, result=None):
     rows, w, c = own.shape
     n, n_out = hi - lo, end - begin
     args = [tab, weights, *feeds, *arrived, own, oth]
     specs = [VMEM] * len(args)
     alias = {}
     if kept is not None:
-        args += [kept, result]
-        specs += [VMEM, HBM]
-        alias = {len(args) - 1: 0}
-    shapes = [jax.ShapeDtypeStruct(own.shape, BF16), jax.ShapeDtypeStruct((n_out, w, c), BF16)]
-    out_specs = [HBM, VMEM]
+        args += [kept]
+        specs += [VMEM]
+        if 1 in which:
+            args += [result]
+            specs += [HBM]
+            alias = {len(args) - 1: 0}
+    shapes, out_specs = [], []
+    scratch = [pltpu.VMEM((2, n_out + 2, w, 3 * c), BF16)]
+    if 1 in which:
+        shapes += [jax.ShapeDtypeStruct(own.shape, BF16)]
+        out_specs += [HBM]
+        scratch += [pltpu.VMEM((n_out, w, c), BF16), pltpu.SemaphoreType.DMA((n_out,))]
+    if 0 in which:
+        shapes += [jax.ShapeDtypeStruct((n_out, w, c), BF16)]
+        out_specs += [VMEM]
     if keep:
         shapes.append(jax.ShapeDtypeStruct((2, 2, w, c), BF16))
         out_specs.append(VMEM)
     return pl.pallas_call(
-        functools.partial(output_kernel, lo, hi, begin, end, slot, step, keep),
+        functools.partial(output_kernel, lo, hi, begin, end, slot, step, keep, which),
         out_shape=shapes,
         in_specs=specs,
         out_specs=out_specs,
         input_output_aliases=alias,
-        scratch_shapes=[
-            pltpu.VMEM((2, n_out + 2, w, 3 * c), BF16),
-            pltpu.VMEM((n_out, w, c), BF16),
-            pltpu.SemaphoreType.DMA((n_out,)),
-        ],
-        compiler_params=PARAMS,
-        cost_estimate=pl.CostEstimate(flops=36 * n_out * w * c * c, bytes_accessed=20 * n * w * c, transcendentals=0),
+        scratch_shapes=scratch,
+        compiler_params=PARAMS,
+        cost_estimate=pl.CostEstimate(
+            flops=18 * len(which) * n_out * w * c * c, bytes_accessed=20 * n * w * c, transcendentals=0
+        ),
         name="output",
     )(*args)
 
@@ -427,27 +444,42 @@
     oth = lax.ppermute(own, "tm", swap)
 
     half = rows // 2
-    cut = half // 2
-    own1, frame, weights, tab, factor = lead(roles(n), own, w_in, decay, phase, cut, half + 1, step)
-    oth1, pair1, border = pair_up(frame, oth, weights, tab, factor, own1, cut, half + 1, step)
+    total, parts = half + 2, 3
+    sizes = [total // parts + (k < total % parts) for k in range(parts)]
+    bounds = [half + 1 - sum(sizes[:k]) for k in range(parts + 1)]
+    spans = [(bounds[k + 1], bounds[k]) for k in range(parts)]
     links = [
         ((t ^ 1) * n_space + s, t * n_space + s + 1) if t % 2 == 0 else ((t ^ 1) * n_space + s + 1, t * n_space + s)
         for t in range(n)
         for s in range(n_space - 1)
     ]
-    halo = lax.ppermute(border, ("tm", "space"), links)
-    arrived1 = exchange(n, 0, tab, pair1, decay, phase)
-    own2, oth2, pair2, weights = drive(frame, oth, weights, tab, factor, -1, cut, step, halo=halo, w_out=w_out)
-    arrived2 = exchange(n, 4, tab, pair2, decay, phase)
-    result, pay1, kept = output(
-        tab, weights, (own1, oth1), arrived1, frame, oth, cut, half + 1, cut + 1, half, 0, step, True
-    )
-    got1 = lax.ppermute(pay1, "tm", swap)
-    result, pay2 = output(
-        tab, weights, (own2, oth2), arrived2, frame, oth, -1, cut, 0, cut + 1, 4, step, False, kept=kept, result=result
-    )
-    got2 = lax.ppermute(pay2, "tm", swap)
-    return place([got1, got2], [(cut + 1, half), (0, cut + 1)], result)[None]
+    feeds, arrived = [], []
+    for k, (lo, hi) in enumerate(spans):
+        if k == 0:
+            mine, frame, weights, tab, factor = lead(roles(n), own, w_in, decay, phase, lo, hi, step)
+            theirs, pair = pair_up(frame, oth, weights, tab, factor, mine, lo, hi, step)
+        elif k == 1:
+            mine, theirs, pair, weights_out, border = drive(
+                frame, oth, weights, tab, factor, lo, hi, step, w_out=w_out
+            )
+            halo = lax.ppermute(border, ("tm", "space"), links)
+        else:
+            mine, theirs, pair = drive(frame, oth, weights, tab, factor, lo, hi, step, halo=halo)
+        feeds.append((mine, theirs))
+        arrived.append(exchange(n, 4 * (k % 2), tab, pair, decay, phase))
+    got, outs, result, kept = [], [], None, None
+    for k, (lo, hi) in enumerate(spans):
+        begin, end = lo + 1, min(hi + 1, half)
+        args = (tab, weights_out, feeds[k], arrived[k], frame, oth, lo, hi, begin, end, 4 * (k % 2), step)
+        if k < parts - 1:
+            result, pay, kept_next = output(*args, True, kept=kept, result=result)
+        else:
+            (pay,) = output(*args, False, which=(0,), kept=kept)
+            (result,) = output(*args, False, which=(1,), kept=kept, result=result)
+        kept = kept_next
+        got.append(lax.ppermute(pay, "tm", swap))
+        outs.append((begin, end))
+    return place(got, outs, result)[None]
 
 
 def solution(mesh):

time: 64.9 us -> 52.8 us (0.81)
  waiting for transfers between devices: 30.1 us -> 17.1 us
  local copies, waits for them, and re-layouts: 4.18 us -> 0.01 us
  starting transfers between devices: 11.5 us -> 14.7 us
  Pallas kernels: 18.6 us -> 20.4 us
    ppermute x2 -> x3, waiting for transfers between devices: 10.2 us -> 5.38 us  [exchange(): r2 = lax.ppermute(relay(slot, tab, pair, r1), 'tm', both_cores(two))]
    ppermute x2 -> x3, waiting for transfers between devices: 14.1 us -> 9.88 us  [exchange(): r1 = lax.ppermute(pair, 'tm', both_cores(one))]
    unnamed x10 -> x2, local copies, waits for them, and re-layouts: 4.18 us -> 0.01 us
    ppermute x1, waiting for transfers between devices: 3.58 us -> 0.41 us  [on_device(): halo = lax.ppermute(border, ('tm', 'space'), links)]
    ppermute x2 -> x3, starting transfers between devices: 3.39 us -> 6.06 us  [exchange(): r2 = lax.ppermute(relay(slot, tab, pair, r1), 'tm', both_cores(two))]
    ppermute x2 -> x3, waiting for transfers between devices: 2.21 us -> 0.01 us  [on_device(): got.append(lax.ppermute(pay, 'tm', swap))]
    pallas_call x2 -> x4, Pallas kernels: 8.34 us -> 9.96 us  [output(): pl.pallas_call(functools.partial(output_kernel, lo, hi, begin, end, slot,...]
    ppermute x1, waiting for transfers between devices: 0.01 us -> 1.4 us  [on_device(): oth = lax.ppermute(own, 'tm', swap)]
  transfers between devices with their start and end apart: 8 -> 11, of which waited for: 5 -> 7; matrix products, arithmetic and copies ran while one was open for 0% -> 0% of each run, Pallas kernels for 17% -> 32%
where the time goes in v3:
time: 52.8 us; the launch traced here: 52.5 us
  Pallas kernels  20.4 us (39%)
  waiting for transfers between devices  17.1 us (32%)
  starting transfers between devices  14.7 us (28%)
    pallas_call x4, Pallas kernels, output(): pl.pallas_call(functools.partial(output_kernel, lo, hi, begin, end, slot,...  9.96 us
    ppermute x3, waiting for transfers between devices, exchange(): r1 = lax.ppermute(pair, 'tm', both_cores(one))  9.88 us
    ppermute x3, starting transfers between devices, exchange(): r2 = lax.ppermute(relay(slot, tab, pair, r1), 'tm', both_cores(two))  6.06 us
    ppermute x3, waiting for transfers between devices, exchange(): r2 = lax.ppermute(relay(slot, tab, pair, r1), 'tm', both_cores(two))  5.38 us
    pallas_call x2, Pallas kernels, drive(): pl.pallas_call(functools.partial(drive_kernel, lo, hi, step, edge, second...  4.76 us
    ppermute x3, starting transfers between devices, exchange(): r1 = lax.ppermute(pair, 'tm', both_cores(one))  3.88 us
    ppermute x1, starting transfers between devices, on_device(): halo = lax.ppermute(border, ('tm', 'space'), links)  3.47 us
    pallas_call x1, Pallas kernels, lead(): pl.pallas_call(functools.partial(lead_kernel, entries, lo, hi, step), out...  2.59 us
  transfers between devices with their start and end apart: 11, of which 7 were waited for; matrix products, arithmetic and copies ran while one was open for 0% of the time, Pallas kernels for 32%

profile of v3, /device:TPU:15, one launch (start us, length us, event | category | flops | bytes accessed | tf_op | source)
XLA Modules:
  0.0 52.5 jit_solution(1533309847813171742)
XLA Ops:
  0.0 0.7 %collective-permute-start = (bf16[32,128,256]{2,1,0:T(8,128)(2,1)}, bf16[32,128,256]{2,1,0:T(8,128)(2,1)S(1)}, u32[]{:S(2)}, u32[]{:S(2)}) collective-permute-start(bf16[32,128,256]{2,1,0:T(8,128)(2,1)} %bitcast.7), channel_id=1, source_target_pairs={{0,4},{4,0},{8,12},{12,8},{16,20},{20,16},{24,28},{28,24},{1,5},{5... | collective-permute-start | bytes 6291464 | tf_op jit(solution)/shard_map/ppermute | solution.py:444
  0.7 2.6 %lead.1 = (f32[6,128,256]{2,1,0:T(8,128)S(1)}, bf16[32,128,256]{2,1,0:T(8,128)(2,1)S(1)}, bf16[3,768,256]{2,1,0:T(8,128)(2,1)S(1)}, f32[32,128]{1,0:T(8,128)S(1)}, f32[1,256]{1,0:T(1,128)S(1)}) custom-call(bf16[32,128,256]{2,1,0:T(8,128)(2,1)} %bitcast.8, bf16[3,768,256]{2,1,0:T(8,128)(2,1)} %bitcast.9, f32[1,128]{1,0:T(1,128)} %bitcast.10, f32[1,128]{1,0:T(1,128)} %bitcast.11), custom_call_target="tpu_custom_call" | custom-call | flops 905969664 | bytes 2097152 | tf_op jit(solution)/shard_map/lead/pallas_call | solution.py:121
  3.3 1.4 %collective-permute-done.refs_1_.oth.refs_7_ = bf16[32,128,256]{2,1,0:T(8,128)(2,1)S(1)} collective-permute-done((bf16[32,128,256]{2,1,0:T(8,128)(2,1)}, bf16[32,128,256]{2,1,0:T(8,128)(2,1)S(1)}, u32[]{:S(2)}, u32[]{:S(2)}) %collective-permute-start) | collective-permute-done | bytes 2097184 | tf_op jit(solution)/shard_map/ppermute | solution.py:444
  4.7 2.7 %drive.2 = (f32[6,128,256]{2,1,0:T(8,128)S(1)}, f32[6,128,256]{2,1,0:T(8,128)S(1)}, bf16[6,128,256]{2,1,0:T(8,128)(2,1)S(1)}, bf16[3,768,256]{2,1,0:T(8,128)(2,1)S(1)}, bf16[2,2,128,256]{3,2,1,0:T(8,128)(2,1)S(1)}) custom-call(bf16[32,128,256]{2,1,0:T(8,128)(2,1)S(1)} %get-tuple-element.27.refs_0_.frame.refs_6_, ...), custom_call_target="tpu_custom_call" | custom-call | flops 1811939328 | bytes 3932160 | tf_op jit(solution)/shard_map/drive/pallas_call | solution.py:243
  7.4 3.5 %collective-permute-start.7 = (bf16[2,2,128,256]{3,2,1,0:T(8,128)(2,1)S(1)}, bf16[2,2,128,256]{3,2,1,0:T(8,128)(2,1)S(1)}, u32[]{:S(2)}, u32[]{:S(2)}) collective-permute-start(bf16[2,2,128,256]{3,2,1,0:T(8,128)(2,1)S(1)} %get-tuple-element.41), channel_id=1, source_target_pairs={{4,1},{5,2},{6,3},{1,4},{2,5},{3,6},{12,9},{13,10},{14,11},{9,12},... | collective-permute-start | bytes 786440 | tf_op jit(solution)/shard_map/ppermute | solution.py:465
  10.8 1.2 %pair.1 = (f32[6,128,256]{2,1,0:T(8,128)S(1)}, bf16[6,128,256]{2,1,0:T(8,128)(2,1)S(1)}) custom-call(bf16[32,128,256]{2,1,0:T(8,128)(2,1)S(1)} %get-tuple-element.27.refs_0_.frame.refs_6_, bf16[32,128,256]{2,1,0:T(8,128)(2,1)S(1)} %collective-permute-done.refs_1_.oth.refs_7_, bf16[3,768,256]{2,1,0:T(8,128)(2,1)S(1)} %get-tuple-element.28.refs_2_.weights, ...), custom_call_target="tpu_custom_call" | custom-call | flops 905969664 | bytes 2097152 | tf_op jit(solution)/shard_map/pair/pallas_call | solution.py:165
  12.0 1.3 %collective-permute-start.1 = (bf16[6,128,256]{2,1,0:T(8,128)(2,1)S(1)}, bf16[6,128,256]{2,1,0:T(8,128)(2,1)S(1)}, u32[]{:S(2)}, u32[]{:S(2)}) collective-permute-start(bf16[6,128,256]{2,1,0:T(8,128)(2,1)S(1)} %get-tuple-element.33.pair), channel_id=1, source_target_pairs={{0,8},{4,12},{8,0},{12,4},{16,24},{20,28},{1,9},{5,13},{9,1},{13,5... | collective-permute-start | bytes 1179656 | tf_op jit(solution)/shard_map/ppermute | solution.py:422
  13.3 1.3 %collective-permute-start.4 = (bf16[6,128,256]{2,1,0:T(8,128)(2,1)S(1)}, bf16[6,128,256]{2,1,0:T(8,128)(2,1)S(1)}, u32[]{:S(2)}, u32[]{:S(2)}) collective-permute-start(bf16[6,128,256]{2,1,0:T(8,128)(2,1)S(1)} %get-tuple-element.37.pair), channel_id=1, source_target_pairs={{0,16},{4,20},{8,24},{12,28},{1,17},{5,21},{9,25},{13,29},{2,18},{... | collective-permute-start | bytes 1179656 | tf_op jit(solution)/shard_map/ppermute | solution.py:422
  15.1 2.1 %drive.3 = (f32[6,128,256]{2,1,0:T(8,128)S(1)}, f32[6,128,256]{2,1,0:T(8,128)S(1)}, bf16[6,128,256]{2,1,0:T(8,128)(2,1)S(1)}) custom-call(bf16[32,128,256]{2,1,0:T(8,128)(2,1)S(1)} %get-tuple-element.27.refs_0_.frame.refs_6_, bf16[32,128,256]{2,1,0:T(8,128)(2,1)S(1)} %collective-permute-done.refs_1_.oth.refs_7_, ...), custom_call_target="tpu_custom_call" | custom-call | flops 1811939328 | bytes 3932160 | tf_op jit(solution)/shard_map/drive/pallas_call | solution.py:243
  17.1 1.3 %collective-permute-start.8 = (bf16[6,128,256]{2,1,0:T(8,128)(2,1)S(1)}, bf16[6,128,256]{2,1,0:T(8,128)(2,1)S(1)}, u32[]{:S(2)}, u32[]{:S(2)}) collective-permute-start(bf16[6,128,256]{2,1,0:T(8,128)(2,1)S(1)} %get-tuple-element.44.pair), channel_id=1, source_target_pairs={{0,8},{4,12},{8,0},{12,4},{16,24},{20,28},{1,9},{5,13},{9,1},{13,5... | collective-permute-start | bytes 1179656 | tf_op jit(solution)/shard_map/ppermute | solution.py:422
  18.4 6.6 %collective-permute-done.1.got.refs_4_ = bf16[6,128,256]{2,1,0:T(8,128)(2,1)S(1)} collective-permute-done((bf16[6,128,256]{2,1,0:T(8,128)(2,1)S(1)}, bf16[6,128,256]{2,1,0:T(8,128)(2,1)S(1)}, u32[]{:S(2)}, u32[]{:S(2)}) %collective-permute-start.1) | collective-permute-done | bytes 393248 | tf_op jit(solution)/shard_map/ppermute | solution.py:422
  25.3 1.3 %collective-permute-start.2 = (bf16[6,128,256]{2,1,0:T(8,128)(2,1)S(1)}, bf16[6,128,256]{2,1,0:T(8,128)(2,1)S(1)}, u32[]{:S(2)}, u32[]{:S(2)}) collective-permute-start(bf16[6,128,256]{2,1,0:T(8,128)(2,1)S(1)} %relay.3), channel_id=1, source_target_pairs={{0,16},{4,20},{8,24},{12,28},{1,17},{5,21},{9,25},{13,29},{2,18},{... | collective-permute-start | bytes 1179656 | tf_op jit(solution)/shard_map/ppermute | solution.py:423
  26.8 3.3 %collective-permute-start.5 = (bf16[6,128,256]{2,1,0:T(8,128)(2,1)S(1)}, bf16[6,128,256]{2,1,0:T(8,128)(2,1)S(1)}, u32[]{:S(2)}, u32[]{:S(2)}) collective-permute-start(bf16[6,128,256]{2,1,0:T(8,128)(2,1)S(1)} %relay.4), channel_id=1, source_target_pairs={{0,8},{4,12},{16,24},{20,28},{24,16},{28,20},{1,9},{5,13},{17,25},... | collective-permute-start | bytes 1179656 | tf_op jit(solution)/shard_map/ppermute | solution.py:423
  30.1 3.3 %collective-permute-done.8.got.refs_4_ = bf16[6,128,256]{2,1,0:T(8,128)(2,1)S(1)} collective-permute-done((bf16[6,128,256]{2,1,0:T(8,128)(2,1)S(1)}, bf16[6,128,256]{2,1,0:T(8,128)(2,1)S(1)}, u32[]{:S(2)}, u32[]{:S(2)}) %collective-permute-start.8) | collective-permute-done | bytes 393248 | tf_op jit(solution)/shard_map/ppermute | solution.py:422
  33.7 1.5 %collective-permute-start.9 = (bf16[6,128,256]{2,1,0:T(8,128)(2,1)S(1)}, bf16[6,128,256]{2,1,0:T(8,128)(2,1)S(1)}, u32[]{:S(2)}, u32[]{:S(2)}) collective-permute-start(bf16[6,128,256]{2,1,0:T(8,128)(2,1)S(1)} %relay.5), channel_id=1, source_target_pairs={{0,16},{4,20},{8,24},{12,28},{1,17},{5,21},{9,25},{13,29},{2,18},{... | collective-permute-start | bytes 1179656 | tf_op jit(solution)/shard_map/ppermute | solution.py:423
  35.2 3.0 %collective-permute-done.2.refs_5_ = bf16[6,128,256]{2,1,0:T(8,128)(2,1)S(1)} collective-permute-done((bf16[6,128,256]{2,1,0:T(8,128)(2,1)S(1)}, bf16[6,128,256]{2,1,0:T(8,128)(2,1)S(1)}, u32[]{:S(2)}, u32[]{:S(2)}) %collective-permute-start.2) | collective-permute-done | bytes 393248 | tf_op jit(solution)/shard_map/ppermute | solution.py:423
  38.2 2.5 %output.4 = (bf16[32,128,256]{2,1,0:T(8,128)(2,1)}, bf16[4,128,256]{2,1,0:T(8,128)(2,1)S(1)}, bf16[2,2,128,256]{3,2,1,0:T(8,128)(2,1)S(1)}) custom-call(f32[32,128]{1,0:T(8,128)S(1)} %get-tuple-element.26.refs_3_.tab.refs_0_, bf16[3,768,256]{2,1,0:T(8,128)(2,1)S(1)} %get-tuple-element.30.refs_1_, f32[6,128,256]{2,1,0:T(8,128)S(1)} %get-tuple-element.31.feed_own.refs_2_, ...), custom_call_target="tpu_custom_call" | custom-call | flops 1207959552 | bytes 3932160 | tf_op jit(solution)/shard_map/output/pallas_call | solution.py:361
  40.7 0.6 %collective-permute-done.5.refs_5_ = bf16[6,128,256]{2,1,0:T(8,128)(2,1)S(1)} collective-permute-done((bf16[6,128,256]{2,1,0:T(8,128)(2,1)S(1)}, bf16[6,128,256]{2,1,0:T(8,128)(2,1)S(1)}, u32[]{:S(2)}, u32[]{:S(2)}) %collective-permute-start.5) | collective-permute-done | bytes 393248 | tf_op jit(solution)/shard_map/ppermute | solution.py:423
  41.4 3.3 %output.5 = (bf16[32,128,256]{2,1,0:T(8,128)(2,1)}, bf16[6,128,256]{2,1,0:T(8,128)(2,1)S(1)}, bf16[2,2,128,256]{3,2,1,0:T(8,128)(2,1)S(1)}) custom-call(f32[32,128]{1,0:T(8,128)S(1)} %get-tuple-element.26.refs_3_.tab.refs_0_, bf16[3,768,256]{2,1,0:T(8,128)(2,1)S(1)} %get-tuple-element.30.refs_1_, ...), custom_call_target="tpu_custom_call", output_to_operand_aliasing={{0}: (9, {})} | custom-call | flops 1811939328 | bytes 3932160 | tf_op jit(solution)/shard_map/output/pallas_call | solution.py:361
  44.8 1.7 %collective-permute-done.9.refs_5_ = bf16[6,128,256]{2,1,0:T(8,128)(2,1)S(1)} collective-permute-done((bf16[6,128,256]{2,1,0:T(8,128)(2,1)S(1)}, bf16[6,128,256]{2,1,0:T(8,128)(2,1)S(1)}, u32[]{:S(2)}, u32[]{:S(2)}) %collective-permute-start.9) | collective-permute-done | bytes 393248 | tf_op jit(solution)/shard_map/ppermute | solution.py:423
  46.5 1.7 %output.6 = bf16[6,128,256]{2,1,0:T(8,128)(2,1)S(1)} custom-call(f32[32,128]{1,0:T(8,128)S(1)} %get-tuple-element.26.refs_3_.tab.refs_0_, bf16[3,768,256]{2,1,0:T(8,128)(2,1)S(1)} %get-tuple-element.30.refs_1_, f32[6,128,256]{2,1,0:T(8,128)S(1)} %get-tuple-element.42.refs_2_, f32[6,128,256]{2,1,0:T(8,128)S(1)} %get-tuple-element.43.refs_3_, ...), custom_call_target="tpu_custom_call" | custom-call | flops 905969664 | bytes 3932160 | tf_op jit(solution)/shard_map/output/pallas_call | solution.py:361
  48.2 0.5 collective-permute-start.10
  48.8 2.4 %output.7.refs_3_ = bf16[32,128,256]{2,1,0:T(8,128)(2,1)} custom-call(f32[32,128]{1,0:T(8,128)S(1)} %get-tuple-element.26.refs_3_.tab.refs_0_, bf16[3,768,256]{2,1,0:T(8,128)(2,1)S(1)} %get-tuple-element.30.refs_1_, f32[6,128,256]{2,1,0:T(8,128)S(1)} %get-tuple-element.42.refs_2_, ...), custom_call_target="tpu_custom_call", output_to_operand_aliasing={{}: (9, {})} | custom-call | flops 905969664 | bytes 3932160 | tf_op jit(solution)/shard_map/output/pallas_call | solution.py:361
  51.2 1.1 %place.1 = bf16[32,128,256]{2,1,0:T(8,128)(2,1)} custom-call(bf16[4,128,256]{2,1,0:T(8,128)(2,1)S(1)} %collective-permute-done.3.refs_0_, bf16[6,128,256]{2,1,0:T(8,128)(2,1)S(1)} %collective-permute-done.6.refs_1_, bf16[6,128,256]{2,1,0:T(8,128)(2,1)S(1)} %collective-permute-done.10.refs_2_, ...), custom_call_target="tpu_custom_call", output_to_operand_aliasing={{}: (3, {})} | custom-call | tf_op jit(solution)/shard_map/place/pallas_call | solution.py:391
  (12 shorter events, 1.3 us)
Async XLA Ops:
  0.0 4.7 %copy-start = (bf16[3,3,256,256]{3,2,1,0:T(8,128)(2,1)S(1)}, bf16[3,3,256,256]{3,2,1,0:T(8,128)(2,1)}, u32[]{:S(2)}) copy-start(bf16[3,3,256,256]{3,2,1,0:T(8,128)(2,1)} %param.9) | copy-start | bytes 3538948
  0.0 4.7 %collective-permute-start = (bf16[32,128,256]{2,1,0:T(8,128)(2,1)}, bf16[32,128,256]{2,1,0:T(8,128)(2,1)S(1)}, u32[]{:S(2)}, u32[]{:S(2)}) collective-permute-start(bf16[32,128,256]{2,1,0:T(8,128)(2,1)} %bitcast.7), channel_id=1, source_target_pairs={{0,4},{4,0},{8,12},{12,8},{16,20},{20,16},{24,28},{28,24},{1,5},{5... | collective-permute-start | bytes 6291464 | tf_op jit(solution)/shard_map/ppermute | solution.py:444
  7.4 7.7 %collective-permute-start.7 = (bf16[2,2,128,256]{3,2,1,0:T(8,128)(2,1)S(1)}, bf16[2,2,128,256]{3,2,1,0:T(8,128)(2,1)S(1)}, u32[]{:S(2)}, u32[]{:S(2)}) collective-permute-start(bf16[2,2,128,256]{3,2,1,0:T(8,128)(2,1)S(1)} %get-tuple-element.41), channel_id=1, source_target_pairs={{4,1},{5,2},{6,3},{1,4},{2,5},{3,6},{12,9},{13,10},{14,11},{9,12},... | collective-permute-start | bytes 786440 | tf_op jit(solution)/shard_map/ppermute | solution.py:465
  12.0 13.0 %collective-permute-start.1 = (bf16[6,128,256]{2,1,0:T(8,128)(2,1)S(1)}, bf16[6,128,256]{2,1,0:T(8,128)(2,1)S(1)}, u32[]{:S(2)}, u32[]{:S(2)}) collective-permute-start(bf16[6,128,256]{2,1,0:T(8,128)(2,1)S(1)} %get-tuple-element.33.pair), channel_id=1, source_target_pairs={{0,8},{4,12},{8,0},{12,4},{16,24},{20,28},{1,9},{5,13},{9,1},{13,5... | collective-permute-start | bytes 1179656 | tf_op jit(solution)/shard_map/ppermute | solution.py:422
  13.3 13.2 %collective-permute-start.4 = (bf16[6,128,256]{2,1,0:T(8,128)(2,1)S(1)}, bf16[6,128,256]{2,1,0:T(8,128)(2,1)S(1)}, u32[]{:S(2)}, u32[]{:S(2)}) collective-permute-start(bf16[6,128,256]{2,1,0:T(8,128)(2,1)S(1)} %get-tuple-element.37.pair), channel_id=1, source_target_pairs={{0,16},{4,20},{8,24},{12,28},{1,17},{5,21},{9,25},{13,29},{2,18},{... | collective-permute-start | bytes 1179656 | tf_op jit(solution)/shard_map/ppermute | solution.py:422
  17.1 16.3 %collective-permute-start.8 = (bf16[6,128,256]{2,1,0:T(8,128)(2,1)S(1)}, bf16[6,128,256]{2,1,0:T(8,128)(2,1)S(1)}, u32[]{:S(2)}, u32[]{:S(2)}) collective-permute-start(bf16[6,128,256]{2,1,0:T(8,128)(2,1)S(1)} %get-tuple-element.44.pair), channel_id=1, source_target_pairs={{0,8},{4,12},{8,0},{12,4},{16,24},{20,28},{1,9},{5,13},{9,1},{13,5... | collective-permute-start | bytes 1179656 | tf_op jit(solution)/shard_map/ppermute | solution.py:422
  25.3 12.9 %collective-permute-start.2 = (bf16[6,128,256]{2,1,0:T(8,128)(2,1)S(1)}, bf16[6,128,256]{2,1,0:T(8,128)(2,1)S(1)}, u32[]{:S(2)}, u32[]{:S(2)}) collective-permute-start(bf16[6,128,256]{2,1,0:T(8,128)(2,1)S(1)} %relay.3), channel_id=1, source_target_pairs={{0,16},{4,20},{8,24},{12,28},{1,17},{5,21},{9,25},{13,29},{2,18},{... | collective-permute-start | bytes 1179656 | tf_op jit(solution)/shard_map/ppermute | solution.py:423
  26.8 14.6 %collective-permute-start.5 = (bf16[6,128,256]{2,1,0:T(8,128)(2,1)S(1)}, bf16[6,128,256]{2,1,0:T(8,128)(2,1)S(1)}, u32[]{:S(2)}, u32[]{:S(2)}) collective-permute-start(bf16[6,128,256]{2,1,0:T(8,128)(2,1)S(1)} %relay.4), channel_id=1, source_target_pairs={{0,8},{4,12},{16,24},{20,28},{24,16},{28,20},{1,9},{5,13},{17,25},... | collective-permute-start | bytes 1179656 | tf_op jit(solution)/shard_map/ppermute | solution.py:423
  33.7 12.8 %collective-permute-start.9 = (bf16[6,128,256]{2,1,0:T(8,128)(2,1)S(1)}, bf16[6,128,256]{2,1,0:T(8,128)(2,1)S(1)}, u32[]{:S(2)}, u32[]{:S(2)}) collective-permute-start(bf16[6,128,256]{2,1,0:T(8,128)(2,1)S(1)} %relay.5), channel_id=1, source_target_pairs={{0,16},{4,20},{8,24},{12,28},{1,17},{5,21},{9,25},{13,29},{2,18},{... | collective-permute-start | bytes 1179656 | tf_op jit(solution)/shard_map/ppermute | solution.py:423
  44.7 6.5 %collective-permute-start.6 = (bf16[6,128,256]{2,1,0:T(8,128)(2,1)S(1)}, bf16[6,128,256]{2,1,0:T(8,128)(2,1)S(1)}, u32[]{:S(2)}, u32[]{:S(2)}) collective-permute-start(bf16[6,128,256]{2,1,0:T(8,128)(2,1)S(1)} %get-tuple-element.40), channel_id=1, source_target_pairs={{0,4},{4,0},{8,12},{12,8},{16,20},{20,16},{24,28},{28,24},{1,5},{5... | collective-permute-start | bytes 1179656 | tf_op jit(solution)/shard_map/ppermute | solution.py:480
  48.2 3.0 %collective-permute-start.10 = (bf16[6,128,256]{2,1,0:T(8,128)(2,1)S(1)}, bf16[6,128,256]{2,1,0:T(8,128)(2,1)S(1)}, u32[]{:S(2)}, u32[]{:S(2)}) collective-permute-start(bf16[6,128,256]{2,1,0:T(8,128)(2,1)S(1)} %output.6), channel_id=1, source_target_pairs={{0,4},{4,0},{8,12},{12,8},{16,20},{20,16},{24,28},{28,24},{1,5},{5... | collective-permute-start | bytes 1179656 | tf_op jit(solution)/shard_map/ppermute | solution.py:480
  48.7 2.5 %collective-permute-start.3 = (bf16[4,128,256]{2,1,0:T(8,128)(2,1)S(1)}, bf16[4,128,256]{2,1,0:T(8,128)(2,1)S(1)}, u32[]{:S(2)}, u32[]{:S(2)}) collective-permute-start(bf16[4,128,256]{2,1,0:T(8,128)(2,1)S(1)} %get-tuple-element.34), channel_id=1, source_target_pairs={{0,4},{4,0},{8,12},{12,8},{16,20},{20,16},{24,28},{28,24},{1,5},{5... | collective-permute-start | bytes 786440 | tf_op jit(solution)/shard_map/ppermute | solution.py:480

commit v4 on v2

v4 whole, which is shorter than its diff:
```python
import functools

import numpy as np
import jax
import jax.numpy as jnp
from jax import lax
from jax.experimental import pallas as pl
from jax.experimental.pallas import tpu as pltpu
from jax.sharding import PartitionSpec as P

F32 = jnp.float32
BF16 = jnp.bfloat16
VMEM = pl.BlockSpec(memory_space=pltpu.VMEM)
HBM = pl.BlockSpec(memory_space=pltpu.HBM)
PARAMS = pltpu.CompilerParams(vmem_limit_bytes=24 * 1024 * 1024)
SLOTS = 16


def cmul(coef, z):
    n = z.shape[-1] // 2
    re, im = z[..., :n], z[..., n:]
    cr, ci = coef
    return jnp.concatenate([cr * re - ci * im, cr * im + ci * re], axis=-1)


def coefficient(tab, i):
    return tab[i : i + 1, :], tab[SLOTS + i : SLOTS + i + 1, :]


def widen(row):
    w = row.shape[0]
    col = lax.broadcasted_iota(jnp.int32, row.shape, 0)
    left = jnp.where(col == 0, 0.0, pltpu.roll(row, 1, 0))
    right = jnp.where(col == w - 1, 0.0, pltpu.roll(row, w - 1, 0))
    return jnp.concatenate([left, row, right], axis=-1).astype(BF16)


def conv_block(wide, weights, start, count, order=(0, 1, 2)):
    w, k = wide.shape[1], wide.shape[2]
    lhs = jnp.concatenate(
        [wide[start + d : start + d + count].reshape(count * w, k) for d in range(3)], axis=-1
    )
    rhs = jnp.concatenate([weights[d] for d in order], axis=0)
    return jnp.dot(lhs, rhs, preferred_element_type=F32)


def load_weights(core, hbm, vmem, sem):
    copies = []
    for d in range(3):
        source = jnp.where(core == 1, 2 - d, d)
        copies.append(pltpu.make_async_copy(hbm.at[source], vmem.at[d], sem.at[d]))
        copies[-1].start()
    return copies


def my_core():
    return lax.rem(lax.axis_index("tm"), 2)


def convolve(weights, wide, row_of, n, step, finish):
    ready = 0
    for s in range(0, n, step):
        size = min(step, n - s)
        while ready < s + size + 2:
            wide[ready] = widen(row_of(ready))
            ready += 1
        finish(s, size, conv_block(wide, weights, s, size))


def lead_kernel(
    entries, lo, mid, hi, step, own, w_hbm, decay, phase, feed, feed_next, frame, weights, tab, factor, wide, dvec, sem
):
    core, chip = my_core(), lax.div(lax.axis_index("tm"), 2)
    rows = own.shape[0]
    n = hi - lo
    vectors = [pltpu.make_async_copy(ref, dvec.at[pl.ds(k, 1)], sem.at[3 + k]) for k, ref in enumerate((decay, phase))]
    for copy in vectors:
        copy.start()
    source = jnp.where(core == 1, rows - 1 - hi, lo - 1)
    near = pltpu.make_async_copy(own.at[pl.ds(source, n + 2)], frame.at[pl.ds(source, n + 2)], sem.at[5])
    near.start()
    wcopies = load_weights(core, w_hbm, weights, sem)
    for copy in vectors:
        copy.wait()
    expo, gate = [jnp.float32(0.0)] * SLOTS, [jnp.float32(0.0)] * SLOTS
    for q, slot, power in entries:
        expo[slot] = jnp.where(chip == q, jnp.float32(power), expo[slot])
        gate[slot] = jnp.where(chip == q, jnp.float32(1.0), gate[slot])
    for slot, power in ((8, 1), (9, 1 - core), (10, core)):
        expo[slot], gate[slot] = jnp.asarray(power).astype(F32), jnp.float32(1.0)
    spread = lambda values: jnp.concatenate([jnp.full((1, dvec.shape[1]), v, F32) for v in values], axis=0)
    expo = spread(expo)
    size = spread(gate) * jnp.exp(-expo * dvec[0:1])
    angle = expo * dvec[1:2]
    tab[...] = jnp.concatenate([size * jnp.cos(angle), size * jnp.sin(angle)], axis=0)
    mag = jnp.exp(-dvec[0:1])
    scale = jnp.sqrt(1.0 - mag * mag)
    factor[...] = jnp.concatenate([scale, scale], axis=-1)
    for copy in (*wcopies, near):
        copy.wait()
    rest = []
    for k, (begin, end) in enumerate(((0, lo - 1), (hi + 1, rows))):
        at = jnp.where(core == 1, rows - end, begin)
        rest.append(
            pltpu.make_async_copy(own.at[pl.ds(at, end - begin)], frame.at[pl.ds(at, end - begin)], sem.at[6 + k])
        )
        rest[-1].start()

    def row_of(p):
        return frame[source + jnp.where(core == 1, n + 1 - p, p)].astype(F32)

    def finish(s, count, acc):
        value = (acc * factor[...]).reshape((count,) + feed.shape[1:])
        for r in range(count):
            depth = lo + s + r
            if depth < mid:
                feed_next[depth - lo] = value[r]
            else:
                feed[depth - mid] = value[r]

    convolve(weights, wide, row_of, n, step, finish)
    for copy in rest:
        copy.wait()


def lead(entries, own, w_in, decay, phase, lo, mid, hi, step):
    rows, w, c = own.shape
    n = hi - lo
    return pl.pallas_call(
        functools.partial(lead_kernel, entries, lo, mid, hi, step),
        out_shape=[
            jax.ShapeDtypeStruct((hi - mid, w, c), F32),
            jax.ShapeDtypeStruct((mid - lo, w, c), F32),
            jax.ShapeDtypeStruct(own.shape, BF16),
            jax.ShapeDtypeStruct(w_in.shape, BF16),
            jax.ShapeDtypeStruct((2 * SLOTS, decay.shape[1]), F32),
            jax.ShapeDtypeStruct((1, 2 * decay.shape[1]), F32),
        ],
        in_specs=[HBM] * 4,
        out_specs=[VMEM] * 6,
        scratch_shapes=[
            pltpu.VMEM((n + 2, w, 3 * c), BF16),
            pltpu.VMEM((2, decay.shape[1]), F32),
            pltpu.SemaphoreType.DMA((8,)),
        ],
        compiler_params=PARAMS,
        cost_estimate=pl.CostEstimate(flops=18 * n * w * c * c, bytes_accessed=2 * own.size, transcendentals=0),
        name="lead",
    )(*(pltpu.with_memory_space_constraint(x, pltpu.HBM) for x in (own, w_in, decay, phase)))


def pair_kernel(lo, hi, step, frame, oth, weights, tab, factor, feed_own, feed, pay, factor_next, *refs):
    *border, wide = refs
    core = my_core()
    rows = oth.shape[0]
    n = hi - lo
    factor_next[...] = factor[...]
    for out in border:
        for f, ref in enumerate((frame, oth)):
            for r in range(2):
                out[f, r] = ref[core * (rows - 2) + r]
    source = jnp.where(core == 1, rows - 1 - hi, lo - 1)

    def row_of(p):
        return oth[source + jnp.where(core == 1, n + 1 - p, p)].astype(F32)

    def finish(s, count, acc):
        value = (acc * factor[...]).reshape((count,) + feed.shape[1:])
        feed[s : s + count] = value
        for r in range(count):
            pair = cmul(coefficient(tab, 9), feed_own[s + r]) + cmul(coefficient(tab, 10), value[r])
            pay[s + r] = pair.astype(BF16)

    convolve(weights, wide, row_of, n, step, finish)


def pair_up(frame, oth, weights, tab, factor, feed_own, lo, hi, step, border):
    rows, w, c = oth.shape
    n = hi - lo
    return pl.pallas_call(
        functools.partial(pair_kernel, lo, hi, step),
        out_shape=[
            jax.ShapeDtypeStruct((n, w, c), F32),
            jax.ShapeDtypeStruct((n, w, c), BF16),
            jax.ShapeDtypeStruct(factor.shape, F32),
        ]
        + [jax.ShapeDtypeStruct((2, 2, w, c), BF16)] * border,
        in_specs=[VMEM] * 6,
        out_specs=[VMEM] * (3 + border),
        scratch_shapes=[pltpu.VMEM((n + 2, w, 3 * c), BF16)],
        compiler_params=PARAMS,
        cost_estimate=pl.CostEstimate(flops=18 * n * w * c * c, bytes_accessed=2 * oth.size, transcendentals=0),
        name="pair",
    )(frame, oth, weights, tab, factor, feed_own)


def edge_kernel(
    lo, hi, step, frame, oth, weights, tab, factor, halo, feed_own, feed_oth, pay, tab_next, wide
):
    core = my_core()
    rows = frame.shape[0]
    n = hi - lo
    tab_next[...] = tab[...]
    outer = jnp.where(core == 1, lax.axis_size("space") - 1, 0)
    inside = jnp.where(lax.axis_index("space") == outer, 0.0, 1.0)
    for f, (ref, feed) in enumerate(((frame, feed_own), (oth, feed_oth))):

        def row_of(p):
            depth = lo - 1 + p
            if depth < 0:
                return halo[1 - f, jnp.where(core == 1, -1 - depth, 2 + depth)].astype(F32)
            return ref[jnp.where(core == 1, rows - 1 - depth, depth)].astype(F32)

        def finish(s, count, acc):
            value = (acc * factor[...]).reshape((count,) + feed.shape[1:])
            for r in range(count):
                row = value[r]
                if lo + s + r < 0:
                    row = row * inside
                feed[s + r] = row
                if f == 1:
                    pair = cmul(coefficient(tab, 9), feed_own[s + r]) + cmul(coefficient(tab, 10), row)
                    pay[s + r] = pair.astype(BF16)

        convolve(weights, wide.at[f], row_of, n, step, finish)


def edge_chunk(frame, oth, weights, tab, factor, halo, lo, hi, step):
    rows, w, c = frame.shape
    n = hi - lo
    return pl.pallas_call(
        functools.partial(edge_kernel, lo, hi, step),
        out_shape=[
            jax.ShapeDtypeStruct((n, w, c), F32),
            jax.ShapeDtypeStruct((n, w, c), F32),
            jax.ShapeDtypeStruct((n, w, c), BF16),
            jax.ShapeDtypeStruct(tab.shape, F32),
        ],
        in_specs=[VMEM] * 6,
        out_specs=[VMEM] * 4,
        scratch_shapes=[pltpu.VMEM((2, n + 2, w, 3 * c), BF16)],
        compiler_params=PARAMS,
        cost_estimate=pl.CostEstimate(flops=36 * n * w * c * c, bytes_accessed=20 * n * w * c, transcendentals=0),
        name="edge",
    )(frame, oth, weights, tab, factor, halo)


def relay_kernel(slot, tab, pair, got, pay):
    cp, cr = coefficient(tab, slot), coefficient(tab, slot + 1)
    for r in range(pair.shape[0]):
        pay[r] = (cmul(cp, pair[r].astype(F32)) + cmul(cr, got[r].astype(F32))).astype(BF16)


def relay(slot, tab, pair, got):
    return pl.pallas_call(
        functools.partial(relay_kernel, slot),
        out_shape=jax.ShapeDtypeStruct(pair.shape, BF16),
        in_specs=[VMEM] * 3,
        out_specs=VMEM,
        compiler_params=PARAMS,
        cost_estimate=pl.CostEstimate(flops=16 * pair.size, bytes_accessed=6 * pair.size, transcendentals=0),
        name="relay",
    )(tab, pair, got)


def output_kernel(lo, hi, begin, end, slot, step, which, keep, n_feeds, n_parts, more, *refs):
    refs = list(refs)
    take = lambda k: [refs.pop(0) for _ in range(k)]
    tab, weights, r1, r2, own, oth = take(6)
    feeds = [take(2) for _ in range(n_feeds)]
    kept = take(1)[0] if hi < end + 1 else None
    parts = take(n_parts)
    take(1 if more else 0)
    parcel = take(1)[0] if 0 in which else None
    result = take(1)[0] if 1 in which else None
    kept_out = take(1)[0] if keep else None
    wide, block, sem = refs
    core = my_core()
    first_core = core == 0
    order = [jnp.where(first_core, d, 2 - d) for d in range(3)]
    n, n_out = hi - lo, end - begin
    w, c = own.shape[1:]
    rows = own.shape[0]
    lam = coefficient(tab, 8)
    e1, e2 = coefficient(tab, slot + 2), coefficient(tab, slot + 3)
    feed_rows = [(pair, r) for pair in feeds for r in range(pair[0].shape[0])]
    at = n_out
    for part in parts:
        parcel[at : at + part.shape[0]] = part[...]
        at += part.shape[0]

    def states(r):
        pair, at = feed_rows[r]
        f_own, f_oth = pair[0][at], pair[1][at]
        carry = cmul(e1, r1[r].astype(F32)) + cmul(e2, r2[r].astype(F32))
        s0 = cmul(lam, carry) + jnp.where(first_core, f_own, f_oth)
        s1 = cmul(lam, s0) + jnp.where(first_core, f_oth, f_own)
        return jnp.where(first_core, s1, s0), jnp.where(first_core, s0, s1)

    ready = 0
    copies = []
    for s in range(0, n_out, step):
        size = min(step, n_out - s)
        while ready < s + size + 2:
            if ready < n:
                pair = states(ready)
                if keep and ready < 2:
                    for f in range(2):
                        kept_out[f, ready] = pair[f].astype(BF16)
            else:
                pair = [kept[f, ready - n].astype(F32) for f in range(2)]
            for f in which:
                wide[f, ready] = widen(pair[f])
            ready += 1
        for f in which:
            frame, dst = ((oth, parcel), (own, block))[f]
            mixed = conv_block(wide.at[f], weights, s, size, order).reshape(size, w, c)
            act = 0.5 * mixed * (1.0 + lax.erf(mixed * np.float32(0.5**0.5)))
            for r in range(s, s + size):
                depth = begin + r
                at = jnp.where(core == 1, rows - 1 - depth, depth)
                dst[r] = (frame[at].astype(F32) + act[r - s]).astype(BF16)
                if f == 1:
                    copies.append(pltpu.make_async_copy(block.at[r], result.at[at], sem.at[r]))
                    copies[-1].start()
    for copy in copies:
        copy.wait()


def output(
    tab, weights, feeds, arrived, own, oth, lo, hi, begin, end, slot, step, which, keep, kept=None, parts=(), result=None
):
    rows, w, c = own.shape
    n, n_out = hi - lo, end - begin
    args = [tab, weights, *arrived, own, oth, *(x for pair in feeds for x in pair)]
    args += ([] if kept is None else [kept]) + list(parts)
    specs = [VMEM] * len(args)
    alias = {}
    if result is not None:
        alias[len(args)] = 0
        args, specs = args + [result], specs + [HBM]
    shapes, out_specs = [], []
    if 0 in which:
        n_parcel = n_out + sum(part.shape[0] for part in parts)
        shapes, out_specs = shapes + [jax.ShapeDtypeStruct((n_parcel, w, c), BF16)], out_specs + [VMEM]
    if 1 in which:
        if result is not None:
            alias = {len(args) - 1: len(shapes)}
        shapes, out_specs = shapes + [jax.ShapeDtypeStruct(own.shape, BF16)], out_specs + [HBM]
    if keep:
        shapes, out_specs = shapes + [jax.ShapeDtypeStruct((2, 2, w, c), BF16)], out_specs + [VMEM]
    return pl.pallas_call(
        functools.partial(
            output_kernel, lo, hi, begin, end, slot, step, which, keep, len(feeds), len(parts), result is not None
        ),
        out_shape=shapes,
        in_specs=specs,
        out_specs=out_specs,
        input_output_aliases=alias,
        scratch_shapes=[
            pltpu.VMEM((2, n_out + 2, w, 3 * c), BF16),
            pltpu.VMEM((n_out, w, c), BF16),
            pltpu.SemaphoreType.DMA((n_out,)),
        ],
        compiler_params=PARAMS,
        cost_estimate=pl.CostEstimate(
            flops=18 * len(which) * n_out * w * c * c, bytes_accessed=20 * n * w * c, transcendentals=0
        ),
        name="output",
    )(*args)


def place_kernel(parcel, _, result, sem):
    core = my_core()
    rows = result.shape[0]
    copies = []
    for depth in range(parcel.shape[0]):
        at = jnp.where(core == 1, depth, rows - 1 - depth)
        copies.append(pltpu.make_async_copy(parcel.at[depth], result.at[at], sem.at[depth]))
        copies[-1].start()
    for copy in copies:
        copy.wait()


def place(parcel, result):
    return pl.pallas_call(
        place_kernel,
        out_shape=jax.ShapeDtypeStruct(result.shape, result.dtype),
        in_specs=[VMEM, HBM],
        out_specs=HBM,
        input_output_aliases={1: 0},
        scratch_shapes=[pltpu.SemaphoreType.DMA((parcel.shape[0],))],
        compiler_params=PARAMS,
        name="place",
    )(parcel, result)


ALONG_X = [(0, 1), (1, 0), (2, 3)], [(0, 2), (1, 3)]
ALONG_Y = [(0, 2), (1, 3)], [(0, 1), (2, 3), (3, 2)]


def roles(n):
    if n != 8:
        return [(q, slot, 0) for q in range(n // 2) for slot in (2, 6)]
    along_x = [(0, 0, 2), (0, 1, 0), (1, 0, 0), (1, 1, 2), (1, 2, 0), (2, 3, 0), (3, 2, 0), (3, 3, 2)]
    along_y = [(0, 4, 0), (2, 4, 0), (2, 5, 4), (3, 5, 0), (1, 7, 0), (2, 6, 2), (2, 7, 0), (3, 6, 2), (3, 7, 0)]
    return along_x + along_y


def both_cores(pairs):
    return [(2 * a + k, 2 * b + k) for a, b in pairs for k in range(2)]


def exchange(n, slot, tab, pair, decay, phase):
    if n == 8:
        one, two = ALONG_X if slot == 0 else ALONG_Y
        r1 = lax.ppermute(pair, "tm", both_cores(one))
        r2 = lax.ppermute(relay(slot, tab, pair, r1), "tm", both_cores(two))
        return r1, r2
    chips, stride, total = n // 2, 1, pair.astype(F32)
    while stride < chips:
        steps = both_cores([(i, i + stride) for i in range(chips - stride)])
        moved = lax.ppermute(total.astype(BF16), "tm", steps).astype(F32)
        size, angle = jnp.exp(-2.0 * stride * decay), 2.0 * stride * phase
        total = total + cmul((size * jnp.cos(angle), size * jnp.sin(angle)), moved)
        stride *= 2
    carry = lax.ppermute(total.astype(BF16), "tm", both_cores([(i, i + 1) for i in range(chips - 1)]))
    return carry, jnp.zeros_like(carry)


def on_device(n, n_space, frames_in, w_input, decay_rate, phase, w_output):
    own = frames_in[0]
    rows, w, c = own.shape
    decay, phase = decay_rate[None], phase[None]
    w_in = w_input.reshape(3, 3 * c, -1)
    w_out = w_output.reshape(3, -1, c)
    swap = [(i, i ^ 1) for i in range(n)]
    step = 3
    oth = lax.ppermute(own, "tm", swap)

    half = rows // 2
    last = max(2, (half + 2) * 6 // 18)
    middle = (half + 2 - last) // 2
    spans = [(last - 1 + middle, half + 1), (last - 1, last - 1 + middle), (-1, last - 1)]
    links = [
        ((t ^ 1) * n_space + s, t * n_space + s + 1) if t % 2 == 0 else ((t ^ 1) * n_space + s + 1, t * n_space + s)
        for t in range(n)
        for s in range(n_space - 1)
    ]
    (lo1, hi1), (lo2, hi2), (lo3, hi3) = spans
    mine1, mine2, frame, weights, tab, factor = lead(roles(n), own, w_in, decay, phase, lo2, lo1, hi1, step)
    theirs1, pair1, factor, border = pair_up(frame, oth, weights, tab, factor, mine1, lo1, hi1, step, True)
    halo = lax.ppermute(border, ("tm", "space"), links)
    theirs2, pair2, factor = pair_up(frame, oth, weights, tab, factor, mine2, lo2, hi2, step, False)
    mine3, theirs3, pair3, tab = edge_chunk(frame, oth, weights, tab, factor, halo, lo3, hi3, step)
    arrived1 = exchange(n, 0, tab, pair1, decay, phase)
    arrived2 = exchange(n, 4, tab, pair2, decay, phase)
    arrived3 = exchange(n, 0, tab, pair3, decay, phase)
    parcel1, result, kept = output(
        tab, w_out, [(mine1, theirs1)], arrived1, frame, oth, lo1, hi1, lo1 + 1, half, 0, step, (0, 1), True
    )
    parcel2, result, kept = output(
        tab, w_out, [(mine2, theirs2)], arrived2, frame, oth, lo2, hi2, lo2 + 1, hi2 + 1, 4, step, (0, 1), True,
        kept=kept, result=result,
    )
    rest = (tab, w_out, [(mine3, theirs3)], arrived3, frame, oth, lo3, hi3, lo3 + 1, hi3 + 1, 0, step)
    (parcel,) = output(*rest, (0,), False, kept=kept, parts=(parcel2, parcel1))
    (result,) = output(*rest, (1,), False, kept=kept, result=result)
    return place(lax.ppermute(parcel, "tm", swap), result)[None]


def solution(mesh):
    in_specs = (P("tm", "space", None, None), P(), P(), P(), P())
    out_specs = P("tm", "space", None, None)
    body = functools.partial(on_device, mesh.shape["tm"], mesh.shape["space"])
    return jax.shard_map(body, mesh=mesh, in_specs=in_specs, out_specs=out_specs, check_vma=False)
```

time: 64.9 us -> 50.1 us (0.77)
  waiting for transfers between devices: 30.1 us -> 13.6 us
  starting transfers between devices: 11.5 us -> 16 us
  local copies, waits for them, and re-layouts: 4.18 us -> 0.01 us
  Pallas kernels: 18.6 us -> 19.9 us
    ppermute x2 -> x3, waiting for transfers between devices: 14.1 us -> 6.52 us  [exchange(): r1 = lax.ppermute(pair, 'tm', both_cores(one))]
    unnamed x10 -> x2, local copies, waits for them, and re-layouts: 4.18 us -> 0.01 us
    ppermute x2 -> x3, waiting for transfers between devices: 10.2 us -> 6.05 us  [exchange(): r2 = lax.ppermute(relay(slot, tab, pair, r1), 'tm', both_cores(two))]
    ppermute x2 -> x3, starting transfers between devices: 3.39 us -> 7.29 us  [exchange(): r2 = lax.ppermute(relay(slot, tab, pair, r1), 'tm', both_cores(two))]
    ppermute x1, waiting for transfers between devices: 3.58 us -> 0.71 us  [on_device(): halo = lax.ppermute(border, ('tm', 'space'), links)]
    ppermute x2 -> x1, waiting for transfers between devices: 2.21 us -> 0.01 us  [on_device(): return place(lax.ppermute(parcel, 'tm', swap), result)[None]]
    pallas_call x2 -> x4, Pallas kernels: 8.34 us -> 9.9 us  [output(): pl.pallas_call(functools.partial(output_kernel, lo, hi, begin, end, slot,...]
    ppermute x2 -> x3, starting transfers between devices: 2.58 us -> 4.01 us  [exchange(): r1 = lax.ppermute(pair, 'tm', both_cores(one))]
  transfers between devices with their start and end apart: 8 -> 9, of which waited for: 5 -> 8; matrix products, arithmetic and copies ran while one was open for 0% -> 0% of each run, Pallas kernels for 17% -> 32%
where the time goes in v4:
time: 50.1 us; the launch traced here: 49.8 us
  Pallas kernels  19.9 us (40%)
  starting transfers between devices  16 us (32%)
  waiting for transfers between devices  13.6 us (27%)
    pallas_call x4, Pallas kernels, output(): pl.pallas_call(functools.partial(output_kernel, lo, hi, begin, end, slot,...  9.9 us
    ppermute x3, starting transfers between devices, exchange(): r2 = lax.ppermute(relay(slot, tab, pair, r1), 'tm', both_cores(two))  7.29 us
    ppermute x3, waiting for transfers between devices, exchange(): r1 = lax.ppermute(pair, 'tm', both_cores(one))  6.52 us
    ppermute x3, waiting for transfers between devices, exchange(): r2 = lax.ppermute(relay(slot, tab, pair, r1), 'tm', both_cores(two))  6.05 us
    ppermute x3, starting transfers between devices, exchange(): r1 = lax.ppermute(pair, 'tm', both_cores(one))  4.01 us
    pallas_call x1, Pallas kernels, lead(): pl.pallas_call(functools.partial(lead_kernel, entries, lo, mid, hi, step)...  3.64 us
    ppermute x1, starting transfers between devices, on_device(): halo = lax.ppermute(border, ('tm', 'space'), links)  3.46 us
    pallas_call x2, Pallas kernels, pair_up(): pl.pallas_call(functools.partial(pair_kernel, lo, hi, step), out_shape=[j...  2.4 us
  transfers between devices with their start and end apart: 9, of which 8 were waited for; matrix products, arithmetic and copies ran while one was open for 0% of the time, Pallas kernels for 32%

profile of v4, /device:TPU:15, one launch (start us, length us, event | category | flops | bytes accessed | tf_op | source)
XLA Modules:
  0.0 49.8 jit_solution(3127060445286740995)
XLA Ops:
  0.0 0.7 %collective-permute-start = (bf16[32,128,256]{2,1,0:T(8,128)(2,1)}, bf16[32,128,256]{2,1,0:T(8,128)(2,1)S(1)}, u32[]{:S(2)}, u32[]{:S(2)}) collective-permute-start(bf16[32,128,256]{2,1,0:T(8,128)(2,1)} %bitcast.10), channel_id=1, source_target_pairs={{0,4},{4,0},{8,12},{12,8},{16,20},{20,16},{24,28},{28,24},{1,5},{5... | collective-permute-start | bytes 6291464 | tf_op jit(solution)/shard_map/ppermute | solution.py:439
  0.7 3.6 %lead.1 = (f32[6,128,256]{2,1,0:T(8,128)S(1)}, f32[6,128,256]{2,1,0:T(8,128)S(1)}, bf16[32,128,256]{2,1,0:T(8,128)(2,1)S(1)}, bf16[3,768,256]{2,1,0:T(8,128)(2,1...) custom-call(bf16[32,128,256]{2,1,0:T(8,128)(2,1)} %bitcast.11, bf16[3,768,256]{2,1,0:T(8,128)(2,1)} %bitcast.12, ...), custom_call_target="tpu_custom_call" | custom-call | flops 1811939328 | bytes 2097152 | tf_op jit(solution)/shard_map/lead/pallas_call | solution.py:129
  4.7 1.2 %pair.2 = (f32[6,128,256]{2,1,0:T(8,128)S(1)}, bf16[6,128,256]{2,1,0:T(8,128)(2,1)S(1)}, f32[1,256]{1,0:T(1,128)S(1)}, bf16[2,2,128,256]{3,2,1,0:T(8,128)(2,1)S(1)}) custom-call(bf16[32,128,256]{2,1,0:T(8,128)(2,1)S(1)} %get-tuple-element.28.frame.refs_4_, bf16[32,128,256]{2,1,0:T(8,128)(2,1)S(1)} %collective-permute-done.oth.refs_5_, ...), custom_call_target="tpu_custom_call" | custom-call | flops 905969664 | bytes 2097152 | tf_op jit(solution)/shard_map/pair/pallas_call | solution.py:180
  5.9 3.5 %collective-permute-start.1 = (bf16[2,2,128,256]{3,2,1,0:T(8,128)(2,1)S(1)}, bf16[2,2,128,256]{3,2,1,0:T(8,128)(2,1)S(1)}, u32[]{:S(2)}, u32[]{:S(2)}) collective-permute-start(bf16[2,2,128,256]{3,2,1,0:T(8,128)(2,1)S(1)} %get-tuple-element.36), channel_id=1, source_target_pairs={{4,1},{5,2},{6,3},{1,4},{2,5},{3,6},{12,9},{13,10},{14,11},{9,12},... | collective-permute-start | bytes 786440 | tf_op jit(solution)/shard_map/ppermute | solution.py:453
  9.4 1.3 %collective-permute-start.6 = (bf16[6,128,256]{2,1,0:T(8,128)(2,1)S(1)}, bf16[6,128,256]{2,1,0:T(8,128)(2,1)S(1)}, u32[]{:S(2)}, u32[]{:S(2)}) collective-permute-start(bf16[6,128,256]{2,1,0:T(8,128)(2,1)S(1)} %get-tuple-element.43.pair), channel_id=1, source_target_pairs={{0,8},{4,12},{8,0},{12,4},{16,24},{20,28},{1,9},{5,13},{9,1},{13,5... | collective-permute-start | bytes 1179656 | tf_op jit(solution)/shard_map/ppermute | solution.py:417
  10.7 1.2 %pair.3 = (f32[6,128,256]{2,1,0:T(8,128)S(1)}, bf16[6,128,256]{2,1,0:T(8,128)(2,1)S(1)}, f32[1,256]{1,0:T(1,128)S(1)}) custom-call(bf16[32,128,256]{2,1,0:T(8,128)(2,1)S(1)} %get-tuple-element.28.frame.refs_4_, bf16[32,128,256]{2,1,0:T(8,128)(2,1)S(1)} %collective-permute-done.oth.refs_5_, bf16[3,768,256]{2,1,0:T(8,128)(2,1)S(1)} %get-tuple-element.29.weights, ...), custom_call_target="tpu_custom_call" | custom-call | flops 905969664 | bytes 2097152 | tf_op jit(solution)/shard_map/pair/pallas_call | solution.py:180
  11.9 1.3 %collective-permute-start.4 = (bf16[6,128,256]{2,1,0:T(8,128)(2,1)S(1)}, bf16[6,128,256]{2,1,0:T(8,128)(2,1)S(1)}, u32[]{:S(2)}, u32[]{:S(2)}) collective-permute-start(bf16[6,128,256]{2,1,0:T(8,128)(2,1)S(1)} %get-tuple-element.41.pair), channel_id=1, source_target_pairs={{0,16},{4,20},{8,24},{12,28},{1,17},{5,21},{9,25},{13,29},{2,18},{... | collective-permute-start | bytes 1179656 | tf_op jit(solution)/shard_map/ppermute | solution.py:417
  13.2 0.7 %collective-permute-done.1.halo = bf16[2,2,128,256]{3,2,1,0:T(8,128)(2,1)S(1)} collective-permute-done((bf16[2,2,128,256]{3,2,1,0:T(8,128)(2,1)S(1)}, bf16[2,2,128,256]{3,2,1,0:T(8,128)(2,1)S(1)}, u32[]{:S(2)}, u32[]{:S(2)}) %collective-permute-start.1) | collective-permute-done | bytes 262176 | tf_op jit(solution)/shard_map/ppermute | solution.py:453
  13.9 2.1 %edge.1 = (f32[6,128,256]{2,1,0:T(8,128)S(1)}, f32[6,128,256]{2,1,0:T(8,128)S(1)}, bf16[6,128,256]{2,1,0:T(8,128)(2,1)S(1)}, f32[32,128]{1,0:T(8,128)S(1)}) custom-call(bf16[32,128,256]{2,1,0:T(8,128)(2,1)S(1)} %get-tuple-element.28.frame.refs_4_, bf16[32,128,256]{2,1,0:T(8,128)(2,1)S(1)} %collective-permute-done.oth.refs_5_, ...), custom_call_target="tpu_custom_call" | custom-call | flops 1811939328 | bytes 3932160 | tf_op jit(solution)/shard_map/edge/pallas_call | solution.py:231
  16.0 1.4 %collective-permute-start.2 = (bf16[6,128,256]{2,1,0:T(8,128)(2,1)S(1)}, bf16[6,128,256]{2,1,0:T(8,128)(2,1)S(1)}, u32[]{:S(2)}, u32[]{:S(2)}) collective-permute-start(bf16[6,128,256]{2,1,0:T(8,128)(2,1)S(1)} %get-tuple-element.38.pair), channel_id=1, source_target_pairs={{0,8},{4,12},{8,0},{12,4},{16,24},{20,28},{1,9},{5,13},{9,1},{13,5... | collective-permute-start | bytes 1179656 | tf_op jit(solution)/shard_map/ppermute | solution.py:417
  17.4 4.9 %collective-permute-done.6.got.refs_2_ = bf16[6,128,256]{2,1,0:T(8,128)(2,1)S(1)} collective-permute-done((bf16[6,128,256]{2,1,0:T(8,128)(2,1)S(1)}, bf16[6,128,256]{2,1,0:T(8,128)(2,1)S(1)}, u32[]{:S(2)}, u32[]{:S(2)}) %collective-permute-start.6) | collective-permute-done | bytes 393248 | tf_op jit(solution)/shard_map/ppermute | solution.py:417
  22.6 1.3 %collective-permute-start.7 = (bf16[6,128,256]{2,1,0:T(8,128)(2,1)S(1)}, bf16[6,128,256]{2,1,0:T(8,128)(2,1)S(1)}, u32[]{:S(2)}, u32[]{:S(2)}) collective-permute-start(bf16[6,128,256]{2,1,0:T(8,128)(2,1)S(1)} %relay.5), channel_id=1, source_target_pairs={{0,16},{4,20},{8,24},{12,28},{1,17},{5,21},{9,25},{13,29},{2,18},{... | collective-permute-start | bytes 1179656 | tf_op jit(solution)/shard_map/ppermute | solution.py:418
  24.6 4.5 %collective-permute-start.5 = (bf16[6,128,256]{2,1,0:T(8,128)(2,1)S(1)}, bf16[6,128,256]{2,1,0:T(8,128)(2,1)S(1)}, u32[]{:S(2)}, u32[]{:S(2)}) collective-permute-start(bf16[6,128,256]{2,1,0:T(8,128)(2,1)S(1)} %relay.4), channel_id=1, source_target_pairs={{0,8},{4,12},{16,24},{20,28},{24,16},{28,20},{1,9},{5,13},{17,25},... | collective-permute-start | bytes 1179656 | tf_op jit(solution)/shard_map/ppermute | solution.py:418
  29.2 1.1 %collective-permute-done.2.got.refs_2_ = bf16[6,128,256]{2,1,0:T(8,128)(2,1)S(1)} collective-permute-done((bf16[6,128,256]{2,1,0:T(8,128)(2,1)S(1)}, bf16[6,128,256]{2,1,0:T(8,128)(2,1)S(1)}, u32[]{:S(2)}, u32[]{:S(2)}) %collective-permute-start.2) | collective-permute-done | bytes 393248 | tf_op jit(solution)/shard_map/ppermute | solution.py:417
  30.5 1.5 %collective-permute-start.3 = (bf16[6,128,256]{2,1,0:T(8,128)(2,1)S(1)}, bf16[6,128,256]{2,1,0:T(8,128)(2,1)S(1)}, u32[]{:S(2)}, u32[]{:S(2)}) collective-permute-start(bf16[6,128,256]{2,1,0:T(8,128)(2,1)S(1)} %relay.3), channel_id=1, source_target_pairs={{0,16},{4,20},{8,24},{12,28},{1,17},{5,21},{9,25},{13,29},{2,18},{... | collective-permute-start | bytes 1179656 | tf_op jit(solution)/shard_map/ppermute | solution.py:418
  32.0 3.5 %collective-permute-done.7.refs_3_ = bf16[6,128,256]{2,1,0:T(8,128)(2,1)S(1)} collective-permute-done((bf16[6,128,256]{2,1,0:T(8,128)(2,1)S(1)}, bf16[6,128,256]{2,1,0:T(8,128)(2,1)S(1)}, u32[]{:S(2)}, u32[]{:S(2)}) %collective-permute-start.7) | collective-permute-done | bytes 393248 | tf_op jit(solution)/shard_map/ppermute | solution.py:418
  35.5 2.5 %output.4 = (bf16[4,128,256]{2,1,0:T(8,128)(2,1)S(1)}, bf16[32,128,256]{2,1,0:T(8,128)(2,1)}, bf16[2,2,128,256]{3,2,1,0:T(8,128)(2,1)S(1)}) custom-call(f32[32,128]{1,0:T(8,128)S(1)} %get-tuple-element.37.tab.refs_0_, bf16[3,768,256]{2,1,0:T(8,128)(2,1)S(1)} %bitcast.6, bf16[6,128,256]{2,1,0:T(8,128)(2,1)S(1)} %collective-permute-done.6.got.refs_2_, ...), custom_call_target="tpu_custom_call" | custom-call | flops 1207959552 | bytes 3932160 | tf_op jit(solution)/shard_map/output/pallas_call | solution.py:352
  38.0 0.7 %collective-permute-done.5.refs_3_ = bf16[6,128,256]{2,1,0:T(8,128)(2,1)S(1)} collective-permute-done((bf16[6,128,256]{2,1,0:T(8,128)(2,1)S(1)}, bf16[6,128,256]{2,1,0:T(8,128)(2,1)S(1)}, u32[]{:S(2)}, u32[]{:S(2)}) %collective-permute-start.5) | collective-permute-done | bytes 393248 | tf_op jit(solution)/shard_map/ppermute | solution.py:418
  38.7 3.3 %output.5 = (bf16[6,128,256]{2,1,0:T(8,128)(2,1)S(1)}, bf16[32,128,256]{2,1,0:T(8,128)(2,1)}, bf16[2,2,128,256]{3,2,1,0:T(8,128)(2,1)S(1)}) custom-call(f32[32,128]{1,0:T(8,128)S(1)} %get-tuple-element.37.tab.refs_0_, bf16[3,768,256]{2,1,0:T(8,128)(2,1)S(1)} %bitcast.7, ...), custom_call_target="tpu_custom_call", output_to_operand_aliasing={{1}: (9, {})} | custom-call | flops 1811939328 | bytes 3932160 | tf_op jit(solution)/shard_map/output/pallas_call | solution.py:352
  42.0 1.8 %collective-permute-done.3.refs_3_ = bf16[6,128,256]{2,1,0:T(8,128)(2,1)S(1)} collective-permute-done((bf16[6,128,256]{2,1,0:T(8,128)(2,1)S(1)}, bf16[6,128,256]{2,1,0:T(8,128)(2,1)S(1)}, u32[]{:S(2)}, u32[]{:S(2)}) %collective-permute-start.3) | collective-permute-done | bytes 393248 | tf_op jit(solution)/shard_map/ppermute | solution.py:418
  43.9 1.7 %output.6 = bf16[16,128,256]{2,1,0:T(8,128)(2,1)S(1)} custom-call(f32[32,128]{1,0:T(8,128)S(1)} %get-tuple-element.37.tab.refs_0_, bf16[3,768,256]{2,1,0:T(8,128)(2,1)S(1)} %bitcast.8, bf16[6,128,256]{2,1,0:T(8,128)(2,1)S(1)} %collective-permute-done.2.got.refs_2_, bf16[6,128,256]{2,1,0:T(8,128)(2,1)S(1)} %collective-permute-done.3.refs_3_, ...), custom_call_target="tpu_custom_call" | custom-call | flops 905969664 | bytes 3932160 | tf_op jit(solution)/shard_map/output/pallas_call | solution.py:352
  45.6 0.5 %collective-permute-start.8 = (bf16[16,128,256]{2,1,0:T(8,128)(2,1)S(1)}, bf16[16,128,256]{2,1,0:T(8,128)(2,1)S(1)}, u32[]{:S(2)}, u32[]{:S(2)}) collective-permute-start(bf16[16,128,256]{2,1,0:T(8,128)(2,1)S(1)} %output.6), channel_id=1, source_target_pairs={{0,4},{4,0},{8,12},{12,8},{16,20},{20,16},{24,28},{28,24},{1,5},{5... | collective-permute-start | bytes 3145736 | tf_op jit(solution)/shard_map/ppermute | solution.py:469
  46.1 2.4 %output.7._ = bf16[32,128,256]{2,1,0:T(8,128)(2,1)} custom-call(f32[32,128]{1,0:T(8,128)S(1)} %get-tuple-element.37.tab.refs_0_, bf16[3,768,256]{2,1,0:T(8,128)(2,1)S(1)} %bitcast.9, bf16[6,128,256]{2,1,0:T(8,128)(2,1)S(1)} %collective-permute-done.2.got.refs_2_, ...), custom_call_target="tpu_custom_call", output_to_operand_aliasing={{}: (9, {})} | custom-call | flops 905969664 | bytes 3932160 | tf_op jit(solution)/shard_map/output/pallas_call | solution.py:352
  48.5 1.1 %place.1 = bf16[32,128,256]{2,1,0:T(8,128)(2,1)} custom-call(bf16[16,128,256]{2,1,0:T(8,128)(2,1)S(1)} %collective-permute-done.8.parcel, bf16[32,128,256]{2,1,0:T(8,128)(2,1)} %output.7._), custom_call_target="tpu_custom_call", output_to_operand_aliasing={{}: (1, {})} | custom-call | tf_op jit(solution)/shard_map/place/pallas_call | solution.py:386
  (8 shorter events, 1.6 us)
Async XLA Ops:
  0.0 4.7 %collective-permute-start = (bf16[32,128,256]{2,1,0:T(8,128)(2,1)}, bf16[32,128,256]{2,1,0:T(8,128)(2,1)S(1)}, u32[]{:S(2)}, u32[]{:S(2)}) collective-permute-start(bf16[32,128,256]{2,1,0:T(8,128)(2,1)} %bitcast.10), channel_id=1, source_target_pairs={{0,4},{4,0},{8,12},{12,8},{16,20},{20,16},{24,28},{28,24},{1,5},{5... | collective-permute-start | bytes 6291464 | tf_op jit(solution)/shard_map/ppermute | solution.py:439
  5.9 8.0 %collective-permute-start.1 = (bf16[2,2,128,256]{3,2,1,0:T(8,128)(2,1)S(1)}, bf16[2,2,128,256]{3,2,1,0:T(8,128)(2,1)S(1)}, u32[]{:S(2)}, u32[]{:S(2)}) collective-permute-start(bf16[2,2,128,256]{3,2,1,0:T(8,128)(2,1)S(1)} %get-tuple-element.36), channel_id=1, source_target_pairs={{4,1},{5,2},{6,3},{1,4},{2,5},{3,6},{12,9},{13,10},{14,11},{9,12},... | collective-permute-start | bytes 786440 | tf_op jit(solution)/shard_map/ppermute | solution.py:453
  9.4 13.0 %collective-permute-start.6 = (bf16[6,128,256]{2,1,0:T(8,128)(2,1)S(1)}, bf16[6,128,256]{2,1,0:T(8,128)(2,1)S(1)}, u32[]{:S(2)}, u32[]{:S(2)}) collective-permute-start(bf16[6,128,256]{2,1,0:T(8,128)(2,1)S(1)} %get-tuple-element.43.pair), channel_id=1, source_target_pairs={{0,8},{4,12},{8,0},{12,4},{16,24},{20,28},{1,9},{5,13},{9,1},{13,5... | collective-permute-start | bytes 1179656 | tf_op jit(solution)/shard_map/ppermute | solution.py:417
  11.9 12.5 %collective-permute-start.4 = (bf16[6,128,256]{2,1,0:T(8,128)(2,1)S(1)}, bf16[6,128,256]{2,1,0:T(8,128)(2,1)S(1)}, u32[]{:S(2)}, u32[]{:S(2)}) collective-permute-start(bf16[6,128,256]{2,1,0:T(8,128)(2,1)S(1)} %get-tuple-element.41.pair), channel_id=1, source_target_pairs={{0,16},{4,20},{8,24},{12,28},{1,17},{5,21},{9,25},{13,29},{2,18},{... | collective-permute-start | bytes 1179656 | tf_op jit(solution)/shard_map/ppermute | solution.py:417
  16.0 19.5 %copy-start = (bf16[3,3,256,256]{3,2,1,0:T(8,128)(2,1)S(1)}, bf16[3,3,256,256]{3,2,1,0:T(8,128)(2,1)}, u32[]{:S(2)}) copy-start(bf16[3,3,256,256]{3,2,1,0:T(8,128)(2,1)} %param.9) | copy-start | bytes 3538948
  16.0 14.3 %collective-permute-start.2 = (bf16[6,128,256]{2,1,0:T(8,128)(2,1)S(1)}, bf16[6,128,256]{2,1,0:T(8,128)(2,1)S(1)}, u32[]{:S(2)}, u32[]{:S(2)}) collective-permute-start(bf16[6,128,256]{2,1,0:T(8,128)(2,1)S(1)} %get-tuple-element.38.pair), channel_id=1, source_target_pairs={{0,8},{4,12},{8,0},{12,4},{16,24},{20,28},{1,9},{5,13},{9,1},{13,5... | collective-permute-start | bytes 1179656 | tf_op jit(solution)/shard_map/ppermute | solution.py:417
  22.6 13.0 %collective-permute-start.7 = (bf16[6,128,256]{2,1,0:T(8,128)(2,1)S(1)}, bf16[6,128,256]{2,1,0:T(8,128)(2,1)S(1)}, u32[]{:S(2)}, u32[]{:S(2)}) collective-permute-start(bf16[6,128,256]{2,1,0:T(8,128)(2,1)S(1)} %relay.5), channel_id=1, source_target_pairs={{0,16},{4,20},{8,24},{12,28},{1,17},{5,21},{9,25},{13,29},{2,18},{... | collective-permute-start | bytes 1179656 | tf_op jit(solution)/shard_map/ppermute | solution.py:418
  24.6 14.1 %collective-permute-start.5 = (bf16[6,128,256]{2,1,0:T(8,128)(2,1)S(1)}, bf16[6,128,256]{2,1,0:T(8,128)(2,1)S(1)}, u32[]{:S(2)}, u32[]{:S(2)}) collective-permute-start(bf16[6,128,256]{2,1,0:T(8,128)(2,1)S(1)} %relay.4), channel_id=1, source_target_pairs={{0,8},{4,12},{16,24},{20,28},{24,16},{28,20},{1,9},{5,13},{17,25},... | collective-permute-start | bytes 1179656 | tf_op jit(solution)/shard_map/ppermute | solution.py:418
  30.5 13.4 %collective-permute-start.3 = (bf16[6,128,256]{2,1,0:T(8,128)(2,1)S(1)}, bf16[6,128,256]{2,1,0:T(8,128)(2,1)S(1)}, u32[]{:S(2)}, u32[]{:S(2)}) collective-permute-start(bf16[6,128,256]{2,1,0:T(8,128)(2,1)S(1)} %relay.3), channel_id=1, source_target_pairs={{0,16},{4,20},{8,24},{12,28},{1,17},{5,21},{9,25},{13,29},{2,18},{... | collective-permute-start | bytes 1179656 | tf_op jit(solution)/shard_map/ppermute | solution.py:418
  45.6 2.9 %collective-permute-start.8 = (bf16[16,128,256]{2,1,0:T(8,128)(2,1)S(1)}, bf16[16,128,256]{2,1,0:T(8,128)(2,1)S(1)}, u32[]{:S(2)}, u32[]{:S(2)}) collective-permute-start(bf16[16,128,256]{2,1,0:T(8,128)(2,1)S(1)} %output.6), channel_id=1, source_target_pairs={{0,4},{4,0},{8,12},{12,8},{16,20},{20,16},{24,28},{28,24},{1,5},{5... | collective-permute-start | bytes 3145736 | tf_op jit(solution)/shard_map/ppermute | solution.py:469

commit v5 on v4

--- a/solution.py
+++ b/solution.py
@@ -13,6 +13,8 @@
 VMEM = pl.BlockSpec(memory_space=pltpu.VMEM)
 HBM = pl.BlockSpec(memory_space=pltpu.HBM)
 PARAMS = pltpu.CompilerParams(vmem_limit_bytes=24 * 1024 * 1024)
+SHORT = pl.CostEstimate(flops=1, bytes_accessed=1, transcendentals=0)
+LONG = pl.CostEstimate(flops=1, bytes_accessed=1, transcendentals=0)
 SLOTS = 16
 
 
@@ -144,21 +146,16 @@
             pltpu.SemaphoreType.DMA((8,)),
         ],
         compiler_params=PARAMS,
-        cost_estimate=pl.CostEstimate(flops=18 * n * w * c * c, bytes_accessed=2 * own.size, transcendentals=0),
+        cost_estimate=SHORT,
         name="lead",
     )(*(pltpu.with_memory_space_constraint(x, pltpu.HBM) for x in (own, w_in, decay, phase)))
 
 
-def pair_kernel(lo, hi, step, frame, oth, weights, tab, factor, feed_own, feed, pay, factor_next, *refs):
-    *border, wide = refs
+def pair_kernel(lo, hi, step, oth, weights, tab, factor, feed_own, feed, pay, tab_next, wide):
     core = my_core()
     rows = oth.shape[0]
     n = hi - lo
-    factor_next[...] = factor[...]
-    for out in border:
-        for f, ref in enumerate((frame, oth)):
-            for r in range(2):
-                out[f, r] = ref[core * (rows - 2) + r]
+    tab_next[...] = tab[...]
     source = jnp.where(core == 1, rows - 1 - hi, lo - 1)
 
     def row_of(p):
@@ -174,7 +171,7 @@
     convolve(weights, wide, row_of, n, step, finish)
 
 
-def pair_up(frame, oth, weights, tab, factor, feed_own, lo, hi, step, border):
+def pair_up(oth, weights, tab, factor, feed_own, lo, hi, step):
     rows, w, c = oth.shape
     n = hi - lo
     return pl.pallas_call(
@@ -182,16 +179,38 @@
         out_shape=[
             jax.ShapeDtypeStruct((n, w, c), F32),
             jax.ShapeDtypeStruct((n, w, c), BF16),
-            jax.ShapeDtypeStruct(factor.shape, F32),
-        ]
-        + [jax.ShapeDtypeStruct((2, 2, w, c), BF16)] * border,
-        in_specs=[VMEM] * 6,
-        out_specs=[VMEM] * (3 + border),
+            jax.ShapeDtypeStruct(tab.shape, F32),
+        ],
+        in_specs=[VMEM] * 5,
+        out_specs=[VMEM] * 3,
         scratch_shapes=[pltpu.VMEM((n + 2, w, 3 * c), BF16)],
         compiler_params=PARAMS,
-        cost_estimate=pl.CostEstimate(flops=18 * n * w * c * c, bytes_accessed=2 * oth.size, transcendentals=0),
+        cost_estimate=SHORT,
         name="pair",
-    )(frame, oth, weights, tab, factor, feed_own)
+    )(oth, weights, tab, factor, feed_own)
+
+
+def border_kernel(frame, oth, tab, border, tab_next):
+    tab_next[...] = tab[...]
+    at = my_core() * (frame.shape[0] - 2)
+    for f, ref in enumerate((frame, oth)):
+        for r in range(2):
+            border[f, r] = ref[at + r]
+
+
+def outer_rows(frame, oth, tab):
+    return pl.pallas_call(
+        border_kernel,
+        out_shape=[
+            jax.ShapeDtypeStruct((2, 2) + frame.shape[1:], BF16),
+            jax.ShapeDtypeStruct(tab.shape, F32),
+        ],
+        in_specs=[VMEM] * 3,
+        out_specs=[VMEM] * 2,
+        compiler_params=PARAMS,
+        cost_estimate=SHORT,
+        name="border",
+    )(frame, oth, tab)
 
 
 def edge_kernel(
@@ -240,12 +259,13 @@
         out_specs=[VMEM] * 4,
         scratch_shapes=[pltpu.VMEM((2, n + 2, w, 3 * c), BF16)],
         compiler_params=PARAMS,
-        cost_estimate=pl.CostEstimate(flops=36 * n * w * c * c, bytes_accessed=20 * n * w * c, transcendentals=0),
+        cost_estimate=SHORT,
         name="edge",
     )(frame, oth, weights, tab, factor, halo)
 
 
-def relay_kernel(slot, tab, pair, got, pay):
+def relay_kernel(slot, tab, pair, got, pay, tab_next):
+    tab_next[...] = tab[...]
     cp, cr = coefficient(tab, slot), coefficient(tab, slot + 1)
     for r in range(pair.shape[0]):
         pay[r] = (cmul(cp, pair[r].astype(F32)) + cmul(cr, got[r].astype(F32))).astype(BF16)
@@ -254,145 +274,179 @@
 def relay(slot, tab, pair, got):
     return pl.pallas_call(
         functools.partial(relay_kernel, slot),
-        out_shape=jax.ShapeDtypeStruct(pair.shape, BF16),
+        out_shape=[jax.ShapeDtypeStruct(pair.shape, BF16), jax.ShapeDtypeStruct(tab.shape, F32)],
         in_specs=[VMEM] * 3,
-        out_specs=VMEM,
-        compiler_params=PARAMS,
-        cost_estimate=pl.CostEstimate(flops=16 * pair.size, bytes_accessed=6 * pair.size, transcendentals=0),
+        out_specs=[VMEM] * 2,
+        compiler_params=PARAMS,
+        cost_estimate=SHORT,
         name="relay",
     )(tab, pair, got)
 
 
-def output_kernel(lo, hi, begin, end, slot, step, which, keep, n_feeds, n_parts, more, *refs):
+def output_kernel(lo, hi, begin, end, slot, step, which, seam, closing, n_parts, blocks_at, more, *refs):
     refs = list(refs)
     take = lambda k: [refs.pop(0) for _ in range(k)]
-    tab, weights, r1, r2, own, oth = take(6)
-    feeds = [take(2) for _ in range(n_feeds)]
-    kept = take(1)[0] if hi < end + 1 else None
+    tab, weights, r1, r2, own, oth, feed_own, feed_oth = take(8)
+    kept = take(1)[0] if not seam else None
+    near, far = take(2) if closing else (None, None)
     parts = take(n_parts)
+    blocks = take(len(blocks_at))
     take(1 if more else 0)
     parcel = take(1)[0] if 0 in which else None
-    result = take(1)[0] if 1 in which else None
-    kept_out = take(1)[0] if keep else None
-    wide, block, sem = refs
+    block = take(1)[0] if 1 in which else None
+    result = take(1)[0] if blocks_at else None
+    kept_out = take(1)[0] if not closing else None
+    near_out, send = take(2) if seam else (None, None)
+    tab_next = take(1)[0] if 0 in which else None
+    wide = take(1)[0]
     core = my_core()
     first_core = core == 0
     order = [jnp.where(first_core, d, 2 - d) for d in range(3)]
     n, n_out = hi - lo, end - begin
     w, c = own.shape[1:]
     rows = own.shape[0]
+    copies = []
+    for ref, depth in zip(blocks, blocks_at):
+        copies += start_rows(ref, result, core, depth, refs[0], len(copies))
+    if tab_next is not None:
+        tab_next[...] = tab[...]
     lam = coefficient(tab, 8)
     e1, e2 = coefficient(tab, slot + 2), coefficient(tab, slot + 3)
-    feed_rows = [(pair, r) for pair in feeds for r in range(pair[0].shape[0])]
     at = n_out
     for part in parts:
         parcel[at : at + part.shape[0]] = part[...]
         at += part.shape[0]
 
     def states(r):
-        pair, at = feed_rows[r]
-        f_own, f_oth = pair[0][at], pair[1][at]
+        f_own, f_oth = feed_own[r], feed_oth[r]
         carry = cmul(e1, r1[r].astype(F32)) + cmul(e2, r2[r].astype(F32))
         s0 = cmul(lam, carry) + jnp.where(first_core, f_own, f_oth)
         s1 = cmul(lam, s0) + jnp.where(first_core, f_oth, f_own)
         return jnp.where(first_core, s1, s0), jnp.where(first_core, s0, s1)
 
+    def emit(f, first_wide, size, depth, place):
+        frame, dst = ((oth, parcel), (own, block))[f]
+        mixed = conv_block(wide.at[f], weights, first_wide, size, order).reshape(size, w, c)
+        act = 0.5 * mixed * (1.0 + lax.erf(mixed * np.float32(0.5**0.5)))
+        for r in range(size):
+            row = jnp.where(core == 1, rows - 1 - depth - r, depth + r)
+            dst[place + r] = (frame[row].astype(F32) + act[r]).astype(BF16)
+
+    if closing:
+        top = n_out + 2
+        for f in which:
+            for k, z in enumerate((near[f, 0], near[f, 1], far[1 - f])):
+                wide[f, top + k] = widen(z.astype(F32))
+            emit(f, top, 1, rows // 2 - 1, (parcel if f == 0 else block).shape[0] - 1)
     ready = 0
-    copies = []
     for s in range(0, n_out, step):
         size = min(step, n_out - s)
         while ready < s + size + 2:
             if ready < n:
                 pair = states(ready)
-                if keep and ready < 2:
-                    for f in range(2):
+                for f in range(2):
+                    if not closing and ready < 2:
                         kept_out[f, ready] = pair[f].astype(BF16)
+                    if seam and ready >= n - 2:
+                        near_out[f, ready - (n - 2)] = pair[f].astype(BF16)
+                    if seam and ready == n - 1:
+                        send[f] = pair[f].astype(BF16)
             else:
                 pair = [kept[f, ready - n].astype(F32) for f in range(2)]
             for f in which:
                 wide[f, ready] = widen(pair[f])
             ready += 1
         for f in which:
-            frame, dst = ((oth, parcel), (own, block))[f]
-            mixed = conv_block(wide.at[f], weights, s, size, order).reshape(size, w, c)
-            act = 0.5 * mixed * (1.0 + lax.erf(mixed * np.float32(0.5**0.5)))
-            for r in range(s, s + size):
-                depth = begin + r
-                at = jnp.where(core == 1, rows - 1 - depth, depth)
-                dst[r] = (frame[at].astype(F32) + act[r - s]).astype(BF16)
-                if f == 1:
-                    copies.append(pltpu.make_async_copy(block.at[r], result.at[at], sem.at[r]))
-                    copies[-1].start()
+            emit(f, s, size, begin + s, s)
     for copy in copies:
         copy.wait()
 
 
+def start_rows(block, result, side, depth, sem, at=0):
+    copies = []
+    for r in range(block.shape[0]):
+        row = jnp.where(side == 1, result.shape[0] - 1 - depth - r, depth + r)
+        copies.append(pltpu.make_async_copy(block.at[r], result.at[row], sem.at[at + r]))
+        copies[-1].start()
+    return copies
+
+
 def output(
-    tab, weights, feeds, arrived, own, oth, lo, hi, begin, end, slot, step, which, keep, kept=None, parts=(), result=None
+    tab, weights, feeds, arrived, own, oth, lo, hi, begin, end, slot, step, which, kept=None, seam=None, parts=(),
+    blocks=(), blocks_at=(), result=None,
 ):
     rows, w, c = own.shape
     n, n_out = hi - lo, end - begin
-    args = [tab, weights, *arrived, own, oth, *(x for pair in feeds for x in pair)]
-    args += ([] if kept is None else [kept]) + list(parts)
+    first, closing = kept is None, seam is not None
+    args = [tab, weights, *arrived, own, oth, *feeds]
+    args += ([] if first else [kept]) + (list(seam) if closing else []) + list(parts) + list(blocks)
     specs = [VMEM] * len(args)
     alias = {}
-    if result is not None:
-        alias[len(args)] = 0
-        args, specs = args + [result], specs + [HBM]
     shapes, out_specs = [], []
+    extra = 1 if closing else 0
     if 0 in which:
-        n_parcel = n_out + sum(part.shape[0] for part in parts)
+        n_parcel = n_out + extra + sum(part.shape[0] for part in parts)
         shapes, out_specs = shapes + [jax.ShapeDtypeStruct((n_parcel, w, c), BF16)], out_specs + [VMEM]
     if 1 in which:
+        shapes = shapes + [jax.ShapeDtypeStruct((n_out + extra, w, c), BF16)]
+        out_specs = out_specs + [VMEM]
+    scratch = [pltpu.VMEM((2, n_out + (5 if closing else 2), w, 3 * c), BF16)]
+    if blocks:
+        scratch += [pltpu.SemaphoreType.DMA((sum(ref.shape[0] for ref in blocks),))]
         if result is not None:
-            alias = {len(args) - 1: len(shapes)}
+            alias = {len(args): len(shapes)}
+            args, specs = args + [result], specs + [HBM]
         shapes, out_specs = shapes + [jax.ShapeDtypeStruct(own.shape, BF16)], out_specs + [HBM]
-    if keep:
+    if not closing:
         shapes, out_specs = shapes + [jax.ShapeDtypeStruct((2, 2, w, c), BF16)], out_specs + [VMEM]
+    if first:
+        shapes = shapes + [jax.ShapeDtypeStruct((2, 2, w, c), BF16), jax.ShapeDtypeStruct((2, w, c), BF16)]
+        out_specs = out_specs + [VMEM, VMEM]
+    if 0 in which:
+        shapes, out_specs = shapes + [jax.ShapeDtypeStruct(tab.shape, F32)], out_specs + [VMEM]
     return pl.pallas_call(
         functools.partial(
-            output_kernel, lo, hi, begin, end, slot, step, which, keep, len(feeds), len(parts), result is not None
+            output_kernel, lo, hi, begin, end, slot, step, which, first, closing, len(parts), blocks_at, result is not None
         ),
         out_shape=shapes,
         in_specs=specs,
         out_specs=out_specs,
         input_output_aliases=alias,
-        scratch_shapes=[
-            pltpu.VMEM((2, n_out + 2, w, 3 * c), BF16),
-            pltpu.VMEM((n_out, w, c), BF16),
-            pltpu.SemaphoreType.DMA((n_out,)),
-        ],
-        compiler_params=PARAMS,
-        cost_estimate=pl.CostEstimate(
-            flops=18 * len(which) * n_out * w * c * c, bytes_accessed=20 * n * w * c, transcendentals=0
-        ),
+        scratch_shapes=scratch,
+        compiler_params=PARAMS,
+        cost_estimate=LONG if first else SHORT,
         name="output",
     )(*args)
 
 
-def place_kernel(parcel, _, result, sem):
+def place_kernel(depth, n_two, parcel, block, _, result, sem):
     core = my_core()
-    rows = result.shape[0]
+    inner = result.shape[0] // 2 - 1
+    n = block.shape[0] - 1
+    at = 0
     copies = []
-    for depth in range(parcel.shape[0]):
-        at = jnp.where(core == 1, depth, rows - 1 - depth)
-        copies.append(pltpu.make_async_copy(parcel.at[depth], result.at[at], sem.at[depth]))
-        copies[-1].start()
+    for ref, side, start, count in ((parcel, 1 - core, 0, n + n_two), (block, core, depth, n)):
+        for r in range(count + 1):
+            to = inner if r == count else start + r
+            row = jnp.where(side == 1, result.shape[0] - 1 - to, to)
+            copies.append(pltpu.make_async_copy(ref.at[r], result.at[row], sem.at[at]))
+            copies[-1].start()
+            at += 1
     for copy in copies:
         copy.wait()
 
 
-def place(parcel, result):
-    return pl.pallas_call(
-        place_kernel,
+def place(parcel, block, depth, result):
+    return pl.pallas_call(
+        functools.partial(place_kernel, depth, parcel.shape[0] - block.shape[0]),
         out_shape=jax.ShapeDtypeStruct(result.shape, result.dtype),
-        in_specs=[VMEM, HBM],
+        in_specs=[VMEM, VMEM, HBM],
         out_specs=HBM,
-        input_output_aliases={1: 0},
-        scratch_shapes=[pltpu.SemaphoreType.DMA((parcel.shape[0],))],
+        input_output_aliases={2: 0},
+        scratch_shapes=[pltpu.SemaphoreType.DMA((parcel.shape[0] + block.shape[0],))],
         compiler_params=PARAMS,
         name="place",
-    )(parcel, result)
+    )(parcel, block, result)
 
 
 ALONG_X = [(0, 1), (1, 0), (2, 3)], [(0, 2), (1, 3)]
@@ -411,12 +465,9 @@
     return [(2 * a + k, 2 * b + k) for a, b in pairs for k in range(2)]
 
 
-def exchange(n, slot, tab, pair, decay, phase):
+def first_stage(n, slot, pair, decay, phase):
     if n == 8:
-        one, two = ALONG_X if slot == 0 else ALONG_Y
-        r1 = lax.ppermute(pair, "tm", both_cores(one))
-        r2 = lax.ppermute(relay(slot, tab, pair, r1), "tm", both_cores(two))
-        return r1, r2
+        return lax.ppermute(pair, "tm", both_cores((ALONG_X if slot == 0 else ALONG_Y)[0]))
     chips, stride, total = n // 2, 1, pair.astype(F32)
     while stride < chips:
         steps = both_cores([(i, i + stride) for i in range(chips - stride)])
@@ -424,8 +475,14 @@
         size, angle = jnp.exp(-2.0 * stride * decay), 2.0 * stride * phase
         total = total + cmul((size * jnp.cos(angle), size * jnp.sin(angle)), moved)
         stride *= 2
-    carry = lax.ppermute(total.astype(BF16), "tm", both_cores([(i, i + 1) for i in range(chips - 1)]))
-    return carry, jnp.zeros_like(carry)
+    return lax.ppermute(total.astype(BF16), "tm", both_cores([(i, i + 1) for i in range(chips - 1)]))
+
+
+def second_stage(n, slot, tab, pair, got):
+    if n != 8:
+        return jnp.zeros_like(got), tab
+    pay, tab = relay(slot, tab, pair, got)
+    return lax.ppermute(pay, "tm", both_cores((ALONG_X if slot == 0 else ALONG_Y)[1])), tab
 
 
 def on_device(n, n_space, frames_in, w_input, decay_rate, phase, w_output):
@@ -439,9 +496,10 @@
     oth = lax.ppermute(own, "tm", swap)
 
     half = rows // 2
-    last = max(2, (half + 2) * 6 // 18)
-    middle = (half + 2 - last) // 2
-    spans = [(last - 1 + middle, half + 1), (last - 1, last - 1 + middle), (-1, last - 1)]
+    total = half + 1
+    last = max(2, total * 5 // 17)
+    middle = max(2, total * 5 // 17)
+    spans = [(last - 1 + middle, half), (last - 1, last - 1 + middle), (-1, last - 1)]
     links = [
         ((t ^ 1) * n_space + s, t * n_space + s + 1) if t % 2 == 0 else ((t ^ 1) * n_space + s + 1, t * n_space + s)
         for t in range(n)
@@ -449,24 +507,30 @@
     ]
     (lo1, hi1), (lo2, hi2), (lo3, hi3) = spans
     mine1, mine2, frame, weights, tab, factor = lead(roles(n), own, w_in, decay, phase, lo2, lo1, hi1, step)
-    theirs1, pair1, factor, border = pair_up(frame, oth, weights, tab, factor, mine1, lo1, hi1, step, True)
+    border, tab = outer_rows(frame, oth, tab)
     halo = lax.ppermute(border, ("tm", "space"), links)
-    theirs2, pair2, factor = pair_up(frame, oth, weights, tab, factor, mine2, lo2, hi2, step, False)
+    theirs1, pair1, tab = pair_up(oth, weights, tab, factor, mine1, lo1, hi1, step)
+    got1 = first_stage(n, 0, pair1, decay, phase)
+    theirs2, pair2, tab = pair_up(oth, weights, tab, factor, mine2, lo2, hi2, step)
+    got2 = first_stage(n, 4, pair2, decay, phase)
     mine3, theirs3, pair3, tab = edge_chunk(frame, oth, weights, tab, factor, halo, lo3, hi3, step)
-    arrived1 = exchange(n, 0, tab, pair1, decay, phase)
-    arrived2 = exchange(n, 4, tab, pair2, decay, phase)
-    arrived3 = exchange(n, 0, tab, pair3, decay, phase)
-    parcel1, result, kept = output(
-        tab, w_out, [(mine1, theirs1)], arrived1, frame, oth, lo1, hi1, lo1 + 1, half, 0, step, (0, 1), True
+    got3 = first_stage(n, 0, pair3, decay, phase)
+    also1, tab = second_stage(n, 0, tab, pair1, got1)
+    also2, tab = second_stage(n, 4, tab, pair2, got2)
+    also3, tab = second_stage(n, 0, tab, pair3, got3)
+    args = (w_out, (mine1, theirs1), (got1, also1), frame, oth, lo1, hi1, lo1 + 1, half - 1, 0, 2)
+    parcel1, block1, kept, near, send, tab = output(tab, *args, (0, 1))
+    far = lax.ppermute(send, "tm", swap)
+    args = (w_out, (mine2, theirs2), (got2, also2), frame, oth, lo2, hi2, lo2 + 1, hi2 + 1, 4, 2)
+    parcel2, block2, result, kept, tab = output(
+        tab, *args, (0, 1), kept=kept, blocks=(block1,), blocks_at=(lo1 + 1,)
     )
-    parcel2, result, kept = output(
-        tab, w_out, [(mine2, theirs2)], arrived2, frame, oth, lo2, hi2, lo2 + 1, hi2 + 1, 4, step, (0, 1), True,
-        kept=kept, result=result,
+    args = (w_out, (mine3, theirs3), (got3, also3), frame, oth, lo3, hi3, lo3 + 1, hi3 + 1, 0, 2)
+    parcel, tab = output(tab, *args, (0,), kept=kept, seam=(near, far), parts=(parcel2, parcel1))
+    block3, result = output(
+        tab, *args, (1,), kept=kept, seam=(near, far), blocks=(block2,), blocks_at=(lo2 + 1,), result=result
     )
-    rest = (tab, w_out, [(mine3, theirs3)], arrived3, frame, oth, lo3, hi3, lo3 + 1, hi3 + 1, 0, step)
-    (parcel,) = output(*rest, (0,), False, kept=kept, parts=(parcel2, parcel1))
-    (result,) = output(*rest, (1,), False, kept=kept, result=result)
-    return place(lax.ppermute(parcel, "tm", swap), result)[None]
+    return place(lax.ppermute(parcel, "tm", swap), block3, lo3 + 1, result)[None]
 
 
 def solution(mesh):

time: 50.1 us -> 48.1 us (0.960)
  the two profiles are of different devices: /device:TPU:15 before, /device:TPU:31 now
where the time goes in v5:
time: 48.1 us; the launch traced here: 47.8 us
  Pallas kernels  17.9 us (37%)
  starting transfers between devices  15.7 us (33%)
  waiting for transfers between devices  13.9 us (29%)
    ppermute x3, waiting for transfers between devices, first_stage(): lax.ppermute(pair, 'tm', both_cores((ALONG_X if slot == 0 else ALONG_Y)[0]))  8.13 us
    pallas_call x4, Pallas kernels, output(): pl.pallas_call(functools.partial(output_kernel, lo, hi, begin, end, slot,...  8.08 us
    ppermute x1, starting transfers between devices, on_device(): far = lax.ppermute(send, 'tm', swap)  5.52 us
    ppermute x3, waiting for transfers between devices, second_stage(): lax.ppermute(pay, 'tm', both_cores((ALONG_X if slot == 0 else ALONG_Y)[1]))  4.69 us
    ppermute x3, starting transfers between devices, second_stage(): lax.ppermute(pay, 'tm', both_cores((ALONG_X if slot == 0 else ALONG_Y)[1]))  4.69 us
    ppermute x3, starting transfers between devices, first_stage(): lax.ppermute(pair, 'tm', both_cores((ALONG_X if slot == 0 else ALONG_Y)[0]))  4.01 us
    pallas_call x1, Pallas kernels, lead(): pl.pallas_call(functools.partial(lead_kernel, entries, lo, mid, hi, step)...  3.64 us
    pallas_call x2, Pallas kernels, pair_up(): pl.pallas_call(functools.partial(pair_kernel, lo, hi, step), out_shape=[j...  2.37 us
  transfers between devices with their start and end apart: 10, of which 5 were waited for; matrix products, arithmetic and copies ran while one was open for 0% of the time, Pallas kernels for 29%

profile of v5, /device:TPU:31, one launch (start us, length us, event | category | flops | bytes accessed | tf_op | source)
XLA Modules:
  0.0 47.8 jit_solution(12825455127609870274)
XLA Ops:
  0.0 0.7 %collective-permute-start = (bf16[32,128,256]{2,1,0:T(8,128)(2,1)}, bf16[32,128,256]{2,1,0:T(8,128)(2,1)S(1)}, u32[]{:S(2)}, u32[]{:S(2)}) collective-permute-start(bf16[32,128,256]{2,1,0:T(8,128)(2,1)} %bitcast.10), channel_id=1, source_target_pairs={{0,4},{4,0},{8,12},{12,8},{16,20},{20,16},{24,28},{28,24},{1,5},{5... | collective-permute-start | bytes 6291464 | tf_op jit(solution)/shard_map/ppermute | solution.py:496
  0.7 3.6 %lead.1 = (f32[7,128,256]{2,1,0:T(8,128)S(1)}, f32[5,128,256]{2,1,0:T(8,128)S(1)}, bf16[32,128,256]{2,1,0:T(8,128)(2,1)S(1)}, bf16[3,768,256]{2,1,0:T(8,128)(2,1...) custom-call(bf16[32,128,256]{2,1,0:T(8,128)(2,1)} %bitcast.11, bf16[3,768,256]{2,1,0:T(8,128)(2,1)} %bitcast.12, ...), custom_call_target="tpu_custom_call" | custom-call | flops 1 | bytes 1 | tf_op jit(solution)/shard_map/lead/pallas_call | solution.py:131
  4.3 0.3 collective-permute-done.oth.refs_5_
  4.7 1.3 %pair.2 = (f32[7,128,256]{2,1,0:T(8,128)S(1)}, bf16[7,128,256]{2,1,0:T(8,128)(2,1)S(1)}, f32[32,128]{1,0:T(8,128)S(1)}) custom-call(bf16[32,128,256]{2,1,0:T(8,128)(2,1)S(1)} %collective-permute-done.oth.refs_5_, bf16[3,768,256]{2,1,0:T(8,128)(2,1)S(1)} %get-tuple-element.45.weights, f32[32,128]{1,0:T(8,128)S(1)} %get-tuple-element.47.tab, ...), custom_call_target="tpu_custom_call" | custom-call | flops 1 | bytes 1 | tf_op jit(solution)/shard_map/pair/pallas_call | solution.py:177
  6.0 1.3 %collective-permute-start.2 = (bf16[7,128,256]{2,1,0:T(8,128)(2,1)S(1)}, bf16[7,128,256]{2,1,0:T(8,128)(2,1)S(1)}, u32[]{:S(2)}, u32[]{:S(2)}) collective-permute-start(bf16[7,128,256]{2,1,0:T(8,128)(2,1)S(1)} %get-tuple-element.55.pair), channel_id=1, source_target_pairs={{0,8},{4,12},{8,0},{12,4},{16,24},{20,28},{1,9},{5,13},{9,1},{13,5... | collective-permute-start | bytes 1376264 | tf_op jit(solution)/shard_map/ppermute | solution.py:470
  7.3 0.7 %collective-permute-start.1 = (bf16[2,2,128,256]{3,2,1,0:T(8,128)(2,1)S(1)}, bf16[2,2,128,256]{3,2,1,0:T(8,128)(2,1)S(1)}, u32[]{:S(2)}, u32[]{:S(2)}) collective-permute-start(bf16[2,2,128,256]{3,2,1,0:T(8,128)(2,1)S(1)} %get-tuple-element.53), channel_id=1, source_target_pairs={{4,1},{5,2},{6,3},{1,4},{2,5},{3,6},{12,9},{13,10},{14,11},{9,12},... | collective-permute-start | bytes 786440 | tf_op jit(solution)/shard_map/ppermute | solution.py:511
  8.0 1.0 %pair.3 = (f32[5,128,256]{2,1,0:T(8,128)S(1)}, bf16[5,128,256]{2,1,0:T(8,128)(2,1)S(1)}, f32[32,128]{1,0:T(8,128)S(1)}) custom-call(bf16[32,128,256]{2,1,0:T(8,128)(2,1)S(1)} %collective-permute-done.oth.refs_5_, bf16[3,768,256]{2,1,0:T(8,128)(2,1)S(1)} %get-tuple-element.45.weights, f32[32,128]{1,0:T(8,128)S(1)} %get-tuple-element.50.tab, ...), custom_call_target="tpu_custom_call" | custom-call | flops 1 | bytes 1 | tf_op jit(solution)/shard_map/pair/pallas_call | solution.py:177
  9.1 1.3 %collective-permute-start.3 = (bf16[5,128,256]{2,1,0:T(8,128)(2,1)S(1)}, bf16[5,128,256]{2,1,0:T(8,128)(2,1)S(1)}, u32[]{:S(2)}, u32[]{:S(2)}) collective-permute-start(bf16[5,128,256]{2,1,0:T(8,128)(2,1)S(1)} %get-tuple-element.57.pair), channel_id=1, source_target_pairs={{0,16},{4,20},{8,24},{12,28},{1,17},{5,21},{9,25},{13,29},{2,18},{... | collective-permute-start | bytes 983048 | tf_op jit(solution)/shard_map/ppermute | solution.py:470
  10.4 1.8 %edge.1 = (f32[5,128,256]{2,1,0:T(8,128)S(1)}, f32[5,128,256]{2,1,0:T(8,128)S(1)}, bf16[5,128,256]{2,1,0:T(8,128)(2,1)S(1)}, f32[32,128]{1,0:T(8,128)S(1)}) custom-call(bf16[32,128,256]{2,1,0:T(8,128)(2,1)S(1)} %get-tuple-element.44.frame.refs_4_, bf16[32,128,256]{2,1,0:T(8,128)(2,1)S(1)} %collective-permute-done.oth.refs_5_, ...), custom_call_target="tpu_custom_call" | custom-call | flops 1 | bytes 1 | tf_op jit(solution)/shard_map/edge/pallas_call | solution.py:250
  12.2 1.4 %collective-permute-start.4 = (bf16[5,128,256]{2,1,0:T(8,128)(2,1)S(1)}, bf16[5,128,256]{2,1,0:T(8,128)(2,1)S(1)}, u32[]{:S(2)}, u32[]{:S(2)}) collective-permute-start(bf16[5,128,256]{2,1,0:T(8,128)(2,1)S(1)} %get-tuple-element.59.pair), channel_id=1, source_target_pairs={{0,8},{4,12},{8,0},{12,4},{16,24},{20,28},{1,9},{5,13},{9,1},{13,5... | collective-permute-start | bytes 983048 | tf_op jit(solution)/shard_map/ppermute | solution.py:470
  13.6 6.1 %collective-permute-done.2.got.refs_2_ = bf16[7,128,256]{2,1,0:T(8,128)(2,1)S(1)} collective-permute-done((bf16[7,128,256]{2,1,0:T(8,128)(2,1)S(1)}, bf16[7,128,256]{2,1,0:T(8,128)(2,1)S(1)}, u32[]{:S(2)}, u32[]{:S(2)}) %collective-permute-start.2) | collective-permute-done | bytes 458784 | tf_op jit(solution)/shard_map/ppermute | solution.py:470
  19.7 0.3 relay.3
  20.0 1.3 %collective-permute-start.5 = (bf16[7,128,256]{2,1,0:T(8,128)(2,1)S(1)}, bf16[7,128,256]{2,1,0:T(8,128)(2,1)S(1)}, u32[]{:S(2)}, u32[]{:S(2)}) collective-permute-start(bf16[7,128,256]{2,1,0:T(8,128)(2,1)S(1)} %get-tuple-element.61), channel_id=1, source_target_pairs={{0,16},{4,20},{8,24},{12,28},{1,17},{5,21},{9,25},{13,29},{2,18},{... | collective-permute-start | bytes 1376264 | tf_op jit(solution)/shard_map/ppermute | solution.py:485
  21.5 1.9 %collective-permute-start.6 = (bf16[5,128,256]{2,1,0:T(8,128)(2,1)S(1)}, bf16[5,128,256]{2,1,0:T(8,128)(2,1)S(1)}, u32[]{:S(2)}, u32[]{:S(2)}) collective-permute-start(bf16[5,128,256]{2,1,0:T(8,128)(2,1)S(1)} %get-tuple-element.64), channel_id=1, source_target_pairs={{0,8},{4,12},{16,24},{20,28},{24,16},{28,20},{1,9},{5,13},{17,25},... | collective-permute-start | bytes 983048 | tf_op jit(solution)/shard_map/ppermute | solution.py:485
  23.4 2.1 %collective-permute-done.4.got.refs_2_ = bf16[5,128,256]{2,1,0:T(8,128)(2,1)S(1)} collective-permute-done((bf16[5,128,256]{2,1,0:T(8,128)(2,1)S(1)}, bf16[5,128,256]{2,1,0:T(8,128)(2,1)S(1)}, u32[]{:S(2)}, u32[]{:S(2)}) %collective-permute-start.4) | collective-permute-done | bytes 327712 | tf_op jit(solution)/shard_map/ppermute | solution.py:470
  25.7 1.5 %collective-permute-start.7 = (bf16[5,128,256]{2,1,0:T(8,128)(2,1)S(1)}, bf16[5,128,256]{2,1,0:T(8,128)(2,1)S(1)}, u32[]{:S(2)}, u32[]{:S(2)}) collective-permute-start(bf16[5,128,256]{2,1,0:T(8,128)(2,1)S(1)} %get-tuple-element.69), channel_id=1, source_target_pairs={{0,16},{4,20},{8,24},{12,28},{1,17},{5,21},{9,25},{13,29},{2,18},{... | collective-permute-start | bytes 983048 | tf_op jit(solution)/shard_map/ppermute | solution.py:485
  27.2 4.7 %collective-permute-done.5.refs_3_ = bf16[7,128,256]{2,1,0:T(8,128)(2,1)S(1)} collective-permute-done((bf16[7,128,256]{2,1,0:T(8,128)(2,1)S(1)}, bf16[7,128,256]{2,1,0:T(8,128)(2,1)S(1)}, u32[]{:S(2)}, u32[]{:S(2)}) %collective-permute-start.5) | collective-permute-done | bytes 458784 | tf_op jit(solution)/shard_map/ppermute | solution.py:485
  31.9 2.1 %output.4 = (bf16[5,128,256]{2,1,0:T(8,128)(2,1)S(1)}, bf16[5,128,256]{2,1,0:T(8,128)(2,1)S(1)}, bf16[2,2,128,256]{3,2,1,0:T(8,128)(2,1)S(1)}, bf16[2,2,128,256]...) custom-call(f32[32,128]{1,0:T(8,128)S(1)} %get-tuple-element.60.refs_0_, ...), custom_call_target="tpu_custom_call" | custom-call | flops 1 | bytes 1 | tf_op jit(solution)/shard_map/output/pallas_call | solution.py:407
  34.0 5.5 %collective-permute-start.8 = (bf16[2,128,256]{2,1,0:T(8,128)(2,1)S(1)}, bf16[2,128,256]{2,1,0:T(8,128)(2,1)S(1)}, u32[]{:S(2)}, u32[]{:S(2)}) collective-permute-start(bf16[2,128,256]{2,1,0:T(8,128)(2,1)S(1)} %get-tuple-element.74), channel_id=1, source_target_pairs={{0,4},{4,0},{8,12},{12,8},{16,20},{20,16},{24,28},{28,24},{1,5},{5... | collective-permute-start | bytes 393224 | tf_op jit(solution)/shard_map/ppermute | solution.py:523
  39.5 2.6 %output.5 = (bf16[5,128,256]{2,1,0:T(8,128)(2,1)S(1)}, bf16[5,128,256]{2,1,0:T(8,128)(2,1)S(1)}, bf16[32,128,256]{2,1,0:T(8,128)(2,1)}, bf16[2,2,128,256]{3,2,1,0:T(8,128)(2,1)S(1)}, f32[32,128]{1,0:T(8,128)S(1)}) custom-call(f32[32,128]{1,0:T(8,128)S(1)} %get-tuple-element.63.refs_0_, bf16[3,768,256]{2,1,0:T(8,128)(2,1)S(1)} %bitcast.7, ...), custom_call_target="tpu_custom_call" | custom-call | flops 1 | bytes 1 | tf_op jit(solution)/shard_map/output/pallas_call | solution.py:407
  42.2 1.4 %output.6 = (bf16[16,128,256]{2,1,0:T(8,128)(2,1)S(1)}, f32[32,128]{1,0:T(8,128)S(1)}) custom-call(f32[32,128]{1,0:T(8,128)S(1)} %get-tuple-element.68.refs_0_, bf16[3,768,256]{2,1,0:T(8,128)(2,1)S(1)} %bitcast.8, bf16[5,128,256]{2,1,0:T(8,128)(2,1)S(1)} %collective-permute-done.4.got.refs_2_, bf16[5,128,256]{2,1,0:T(8,128)(2,1)S(1)} %collective-permute-done.7.refs_3_, ...), custom_call_target="tpu_custom_call" | custom-call | flops 1 | bytes 1 | tf_op jit(solution)/shard_map/output/pallas_call | solution.py:407
  43.7 1.9 %output.7 = (bf16[6,128,256]{2,1,0:T(8,128)(2,1)S(1)}, bf16[32,128,256]{2,1,0:T(8,128)(2,1)}) custom-call(f32[32,128]{1,0:T(8,128)S(1)} %get-tuple-element.78.refs_0_, bf16[3,768,256]{2,1,0:T(8,128)(2,1)S(1)} %bitcast.9, bf16[5,128,256]{2,1,0:T(8,128)(2,1)S(1)} %collective-permute-done.4.got.refs_2_, ...), custom_call_target="tpu_custom_call", output_to_operand_aliasing={{1}: (12, {})} | custom-call | flops 1 | bytes 1 | tf_op jit(solution)/shard_map/output/pallas_call | solution.py:407
  45.6 0.7 %collective-permute-done.9.parcel = bf16[16,128,256]{2,1,0:T(8,128)(2,1)S(1)} collective-permute-done((bf16[16,128,256]{2,1,0:T(8,128)(2,1)S(1)}, bf16[16,128,256]{2,1,0:T(8,128)(2,1)S(1)}, u32[]{:S(2)}, u32[]{:S(2)}) %collective-permute-start.9) | collective-permute-done | bytes 1048608 | tf_op jit(solution)/shard_map/ppermute | solution.py:533
  46.3 1.3 %place.1 = bf16[32,128,256]{2,1,0:T(8,128)(2,1)} custom-call(bf16[16,128,256]{2,1,0:T(8,128)(2,1)S(1)} %collective-permute-done.9.parcel, bf16[6,128,256]{2,1,0:T(8,128)(2,1)S(1)} %get-tuple-element.81.block, bf16[32,128,256]{2,1,0:T(8,128)(2,1)} %get-tuple-element.82._), custom_call_target="tpu_custom_call", output_to_operand_aliasing={{}: (2, {})} | custom-call | tf_op jit(solution)/shard_map/place/pallas_call | solution.py:440
  (11 shorter events, 0.6 us)
Async XLA Ops:
  0.0 4.7 %collective-permute-start = (bf16[32,128,256]{2,1,0:T(8,128)(2,1)}, bf16[32,128,256]{2,1,0:T(8,128)(2,1)S(1)}, u32[]{:S(2)}, u32[]{:S(2)}) collective-permute-start(bf16[32,128,256]{2,1,0:T(8,128)(2,1)} %bitcast.10), channel_id=1, source_target_pairs={{0,4},{4,0},{8,12},{12,8},{16,20},{20,16},{24,28},{28,24},{1,5},{5... | collective-permute-start | bytes 6291464 | tf_op jit(solution)/shard_map/ppermute | solution.py:496
  6.0 13.6 %collective-permute-start.2 = (bf16[7,128,256]{2,1,0:T(8,128)(2,1)S(1)}, bf16[7,128,256]{2,1,0:T(8,128)(2,1)S(1)}, u32[]{:S(2)}, u32[]{:S(2)}) collective-permute-start(bf16[7,128,256]{2,1,0:T(8,128)(2,1)S(1)} %get-tuple-element.55.pair), channel_id=1, source_target_pairs={{0,8},{4,12},{8,0},{12,4},{16,24},{20,28},{1,9},{5,13},{9,1},{13,5... | collective-permute-start | bytes 1376264 | tf_op jit(solution)/shard_map/ppermute | solution.py:470
  7.3 3.0 %collective-permute-start.1 = (bf16[2,2,128,256]{3,2,1,0:T(8,128)(2,1)S(1)}, bf16[2,2,128,256]{3,2,1,0:T(8,128)(2,1)S(1)}, u32[]{:S(2)}, u32[]{:S(2)}) collective-permute-start(bf16[2,2,128,256]{3,2,1,0:T(8,128)(2,1)S(1)} %get-tuple-element.53), channel_id=1, source_target_pairs={{4,1},{5,2},{6,3},{1,4},{2,5},{3,6},{12,9},{13,10},{14,11},{9,12},... | collective-permute-start | bytes 786440 | tf_op jit(solution)/shard_map/ppermute | solution.py:511
  9.1 12.2 %collective-permute-start.3 = (bf16[5,128,256]{2,1,0:T(8,128)(2,1)S(1)}, bf16[5,128,256]{2,1,0:T(8,128)(2,1)S(1)}, u32[]{:S(2)}, u32[]{:S(2)}) collective-permute-start(bf16[5,128,256]{2,1,0:T(8,128)(2,1)S(1)} %get-tuple-element.57.pair), channel_id=1, source_target_pairs={{0,16},{4,20},{8,24},{12,28},{1,17},{5,21},{9,25},{13,29},{2,18},{... | collective-permute-start | bytes 983048 | tf_op jit(solution)/shard_map/ppermute | solution.py:470
  12.2 19.7 %copy-start = (bf16[3,3,256,256]{3,2,1,0:T(8,128)(2,1)S(1)}, bf16[3,3,256,256]{3,2,1,0:T(8,128)(2,1)}, u32[]{:S(2)}) copy-start(bf16[3,3,256,256]{3,2,1,0:T(8,128)(2,1)} %param.9) | copy-start | bytes 3538948
  12.2 13.3 %collective-permute-start.4 = (bf16[5,128,256]{2,1,0:T(8,128)(2,1)S(1)}, bf16[5,128,256]{2,1,0:T(8,128)(2,1)S(1)}, u32[]{:S(2)}, u32[]{:S(2)}) collective-permute-start(bf16[5,128,256]{2,1,0:T(8,128)(2,1)S(1)} %get-tuple-element.59.pair), channel_id=1, source_target_pairs={{0,8},{4,12},{8,0},{12,4},{16,24},{20,28},{1,9},{5,13},{9,1},{13,5... | collective-permute-start | bytes 983048 | tf_op jit(solution)/shard_map/ppermute | solution.py:470
  20.0 11.9 %collective-permute-start.5 = (bf16[7,128,256]{2,1,0:T(8,128)(2,1)S(1)}, bf16[7,128,256]{2,1,0:T(8,128)(2,1)S(1)}, u32[]{:S(2)}, u32[]{:S(2)}) collective-permute-start(bf16[7,128,256]{2,1,0:T(8,128)(2,1)S(1)} %get-tuple-element.61), channel_id=1, source_target_pairs={{0,16},{4,20},{8,24},{12,28},{1,17},{5,21},{9,25},{13,29},{2,18},{... | collective-permute-start | bytes 1376264 | tf_op jit(solution)/shard_map/ppermute | solution.py:485
  21.5 18.1 %collective-permute-start.6 = (bf16[5,128,256]{2,1,0:T(8,128)(2,1)S(1)}, bf16[5,128,256]{2,1,0:T(8,128)(2,1)S(1)}, u32[]{:S(2)}, u32[]{:S(2)}) collective-permute-start(bf16[5,128,256]{2,1,0:T(8,128)(2,1)S(1)} %get-tuple-element.64), channel_id=1, source_target_pairs={{0,8},{4,12},{16,24},{20,28},{24,16},{28,20},{1,9},{5,13},{17,25},... | collective-permute-start | bytes 983048 | tf_op jit(solution)/shard_map/ppermute | solution.py:485
  25.7 16.5 %collective-permute-start.7 = (bf16[5,128,256]{2,1,0:T(8,128)(2,1)S(1)}, bf16[5,128,256]{2,1,0:T(8,128)(2,1)S(1)}, u32[]{:S(2)}, u32[]{:S(2)}) collective-permute-start(bf16[5,128,256]{2,1,0:T(8,128)(2,1)S(1)} %get-tuple-element.69), channel_id=1, source_target_pairs={{0,16},{4,20},{8,24},{12,28},{1,17},{5,21},{9,25},{13,29},{2,18},{... | collective-permute-start | bytes 983048 | tf_op jit(solution)/shard_map/ppermute | solution.py:485
  34.0 8.1 %collective-permute-start.8 = (bf16[2,128,256]{2,1,0:T(8,128)(2,1)S(1)}, bf16[2,128,256]{2,1,0:T(8,128)(2,1)S(1)}, u32[]{:S(2)}, u32[]{:S(2)}) collective-permute-start(bf16[2,128,256]{2,1,0:T(8,128)(2,1)S(1)} %get-tuple-element.74), channel_id=1, source_target_pairs={{0,4},{4,0},{8,12},{12,8},{16,20},{20,16},{24,28},{28,24},{1,5},{5... | collective-permute-start | bytes 393224 | tf_op jit(solution)/shard_map/ppermute | solution.py:523
  43.6 2.7 %collective-permute-start.9 = (bf16[16,128,256]{2,1,0:T(8,128)(2,1)S(1)}, bf16[16,128,256]{2,1,0:T(8,128)(2,1)S(1)}, u32[]{:S(2)}, u32[]{:S(2)}) collective-permute-start(bf16[16,128,256]{2,1,0:T(8,128)(2,1)S(1)} %get-tuple-element.77), channel_id=1, source_target_pairs={{0,4},{4,0},{8,12},{12,8},{16,20},{20,16},{24,28},{28,24},{1,5},{5... | collective-permute-start | bytes 3145736 | tf_op jit(solution)/shard_map/ppermute | solution.py:533

commit v6 on v5

--- a/solution.py
+++ b/solution.py
@@ -14,6 +14,7 @@
 HBM = pl.BlockSpec(memory_space=pltpu.HBM)
 PARAMS = pltpu.CompilerParams(vmem_limit_bytes=24 * 1024 * 1024)
 SHORT = pl.CostEstimate(flops=1, bytes_accessed=1, transcendentals=0)
+CLOSING = pl.CostEstimate(flops=4000000000, bytes_accessed=1, transcendentals=0)
 LONG = pl.CostEstimate(flops=1, bytes_accessed=1, transcendentals=0)
 SLOTS = 16
 
@@ -259,7 +260,7 @@
         out_specs=[VMEM] * 4,
         scratch_shapes=[pltpu.VMEM((2, n + 2, w, 3 * c), BF16)],
         compiler_params=PARAMS,
-        cost_estimate=SHORT,
+        cost_estimate=pl.CostEstimate(flops=1, bytes_accessed=1, transcendentals=0),
         name="edge",
     )(frame, oth, weights, tab, factor, halo)
 
@@ -271,14 +272,14 @@
         pay[r] = (cmul(cp, pair[r].astype(F32)) + cmul(cr, got[r].astype(F32))).astype(BF16)
 
 
-def relay(slot, tab, pair, got):
+def relay(slot, tab, pair, got, hint=SHORT):
     return pl.pallas_call(
         functools.partial(relay_kernel, slot),
         out_shape=[jax.ShapeDtypeStruct(pair.shape, BF16), jax.ShapeDtypeStruct(tab.shape, F32)],
         in_specs=[VMEM] * 3,
         out_specs=[VMEM] * 2,
         compiler_params=PARAMS,
-        cost_estimate=SHORT,
+        cost_estimate=hint,
         name="relay",
     )(tab, pair, got)
 
@@ -306,16 +307,14 @@
     w, c = own.shape[1:]
     rows = own.shape[0]
     copies = []
-    for ref, depth in zip(blocks, blocks_at):
-        copies += start_rows(ref, result, core, depth, refs[0], len(copies))
+    for ref, (depth, mine) in zip(blocks, blocks_at):
+        copies.append(start_rows(ref, result, core if mine else 1 - core, depth, refs[0].at[len(copies)]))
     if tab_next is not None:
         tab_next[...] = tab[...]
     lam = coefficient(tab, 8)
     e1, e2 = coefficient(tab, slot + 2), coefficient(tab, slot + 3)
-    at = n_out
     for part in parts:
-        parcel[at : at + part.shape[0]] = part[...]
-        at += part.shape[0]
+        parcel[pl.ds(jnp.where(first_core, n_out, 0), part.shape[0])] = part[...]
 
     def states(r):
         f_own, f_oth = feed_own[r], feed_oth[r]
@@ -324,20 +323,21 @@
         s1 = cmul(lam, s0) + jnp.where(first_core, f_oth, f_own)
         return jnp.where(first_core, s1, s0), jnp.where(first_core, s0, s1)
 
-    def emit(f, first_wide, size, depth, place):
+    def emit(f, first_wide, size, depth, place, span):
         frame, dst = ((oth, parcel), (own, block))[f]
         mixed = conv_block(wide.at[f], weights, first_wide, size, order).reshape(size, w, c)
         act = 0.5 * mixed * (1.0 + lax.erf(mixed * np.float32(0.5**0.5)))
         for r in range(size):
             row = jnp.where(core == 1, rows - 1 - depth - r, depth + r)
-            dst[place + r] = (frame[row].astype(F32) + act[r]).astype(BF16)
+            to = jnp.where(first_core, place + r, span - 1 - place - r) if span else place + r
+            dst[to] = (frame[row].astype(F32) + act[r]).astype(BF16)
 
     if closing:
         top = n_out + 2
         for f in which:
             for k, z in enumerate((near[f, 0], near[f, 1], far[1 - f])):
                 wide[f, top + k] = widen(z.astype(F32))
-            emit(f, top, 1, rows // 2 - 1, (parcel if f == 0 else block).shape[0] - 1)
+            emit(f, top, 1, rows // 2 - 1, (parcel if f == 0 else block).shape[0] - 1, 0)
     ready = 0
     for s in range(0, n_out, step):
         size = min(step, n_out - s)
@@ -357,18 +357,17 @@
                 wide[f, ready] = widen(pair[f])
             ready += 1
         for f in which:
-            emit(f, s, size, begin + s, s)
+            emit(f, s, size, begin + s, s, (parcel if f == 0 else block).shape[0] - (1 if closing else 0))
     for copy in copies:
         copy.wait()
 
 
-def start_rows(block, result, side, depth, sem, at=0):
-    copies = []
-    for r in range(block.shape[0]):
-        row = jnp.where(side == 1, result.shape[0] - 1 - depth - r, depth + r)
-        copies.append(pltpu.make_async_copy(block.at[r], result.at[row], sem.at[at + r]))
-        copies[-1].start()
-    return copies
+def start_rows(block, result, side, depth, sem):
+    n = block.shape[0]
+    start = jnp.where(side == 1, result.shape[0] - depth - n, depth)
+    copy = pltpu.make_async_copy(block, result.at[pl.ds(start, n)], sem)
+    copy.start()
+    return copy
 
 
 def output(
@@ -392,7 +391,7 @@
         out_specs = out_specs + [VMEM]
     scratch = [pltpu.VMEM((2, n_out + (5 if closing else 2), w, 3 * c), BF16)]
     if blocks:
-        scratch += [pltpu.SemaphoreType.DMA((sum(ref.shape[0] for ref in blocks),))]
+        scratch += [pltpu.SemaphoreType.DMA((len(blocks),))]
         if result is not None:
             alias = {len(args): len(shapes)}
             args, specs = args + [result], specs + [HBM]
@@ -414,36 +413,31 @@
         input_output_aliases=alias,
         scratch_shapes=scratch,
         compiler_params=PARAMS,
-        cost_estimate=LONG if first else SHORT,
+        cost_estimate=LONG if first else CLOSING if closing and 0 in which else SHORT,
         name="output",
     )(*args)
 
 
-def place_kernel(depth, n_two, parcel, block, _, result, sem):
+def place_kernel(depth, parcel, block, _, result, sem):
     core = my_core()
     inner = result.shape[0] // 2 - 1
-    n = block.shape[0] - 1
-    at = 0
     copies = []
-    for ref, side, start, count in ((parcel, 1 - core, 0, n + n_two), (block, core, depth, n)):
-        for r in range(count + 1):
-            to = inner if r == count else start + r
-            row = jnp.where(side == 1, result.shape[0] - 1 - to, to)
-            copies.append(pltpu.make_async_copy(ref.at[r], result.at[row], sem.at[at]))
-            copies[-1].start()
-            at += 1
+    for k, (ref, side) in enumerate(((parcel, 1 - core), (block, core))):
+        n = ref.shape[0] - 1
+        copies.append(start_rows(ref.at[pl.ds(0, n)], result, side, depth, sem.at[2 * k]))
+        copies.append(start_rows(ref.at[pl.ds(n, 1)], result, side, inner, sem.at[2 * k + 1]))
     for copy in copies:
         copy.wait()
 
 
 def place(parcel, block, depth, result):
     return pl.pallas_call(
-        functools.partial(place_kernel, depth, parcel.shape[0] - block.shape[0]),
+        functools.partial(place_kernel, depth),
         out_shape=jax.ShapeDtypeStruct(result.shape, result.dtype),
         in_specs=[VMEM, VMEM, HBM],
         out_specs=HBM,
         input_output_aliases={2: 0},
-        scratch_shapes=[pltpu.SemaphoreType.DMA((parcel.shape[0] + block.shape[0],))],
+        scratch_shapes=[pltpu.SemaphoreType.DMA((4,))],
         compiler_params=PARAMS,
         name="place",
     )(parcel, block, result)
@@ -478,10 +472,10 @@
     return lax.ppermute(total.astype(BF16), "tm", both_cores([(i, i + 1) for i in range(chips - 1)]))
 
 
-def second_stage(n, slot, tab, pair, got):
+def second_stage(n, slot, tab, pair, got, hint=SHORT):
     if n != 8:
         return jnp.zeros_like(got), tab
-    pay, tab = relay(slot, tab, pair, got)
+    pay, tab = relay(slot, tab, pair, got, hint)
     return lax.ppermute(pay, "tm", both_cores((ALONG_X if slot == 0 else ALONG_Y)[1])), tab
 
 
@@ -497,7 +491,7 @@
 
     half = rows // 2
     total = half + 1
-    last = max(2, total * 5 // 17)
+    last = max(3, total * 5 // 17)
     middle = max(2, total * 5 // 17)
     spans = [(last - 1 + middle, half), (last - 1, last - 1 + middle), (-1, last - 1)]
     links = [
@@ -517,18 +511,20 @@
     got3 = first_stage(n, 0, pair3, decay, phase)
     also1, tab = second_stage(n, 0, tab, pair1, got1)
     also2, tab = second_stage(n, 4, tab, pair2, got2)
-    also3, tab = second_stage(n, 0, tab, pair3, got3)
+    also3, tab = second_stage(n, 0, tab, pair3, got3, pl.CostEstimate(flops=1, bytes_accessed=1, transcendentals=0))
     args = (w_out, (mine1, theirs1), (got1, also1), frame, oth, lo1, hi1, lo1 + 1, half - 1, 0, 2)
     parcel1, block1, kept, near, send, tab = output(tab, *args, (0, 1))
     far = lax.ppermute(send, "tm", swap)
     args = (w_out, (mine2, theirs2), (got2, also2), frame, oth, lo2, hi2, lo2 + 1, hi2 + 1, 4, 2)
     parcel2, block2, result, kept, tab = output(
-        tab, *args, (0, 1), kept=kept, blocks=(block1,), blocks_at=(lo1 + 1,)
+        tab, *args, (0, 1), kept=kept, parts=(parcel1,), blocks=(block1,), blocks_at=((lo1 + 1, 1),)
     )
+    early = lax.ppermute(parcel2, "tm", swap)
     args = (w_out, (mine3, theirs3), (got3, also3), frame, oth, lo3, hi3, lo3 + 1, hi3 + 1, 0, 2)
-    parcel, tab = output(tab, *args, (0,), kept=kept, seam=(near, far), parts=(parcel2, parcel1))
+    parcel, tab = output(tab, *args, (0,), kept=kept, seam=(near, far))
     block3, result = output(
-        tab, *args, (1,), kept=kept, seam=(near, far), blocks=(block2,), blocks_at=(lo2 + 1,), result=result
+        tab, *args, (1,), kept=kept, seam=(near, far), blocks=(block2, early), blocks_at=((lo2 + 1, 1), (lo2 + 1, 0)),
+        result=result,
     )
     return place(lax.ppermute(parcel, "tm", swap), block3, lo3 + 1, result)[None]
 

time: 48.1 us -> 47.7 us (level)
  starting transfers between devices: 15.7 us -> 16.2 us
  waiting for transfers between devices: 13.9 us -> 13.4 us
    ppermute x1, waiting for transfers between devices: 0.7 us -> 0.01 us  [on_device(): lax.ppermute(parcel, 'tm', swap)]
  transfers between devices with their start and end apart: 10 -> 11, of which waited for: 5 -> 5; matrix products, arithmetic and copies ran while one was open for 0% -> 0% of each run, Pallas kernels for 29% -> 32%
where the time goes in v6:
time: 47.7 us; the launch traced here: 47.4 us
  Pallas kernels  17.5 us (37%)
  starting transfers between devices  16.2 us (34%)
  waiting for transfers between devices  13.4 us (28%)
    ppermute x3, waiting for transfers between devices, first_stage(): lax.ppermute(pair, 'tm', both_cores((ALONG_X if slot == 0 else ALONG_Y)[0]))  8.15 us
    pallas_call x4, Pallas kernels, output(): pl.pallas_call(functools.partial(output_kernel, lo, hi, begin, end, slot,...  8.06 us
    ppermute x1, starting transfers between devices, on_device(): far = lax.ppermute(send, 'tm', swap)  5.51 us
    ppermute x3, waiting for transfers between devices, second_stage(): lax.ppermute(pay, 'tm', both_cores((ALONG_X if slot == 0 else ALONG_Y)[1]))  4.69 us
    ppermute x3, starting transfers between devices, second_stage(): lax.ppermute(pay, 'tm', both_cores((ALONG_X if slot == 0 else ALONG_Y)[1]))  4.69 us
    ppermute x3, starting transfers between devices, first_stage(): lax.ppermute(pair, 'tm', both_cores((ALONG_X if slot == 0 else ALONG_Y)[0]))  4.01 us
    pallas_call x1, Pallas kernels, lead(): pl.pallas_call(functools.partial(lead_kernel, entries, lo, mid, hi, step)...  3.64 us
    pallas_call x2, Pallas kernels, pair_up(): pl.pallas_call(functools.partial(pair_kernel, lo, hi, step), out_shape=[j...  2.37 us
  transfers between devices with their start and end apart: 11, of which 5 were waited for; matrix products, arithmetic and copies ran while one was open for 0% of the time, Pallas kernels for 32%

profile of v6, /device:TPU:31, one launch (start us, length us, event | category | flops | bytes accessed | tf_op | source)
XLA Modules:
  0.0 47.4 jit_solution(14933758757549563530)
XLA Ops:
  0.0 0.7 %collective-permute-start = (bf16[32,128,256]{2,1,0:T(8,128)(2,1)}, bf16[32,128,256]{2,1,0:T(8,128)(2,1)S(1)}, u32[]{:S(2)}, u32[]{:S(2)}) collective-permute-start(bf16[32,128,256]{2,1,0:T(8,128)(2,1)} %bitcast.10), channel_id=1, source_target_pairs={{0,4},{4,0},{8,12},{12,8},{16,20},{20,16},{24,28},{28,24},{1,5},{5... | collective-permute-start | bytes 6291464 | tf_op jit(solution)/shard_map/ppermute | solution.py:490
  0.7 3.6 %lead.1 = (f32[7,128,256]{2,1,0:T(8,128)S(1)}, f32[5,128,256]{2,1,0:T(8,128)S(1)}, bf16[32,128,256]{2,1,0:T(8,128)(2,1)S(1)}, bf16[3,768,256]{2,1,0:T(8,128)(2,1...) custom-call(bf16[32,128,256]{2,1,0:T(8,128)(2,1)} %bitcast.11, bf16[3,768,256]{2,1,0:T(8,128)(2,1)} %bitcast.12, ...), custom_call_target="tpu_custom_call" | custom-call | flops 1 | bytes 1 | tf_op jit(solution)/shard_map/lead/pallas_call | solution.py:132
  4.3 0.3 collective-permute-done.oth.refs_5_
  4.7 1.3 %pair.2 = (f32[7,128,256]{2,1,0:T(8,128)S(1)}, bf16[7,128,256]{2,1,0:T(8,128)(2,1)S(1)}, f32[32,128]{1,0:T(8,128)S(1)}) custom-call(bf16[32,128,256]{2,1,0:T(8,128)(2,1)S(1)} %collective-permute-done.oth.refs_5_, bf16[3,768,256]{2,1,0:T(8,128)(2,1)S(1)} %get-tuple-element.45.weights, f32[32,128]{1,0:T(8,128)S(1)} %get-tuple-element.47.tab, ...), custom_call_target="tpu_custom_call" | custom-call | flops 1 | bytes 1 | tf_op jit(solution)/shard_map/pair/pallas_call | solution.py:178
  6.0 1.3 %collective-permute-start.2 = (bf16[7,128,256]{2,1,0:T(8,128)(2,1)S(1)}, bf16[7,128,256]{2,1,0:T(8,128)(2,1)S(1)}, u32[]{:S(2)}, u32[]{:S(2)}) collective-permute-start(bf16[7,128,256]{2,1,0:T(8,128)(2,1)S(1)} %get-tuple-element.55.pair), channel_id=1, source_target_pairs={{0,8},{4,12},{8,0},{12,4},{16,24},{20,28},{1,9},{5,13},{9,1},{13,5... | collective-permute-start | bytes 1376264 | tf_op jit(solution)/shard_map/ppermute | solution.py:464
  7.3 0.7 %collective-permute-start.1 = (bf16[2,2,128,256]{3,2,1,0:T(8,128)(2,1)S(1)}, bf16[2,2,128,256]{3,2,1,0:T(8,128)(2,1)S(1)}, u32[]{:S(2)}, u32[]{:S(2)}) collective-permute-start(bf16[2,2,128,256]{3,2,1,0:T(8,128)(2,1)S(1)} %get-tuple-element.53), channel_id=1, source_target_pairs={{4,1},{5,2},{6,3},{1,4},{2,5},{3,6},{12,9},{13,10},{14,11},{9,12},... | collective-permute-start | bytes 786440 | tf_op jit(solution)/shard_map/ppermute | solution.py:505
  8.0 1.0 %pair.3 = (f32[5,128,256]{2,1,0:T(8,128)S(1)}, bf16[5,128,256]{2,1,0:T(8,128)(2,1)S(1)}, f32[32,128]{1,0:T(8,128)S(1)}) custom-call(bf16[32,128,256]{2,1,0:T(8,128)(2,1)S(1)} %collective-permute-done.oth.refs_5_, bf16[3,768,256]{2,1,0:T(8,128)(2,1)S(1)} %get-tuple-element.45.weights, f32[32,128]{1,0:T(8,128)S(1)} %get-tuple-element.50.tab, ...), custom_call_target="tpu_custom_call" | custom-call | flops 1 | bytes 1 | tf_op jit(solution)/shard_map/pair/pallas_call | solution.py:178
  9.1 1.3 %collective-permute-start.3 = (bf16[5,128,256]{2,1,0:T(8,128)(2,1)S(1)}, bf16[5,128,256]{2,1,0:T(8,128)(2,1)S(1)}, u32[]{:S(2)}, u32[]{:S(2)}) collective-permute-start(bf16[5,128,256]{2,1,0:T(8,128)(2,1)S(1)} %get-tuple-element.57.pair), channel_id=1, source_target_pairs={{0,16},{4,20},{8,24},{12,28},{1,17},{5,21},{9,25},{13,29},{2,18},{... | collective-permute-start | bytes 983048 | tf_op jit(solution)/shard_map/ppermute | solution.py:464
  10.4 1.8 %edge.1 = (f32[5,128,256]{2,1,0:T(8,128)S(1)}, f32[5,128,256]{2,1,0:T(8,128)S(1)}, bf16[5,128,256]{2,1,0:T(8,128)(2,1)S(1)}, f32[32,128]{1,0:T(8,128)S(1)}) custom-call(bf16[32,128,256]{2,1,0:T(8,128)(2,1)S(1)} %get-tuple-element.44.frame.refs_4_, bf16[32,128,256]{2,1,0:T(8,128)(2,1)S(1)} %collective-permute-done.oth.refs_5_, ...), custom_call_target="tpu_custom_call" | custom-call | flops 1 | bytes 1 | tf_op jit(solution)/shard_map/edge/pallas_call | solution.py:251
  12.2 1.4 %collective-permute-start.4 = (bf16[5,128,256]{2,1,0:T(8,128)(2,1)S(1)}, bf16[5,128,256]{2,1,0:T(8,128)(2,1)S(1)}, u32[]{:S(2)}, u32[]{:S(2)}) collective-permute-start(bf16[5,128,256]{2,1,0:T(8,128)(2,1)S(1)} %get-tuple-element.59.pair), channel_id=1, source_target_pairs={{0,8},{4,12},{8,0},{12,4},{16,24},{20,28},{1,9},{5,13},{9,1},{13,5... | collective-permute-start | bytes 983048 | tf_op jit(solution)/shard_map/ppermute | solution.py:464
  13.6 6.1 %collective-permute-done.2.got.refs_2_ = bf16[7,128,256]{2,1,0:T(8,128)(2,1)S(1)} collective-permute-done((bf16[7,128,256]{2,1,0:T(8,128)(2,1)S(1)}, bf16[7,128,256]{2,1,0:T(8,128)(2,1)S(1)}, u32[]{:S(2)}, u32[]{:S(2)}) %collective-permute-start.2) | collective-permute-done | bytes 458784 | tf_op jit(solution)/shard_map/ppermute | solution.py:464
  19.7 0.3 relay.3
  20.0 1.3 %collective-permute-start.5 = (bf16[7,128,256]{2,1,0:T(8,128)(2,1)S(1)}, bf16[7,128,256]{2,1,0:T(8,128)(2,1)S(1)}, u32[]{:S(2)}, u32[]{:S(2)}) collective-permute-start(bf16[7,128,256]{2,1,0:T(8,128)(2,1)S(1)} %get-tuple-element.61), channel_id=1, source_target_pairs={{0,16},{4,20},{8,24},{12,28},{1,17},{5,21},{9,25},{13,29},{2,18},{... | collective-permute-start | bytes 1376264 | tf_op jit(solution)/shard_map/ppermute | solution.py:479
  21.5 1.9 %collective-permute-start.6 = (bf16[5,128,256]{2,1,0:T(8,128)(2,1)S(1)}, bf16[5,128,256]{2,1,0:T(8,128)(2,1)S(1)}, u32[]{:S(2)}, u32[]{:S(2)}) collective-permute-start(bf16[5,128,256]{2,1,0:T(8,128)(2,1)S(1)} %get-tuple-element.64), channel_id=1, source_target_pairs={{0,8},{4,12},{16,24},{20,28},{24,16},{28,20},{1,9},{5,13},{17,25},... | collective-permute-start | bytes 983048 | tf_op jit(solution)/shard_map/ppermute | solution.py:479
  23.4 2.1 %collective-permute-done.4.got.refs_2_ = bf16[5,128,256]{2,1,0:T(8,128)(2,1)S(1)} collective-permute-done((bf16[5,128,256]{2,1,0:T(8,128)(2,1)S(1)}, bf16[5,128,256]{2,1,0:T(8,128)(2,1)S(1)}, u32[]{:S(2)}, u32[]{:S(2)}) %collective-permute-start.4) | collective-permute-done | bytes 327712 | tf_op jit(solution)/shard_map/ppermute | solution.py:464
  25.7 1.5 %collective-permute-start.7 = (bf16[5,128,256]{2,1,0:T(8,128)(2,1)S(1)}, bf16[5,128,256]{2,1,0:T(8,128)(2,1)S(1)}, u32[]{:S(2)}, u32[]{:S(2)}) collective-permute-start(bf16[5,128,256]{2,1,0:T(8,128)(2,1)S(1)} %get-tuple-element.70), channel_id=1, source_target_pairs={{0,16},{4,20},{8,24},{12,28},{1,17},{5,21},{9,25},{13,29},{2,18},{... | collective-permute-start | bytes 983048 | tf_op jit(solution)/shard_map/ppermute | solution.py:479
  27.2 4.7 %collective-permute-done.5.refs_3_ = bf16[7,128,256]{2,1,0:T(8,128)(2,1)S(1)} collective-permute-done((bf16[7,128,256]{2,1,0:T(8,128)(2,1)S(1)}, bf16[7,128,256]{2,1,0:T(8,128)(2,1)S(1)}, u32[]{:S(2)}, u32[]{:S(2)}) %collective-permute-start.5) | collective-permute-done | bytes 458784 | tf_op jit(solution)/shard_map/ppermute | solution.py:479
  31.9 2.2 %output.4 = (bf16[5,128,256]{2,1,0:T(8,128)(2,1)S(1)}, bf16[5,128,256]{2,1,0:T(8,128)(2,1)S(1)}, bf16[2,2,128,256]{3,2,1,0:T(8,128)(2,1)S(1)}, bf16[2,2,128,256]...) custom-call(f32[32,128]{1,0:T(8,128)S(1)} %get-tuple-element.60.refs_0_, ...), custom_call_target="tpu_custom_call" | custom-call | flops 1 | bytes 1 | tf_op jit(solution)/shard_map/output/pallas_call | solution.py:406
  34.0 5.5 %collective-permute-start.8 = (bf16[2,128,256]{2,1,0:T(8,128)(2,1)S(1)}, bf16[2,128,256]{2,1,0:T(8,128)(2,1)S(1)}, u32[]{:S(2)}, u32[]{:S(2)}) collective-permute-start(bf16[2,128,256]{2,1,0:T(8,128)(2,1)S(1)} %get-tuple-element.75), channel_id=1, source_target_pairs={{0,4},{4,0},{8,12},{12,8},{16,20},{20,16},{24,28},{28,24},{1,5},{5... | collective-permute-start | bytes 393224 | tf_op jit(solution)/shard_map/ppermute | solution.py:517
  39.5 2.6 %output.5 = (bf16[10,128,256]{2,1,0:T(8,128)(2,1)S(1)}, bf16[5,128,256]{2,1,0:T(8,128)(2,1)S(1)}, bf16[32,128,256]{2,1,0:T(8,128)(2,1)}, bf16[2,2,128,256]{3,2,1,0:T(8,128)(2,1)S(1)}, f32[32,128]{1,0:T(8,128)S(1)}) custom-call(f32[32,128]{1,0:T(8,128)S(1)} %get-tuple-element.63.refs_0_, bf16[3,768,256]{2,1,0:T(8,128)(2,1)S(1)} %bitcast.7, ...), custom_call_target="tpu_custom_call" | custom-call | flops 1 | bytes 1 | tf_op jit(solution)/shard_map/output/pallas_call | solution.py:406
  42.2 1.3 %output.6 = (bf16[6,128,256]{2,1,0:T(8,128)(2,1)S(1)}, f32[32,128]{1,0:T(8,128)S(1)}) custom-call(f32[32,128]{1,0:T(8,128)S(1)} %get-tuple-element.69.refs_0_, bf16[3,768,256]{2,1,0:T(8,128)(2,1)S(1)} %bitcast.8, bf16[5,128,256]{2,1,0:T(8,128)(2,1)S(1)} %collective-permute-done.4.got.refs_2_, bf16[5,128,256]{2,1,0:T(8,128)(2,1)S(1)} %collective-permute-done.7.refs_3_, ...), custom_call_target="tpu_custom_call" | custom-call | flops 4000000000 | bytes 1 | tf_op jit(solution)/shard_map/output/pallas_call | solution.py:406
  43.5 0.5 %collective-permute-start.9 = (bf16[6,128,256]{2,1,0:T(8,128)(2,1)S(1)}, bf16[6,128,256]{2,1,0:T(8,128)(2,1)S(1)}, u32[]{:S(2)}, u32[]{:S(2)}) collective-permute-start(bf16[6,128,256]{2,1,0:T(8,128)(2,1)S(1)} %get-tuple-element.76), channel_id=1, source_target_pairs={{0,4},{4,0},{8,12},{12,8},{16,20},{20,16},{24,28},{28,24},{1,5},{5... | collective-permute-start | bytes 1179656 | tf_op jit(solution)/shard_map/ppermute | solution.py:529
  44.3 2.0 %output.7 = (bf16[6,128,256]{2,1,0:T(8,128)(2,1)S(1)}, bf16[32,128,256]{2,1,0:T(8,128)(2,1)}) custom-call(f32[32,128]{1,0:T(8,128)S(1)} %get-tuple-element.77.refs_0_, bf16[3,768,256]{2,1,0:T(8,128)(2,1)S(1)} %bitcast.9, bf16[5,128,256]{2,1,0:T(8,128)(2,1)S(1)} %collective-permute-done.4.got.refs_2_, ...), custom_call_target="tpu_custom_call", output_to_operand_aliasing={{1}: (13, {})} | custom-call | flops 1 | bytes 1 | tf_op jit(solution)/shard_map/output/pallas_call | solution.py:406
  46.3 0.9 %place.1 = bf16[32,128,256]{2,1,0:T(8,128)(2,1)} custom-call(bf16[6,128,256]{2,1,0:T(8,128)(2,1)S(1)} %collective-permute-done.9.parcel, bf16[6,128,256]{2,1,0:T(8,128)(2,1)S(1)} %get-tuple-element.81.block, bf16[32,128,256]{2,1,0:T(8,128)(2,1)} %get-tuple-element.82._), custom_call_target="tpu_custom_call", output_to_operand_aliasing={{}: (2, {})} | custom-call | tf_op jit(solution)/shard_map/place/pallas_call | solution.py:434
  (13 shorter events, 0.8 us)
Async XLA Ops:
  0.0 4.7 %collective-permute-start = (bf16[32,128,256]{2,1,0:T(8,128)(2,1)}, bf16[32,128,256]{2,1,0:T(8,128)(2,1)S(1)}, u32[]{:S(2)}, u32[]{:S(2)}) collective-permute-start(bf16[32,128,256]{2,1,0:T(8,128)(2,1)} %bitcast.10), channel_id=1, source_target_pairs={{0,4},{4,0},{8,12},{12,8},{16,20},{20,16},{24,28},{28,24},{1,5},{5... | collective-permute-start | bytes 6291464 | tf_op jit(solution)/shard_map/ppermute | solution.py:490
  6.0 13.6 %collective-permute-start.2 = (bf16[7,128,256]{2,1,0:T(8,128)(2,1)S(1)}, bf16[7,128,256]{2,1,0:T(8,128)(2,1)S(1)}, u32[]{:S(2)}, u32[]{:S(2)}) collective-permute-start(bf16[7,128,256]{2,1,0:T(8,128)(2,1)S(1)} %get-tuple-element.55.pair), channel_id=1, source_target_pairs={{0,8},{4,12},{8,0},{12,4},{16,24},{20,28},{1,9},{5,13},{9,1},{13,5... | collective-permute-start | bytes 1376264 | tf_op jit(solution)/shard_map/ppermute | solution.py:464
  7.3 3.0 %collective-permute-start.1 = (bf16[2,2,128,256]{3,2,1,0:T(8,128)(2,1)S(1)}, bf16[2,2,128,256]{3,2,1,0:T(8,128)(2,1)S(1)}, u32[]{:S(2)}, u32[]{:S(2)}) collective-permute-start(bf16[2,2,128,256]{3,2,1,0:T(8,128)(2,1)S(1)} %get-tuple-element.53), channel_id=1, source_target_pairs={{4,1},{5,2},{6,3},{1,4},{2,5},{3,6},{12,9},{13,10},{14,11},{9,12},... | collective-permute-start | bytes 786440 | tf_op jit(solution)/shard_map/ppermute | solution.py:505
  9.1 12.2 %collective-permute-start.3 = (bf16[5,128,256]{2,1,0:T(8,128)(2,1)S(1)}, bf16[5,128,256]{2,1,0:T(8,128)(2,1)S(1)}, u32[]{:S(2)}, u32[]{:S(2)}) collective-permute-start(bf16[5,128,256]{2,1,0:T(8,128)(2,1)S(1)} %get-tuple-element.57.pair), channel_id=1, source_target_pairs={{0,16},{4,20},{8,24},{12,28},{1,17},{5,21},{9,25},{13,29},{2,18},{... | collective-permute-start | bytes 983048 | tf_op jit(solution)/shard_map/ppermute | solution.py:464
  12.2 19.7 %copy-start = (bf16[3,3,256,256]{3,2,1,0:T(8,128)(2,1)S(1)}, bf16[3,3,256,256]{3,2,1,0:T(8,128)(2,1)}, u32[]{:S(2)}) copy-start(bf16[3,3,256,256]{3,2,1,0:T(8,128)(2,1)} %param.9) | copy-start | bytes 3538948
  12.2 13.3 %collective-permute-start.4 = (bf16[5,128,256]{2,1,0:T(8,128)(2,1)S(1)}, bf16[5,128,256]{2,1,0:T(8,128)(2,1)S(1)}, u32[]{:S(2)}, u32[]{:S(2)}) collective-permute-start(bf16[5,128,256]{2,1,0:T(8,128)(2,1)S(1)} %get-tuple-element.59.pair), channel_id=1, source_target_pairs={{0,8},{4,12},{8,0},{12,4},{16,24},{20,28},{1,9},{5,13},{9,1},{13,5... | collective-permute-start | bytes 983048 | tf_op jit(solution)/shard_map/ppermute | solution.py:464
  20.0 11.9 %collective-permute-start.5 = (bf16[7,128,256]{2,1,0:T(8,128)(2,1)S(1)}, bf16[7,128,256]{2,1,0:T(8,128)(2,1)S(1)}, u32[]{:S(2)}, u32[]{:S(2)}) collective-permute-start(bf16[7,128,256]{2,1,0:T(8,128)(2,1)S(1)} %get-tuple-element.61), channel_id=1, source_target_pairs={{0,16},{4,20},{8,24},{12,28},{1,17},{5,21},{9,25},{13,29},{2,18},{... | collective-permute-start | bytes 1376264 | tf_op jit(solution)/shard_map/ppermute | solution.py:479
  21.5 18.1 %collective-permute-start.6 = (bf16[5,128,256]{2,1,0:T(8,128)(2,1)S(1)}, bf16[5,128,256]{2,1,0:T(8,128)(2,1)S(1)}, u32[]{:S(2)}, u32[]{:S(2)}) collective-permute-start(bf16[5,128,256]{2,1,0:T(8,128)(2,1)S(1)} %get-tuple-element.64), channel_id=1, source_target_pairs={{0,8},{4,12},{16,24},{20,28},{24,16},{28,20},{1,9},{5,13},{17,25},... | collective-permute-start | bytes 983048 | tf_op jit(solution)/shard_map/ppermute | solution.py:479
  25.7 16.5 %collective-permute-start.7 = (bf16[5,128,256]{2,1,0:T(8,128)(2,1)S(1)}, bf16[5,128,256]{2,1,0:T(8,128)(2,1)S(1)}, u32[]{:S(2)}, u32[]{:S(2)}) collective-permute-start(bf16[5,128,256]{2,1,0:T(8,128)(2,1)S(1)} %get-tuple-element.70), channel_id=1, source_target_pairs={{0,16},{4,20},{8,24},{12,28},{1,17},{5,21},{9,25},{13,29},{2,18},{... | collective-permute-start | bytes 983048 | tf_op jit(solution)/shard_map/ppermute | solution.py:479
  34.0 8.2 %collective-permute-start.8 = (bf16[2,128,256]{2,1,0:T(8,128)(2,1)S(1)}, bf16[2,128,256]{2,1,0:T(8,128)(2,1)S(1)}, u32[]{:S(2)}, u32[]{:S(2)}) collective-permute-start(bf16[2,128,256]{2,1,0:T(8,128)(2,1)S(1)} %get-tuple-element.75), channel_id=1, source_target_pairs={{0,4},{4,0},{8,12},{12,8},{16,20},{20,16},{24,28},{28,24},{1,5},{5... | collective-permute-start | bytes 393224 | tf_op jit(solution)/shard_map/ppermute | solution.py:517
  42.1 2.2 %collective-permute-start.10 = (bf16[10,128,256]{2,1,0:T(8,128)(2,1)S(1)}, bf16[10,128,256]{2,1,0:T(8,128)(2,1)S(1)}, u32[]{:S(2)}, u32[]{:S(2)}) collective-permute-start(bf16[10,128,256]{2,1,0:T(8,128)(2,1)S(1)} %get-tuple-element.79), channel_id=1, source_target_pairs={{0,4},{4,0},{8,12},{12,8},{16,20},{20,16},{24,28},{28,24},{1,5},{5... | collective-permute-start | bytes 1966088 | tf_op jit(solution)/shard_map/ppermute | solution.py:522
  43.5 2.8 %collective-permute-start.9 = (bf16[6,128,256]{2,1,0:T(8,128)(2,1)S(1)}, bf16[6,128,256]{2,1,0:T(8,128)(2,1)S(1)}, u32[]{:S(2)}, u32[]{:S(2)}) collective-permute-start(bf16[6,128,256]{2,1,0:T(8,128)(2,1)S(1)} %get-tuple-element.76), channel_id=1, source_target_pairs={{0,4},{4,0},{8,12},{12,8},{16,20},{20,16},{24,28},{28,24},{1,5},{5... | collective-permute-start | bytes 1179656 | tf_op jit(solution)/shard_map/ppermute | solution.py:529

commit v7 on v6

--- a/solution.py
+++ b/solution.py
@@ -289,7 +289,7 @@
     take = lambda k: [refs.pop(0) for _ in range(k)]
     tab, weights, r1, r2, own, oth, feed_own, feed_oth = take(8)
     kept = take(1)[0] if not seam else None
-    near, far = take(2) if closing else (None, None)
+    rim = take(1)[0] if closing else None
     parts = take(n_parts)
     blocks = take(len(blocks_at))
     take(1 if more else 0)
@@ -323,21 +323,17 @@
         s1 = cmul(lam, s0) + jnp.where(first_core, f_oth, f_own)
         return jnp.where(first_core, s1, s0), jnp.where(first_core, s0, s1)
 
-    def emit(f, first_wide, size, depth, place, span):
+    def emit(f, first_wide, size, depth, span):
         frame, dst = ((oth, parcel), (own, block))[f]
         mixed = conv_block(wide.at[f], weights, first_wide, size, order).reshape(size, w, c)
         act = 0.5 * mixed * (1.0 + lax.erf(mixed * np.float32(0.5**0.5)))
         for r in range(size):
             row = jnp.where(core == 1, rows - 1 - depth - r, depth + r)
-            to = jnp.where(first_core, place + r, span - 1 - place - r) if span else place + r
+            to = jnp.where(first_core, first_wide + r, span - 1 - first_wide - r)
             dst[to] = (frame[row].astype(F32) + act[r]).astype(BF16)
 
-    if closing:
-        top = n_out + 2
-        for f in which:
-            for k, z in enumerate((near[f, 0], near[f, 1], far[1 - f])):
-                wide[f, top + k] = widen(z.astype(F32))
-            emit(f, top, 1, rows // 2 - 1, (parcel if f == 0 else block).shape[0] - 1, 0)
+    if closing and 0 in which:
+        parcel[parcel.shape[0] - 1] = rim[0]
     ready = 0
     for s in range(0, n_out, step):
         size = min(step, n_out - s)
@@ -357,7 +353,7 @@
                 wide[f, ready] = widen(pair[f])
             ready += 1
         for f in which:
-            emit(f, s, size, begin + s, s, (parcel if f == 0 else block).shape[0] - (1 if closing else 0))
+            emit(f, s, size, begin + s, parcel.shape[0] - (1 if closing else 0) if f == 0 else n_out)
     for copy in copies:
         copy.wait()
 
@@ -387,9 +383,9 @@
         n_parcel = n_out + extra + sum(part.shape[0] for part in parts)
         shapes, out_specs = shapes + [jax.ShapeDtypeStruct((n_parcel, w, c), BF16)], out_specs + [VMEM]
     if 1 in which:
-        shapes = shapes + [jax.ShapeDtypeStruct((n_out + extra, w, c), BF16)]
+        shapes = shapes + [jax.ShapeDtypeStruct((n_out, w, c), BF16)]
         out_specs = out_specs + [VMEM]
-    scratch = [pltpu.VMEM((2, n_out + (5 if closing else 2), w, 3 * c), BF16)]
+    scratch = [pltpu.VMEM((2, n_out + 2, w, 3 * c), BF16)]
     if blocks:
         scratch += [pltpu.SemaphoreType.DMA((len(blocks),))]
         if result is not None:
@@ -418,29 +414,59 @@
     )(*args)
 
 
-def place_kernel(depth, parcel, block, _, result, sem):
+def rim_kernel(tab, weights, near, far, own, oth, rim, tab_next, wide):
+    core = my_core()
+    order = [jnp.where(core == 0, d, 2 - d) for d in range(3)]
+    tab_next[...] = tab[...]
+    depth = own.shape[0] // 2 - 1
+    row = jnp.where(core == 1, own.shape[0] - 1 - depth, depth)
+    for f, frame in enumerate((oth, own)):
+        for k, z in enumerate((near[f, 0], near[f, 1], far[1 - f])):
+            wide[f, k] = widen(z.astype(F32))
+        mixed = conv_block(wide.at[f], weights, 0, 1, order)
+        act = 0.5 * mixed * (1.0 + lax.erf(mixed * np.float32(0.5**0.5)))
+        rim[f] = (frame[row].astype(F32) + act).astype(BF16)
+
+
+def rim_rows(tab, weights, near, far, own, oth):
+    w, c = own.shape[1:]
+    return pl.pallas_call(
+        rim_kernel,
+        out_shape=[jax.ShapeDtypeStruct((2, w, c), BF16), jax.ShapeDtypeStruct(tab.shape, F32)],
+        in_specs=[VMEM] * 6,
+        out_specs=[VMEM] * 2,
+        scratch_shapes=[pltpu.VMEM((2, 3, w, 3 * c), BF16)],
+        compiler_params=PARAMS,
+        cost_estimate=SHORT,
+        name="rim",
+    )(tab, weights, near, far, own, oth)
+
+
+def place_kernel(depth, parcel, block, rim, _, result, sem):
     core = my_core()
     inner = result.shape[0] // 2 - 1
-    copies = []
-    for k, (ref, side) in enumerate(((parcel, 1 - core), (block, core))):
-        n = ref.shape[0] - 1
-        copies.append(start_rows(ref.at[pl.ds(0, n)], result, side, depth, sem.at[2 * k]))
-        copies.append(start_rows(ref.at[pl.ds(n, 1)], result, side, inner, sem.at[2 * k + 1]))
+    n = parcel.shape[0] - 1
+    copies = [
+        start_rows(parcel.at[pl.ds(0, n)], result, 1 - core, depth, sem.at[0]),
+        start_rows(parcel.at[pl.ds(n, 1)], result, 1 - core, inner, sem.at[1]),
+        start_rows(block, result, core, depth, sem.at[2]),
+        start_rows(rim.at[pl.ds(1, 1)], result, core, inner, sem.at[3]),
+    ]
     for copy in copies:
         copy.wait()
 
 
-def place(parcel, block, depth, result):
+def place(parcel, block, rim, depth, result):
     return pl.pallas_call(
         functools.partial(place_kernel, depth),
         out_shape=jax.ShapeDtypeStruct(result.shape, result.dtype),
-        in_specs=[VMEM, VMEM, HBM],
+        in_specs=[VMEM, VMEM, VMEM, HBM],
         out_specs=HBM,
-        input_output_aliases={2: 0},
+        input_output_aliases={3: 0},
         scratch_shapes=[pltpu.SemaphoreType.DMA((4,))],
         compiler_params=PARAMS,
         name="place",
-    )(parcel, block, result)
+    )(parcel, block, rim, result)
 
 
 ALONG_X = [(0, 1), (1, 0), (2, 3)], [(0, 2), (1, 3)]
@@ -520,13 +546,14 @@
         tab, *args, (0, 1), kept=kept, parts=(parcel1,), blocks=(block1,), blocks_at=((lo1 + 1, 1),)
     )
     early = lax.ppermute(parcel2, "tm", swap)
+    rim, tab = rim_rows(tab, w_out, near, far, frame, oth)
     args = (w_out, (mine3, theirs3), (got3, also3), frame, oth, lo3, hi3, lo3 + 1, hi3 + 1, 0, 2)
-    parcel, tab = output(tab, *args, (0,), kept=kept, seam=(near, far))
+    parcel, tab = output(tab, *args, (0,), kept=kept, seam=(rim,))
     block3, result = output(
-        tab, *args, (1,), kept=kept, seam=(near, far), blocks=(block2, early), blocks_at=((lo2 + 1, 1), (lo2 + 1, 0)),
+        tab, *args, (1,), kept=kept, seam=(rim,), blocks=(block2, early), blocks_at=((lo2 + 1, 1), (lo2 + 1, 0)),
         result=result,
     )
-    return place(lax.ppermute(parcel, "tm", swap), block3, lo3 + 1, result)[None]
+    return place(lax.ppermute(parcel, "tm", swap), block3, rim, lo3 + 1, result)[None]
 
 
 def solution(mesh):

time: 47.7 us -> 47.8 us (level)
    pallas_call x0 -> x1, Pallas kernels: none -> 0.52 us  [rim_rows(): pl.pallas_call(rim_kernel, out_shape=[jax.ShapeDtypeStruct((2, w, c), BF1...]
  transfers between devices with their start and end apart: 11 -> 11, of which waited for: 5 -> 4; matrix products, arithmetic and copies ran while one was open for 0% -> 0% of each run, Pallas kernels for 32% -> 33%
where the time goes in v7:
time: 47.8 us; the launch traced here: 47.6 us
  Pallas kernels  17.8 us (37%)
  starting transfers between devices  16.2 us (34%)
  waiting for transfers between devices  13.2 us (28%)
    ppermute x3, waiting for transfers between devices, first_stage(): lax.ppermute(pair, 'tm', both_cores((ALONG_X if slot == 0 else ALONG_Y)[0]))  8.15 us
    pallas_call x4, Pallas kernels, output(): pl.pallas_call(functools.partial(output_kernel, lo, hi, begin, end, slot,...  7.87 us
    ppermute x1, starting transfers between devices, on_device(): far = lax.ppermute(send, 'tm', swap)  5.51 us
    ppermute x3, waiting for transfers between devices, second_stage(): lax.ppermute(pay, 'tm', both_cores((ALONG_X if slot == 0 else ALONG_Y)[1]))  4.69 us
    ppermute x3, starting transfers between devices, second_stage(): lax.ppermute(pay, 'tm', both_cores((ALONG_X if slot == 0 else ALONG_Y)[1]))  4.69 us
    ppermute x3, starting transfers between devices, first_stage(): lax.ppermute(pair, 'tm', both_cores((ALONG_X if slot == 0 else ALONG_Y)[0]))  4.01 us
    pallas_call x1, Pallas kernels, lead(): pl.pallas_call(functools.partial(lead_kernel, entries, lo, mid, hi, step)...  3.64 us
    pallas_call x2, Pallas kernels, pair_up(): pl.pallas_call(functools.partial(pair_kernel, lo, hi, step), out_shape=[j...  2.37 us
  transfers between devices with their start and end apart: 11, of which 4 were waited for; matrix products, arithmetic and copies ran while one was open for 0% of the time, Pallas kernels for 33%

profile of v7, /device:TPU:31, one launch (start us, length us, event | category | flops | bytes accessed | tf_op | source)
XLA Modules:
  0.0 47.6 jit_solution(5002142943536699311)
XLA Ops:
  0.0 0.7 %collective-permute-start = (bf16[32,128,256]{2,1,0:T(8,128)(2,1)}, bf16[32,128,256]{2,1,0:T(8,128)(2,1)S(1)}, u32[]{:S(2)}, u32[]{:S(2)}) collective-permute-start(bf16[32,128,256]{2,1,0:T(8,128)(2,1)} %bitcast.11), channel_id=1, source_target_pairs={{0,4},{4,0},{8,12},{12,8},{16,20},{20,16},{24,28},{28,24},{1,5},{5... | collective-permute-start | bytes 6291464 | tf_op jit(solution)/shard_map/ppermute | solution.py:516
  0.7 3.6 %lead.1 = (f32[7,128,256]{2,1,0:T(8,128)S(1)}, f32[5,128,256]{2,1,0:T(8,128)S(1)}, bf16[32,128,256]{2,1,0:T(8,128)(2,1)S(1)}, bf16[3,768,256]{2,1,0:T(8,128)(2,1...) custom-call(bf16[32,128,256]{2,1,0:T(8,128)(2,1)} %bitcast.12, bf16[3,768,256]{2,1,0:T(8,128)(2,1)} %bitcast.13, ...), custom_call_target="tpu_custom_call" | custom-call | flops 1 | bytes 1 | tf_op jit(solution)/shard_map/lead/pallas_call | solution.py:132
  4.3 0.3 collective-permute-done.oth.refs_5_
  4.7 1.3 %pair.2 = (f32[7,128,256]{2,1,0:T(8,128)S(1)}, bf16[7,128,256]{2,1,0:T(8,128)(2,1)S(1)}, f32[32,128]{1,0:T(8,128)S(1)}) custom-call(bf16[32,128,256]{2,1,0:T(8,128)(2,1)S(1)} %collective-permute-done.oth.refs_5_, bf16[3,768,256]{2,1,0:T(8,128)(2,1)S(1)} %get-tuple-element.47.weights, f32[32,128]{1,0:T(8,128)S(1)} %get-tuple-element.49.tab, ...), custom_call_target="tpu_custom_call" | custom-call | flops 1 | bytes 1 | tf_op jit(solution)/shard_map/pair/pallas_call | solution.py:178
  6.0 1.3 %collective-permute-start.2 = (bf16[7,128,256]{2,1,0:T(8,128)(2,1)S(1)}, bf16[7,128,256]{2,1,0:T(8,128)(2,1)S(1)}, u32[]{:S(2)}, u32[]{:S(2)}) collective-permute-start(bf16[7,128,256]{2,1,0:T(8,128)(2,1)S(1)} %get-tuple-element.57.pair), channel_id=1, source_target_pairs={{0,8},{4,12},{8,0},{12,4},{16,24},{20,28},{1,9},{5,13},{9,1},{13,5... | collective-permute-start | bytes 1376264 | tf_op jit(solution)/shard_map/ppermute | solution.py:490
  7.3 0.7 %collective-permute-start.1 = (bf16[2,2,128,256]{3,2,1,0:T(8,128)(2,1)S(1)}, bf16[2,2,128,256]{3,2,1,0:T(8,128)(2,1)S(1)}, u32[]{:S(2)}, u32[]{:S(2)}) collective-permute-start(bf16[2,2,128,256]{3,2,1,0:T(8,128)(2,1)S(1)} %get-tuple-element.55), channel_id=1, source_target_pairs={{4,1},{5,2},{6,3},{1,4},{2,5},{3,6},{12,9},{13,10},{14,11},{9,12},... | collective-permute-start | bytes 786440 | tf_op jit(solution)/shard_map/ppermute | solution.py:531
  8.0 1.0 %pair.3 = (f32[5,128,256]{2,1,0:T(8,128)S(1)}, bf16[5,128,256]{2,1,0:T(8,128)(2,1)S(1)}, f32[32,128]{1,0:T(8,128)S(1)}) custom-call(bf16[32,128,256]{2,1,0:T(8,128)(2,1)S(1)} %collective-permute-done.oth.refs_5_, bf16[3,768,256]{2,1,0:T(8,128)(2,1)S(1)} %get-tuple-element.47.weights, f32[32,128]{1,0:T(8,128)S(1)} %get-tuple-element.52.tab, ...), custom_call_target="tpu_custom_call" | custom-call | flops 1 | bytes 1 | tf_op jit(solution)/shard_map/pair/pallas_call | solution.py:178
  9.1 1.3 %collective-permute-start.3 = (bf16[5,128,256]{2,1,0:T(8,128)(2,1)S(1)}, bf16[5,128,256]{2,1,0:T(8,128)(2,1)S(1)}, u32[]{:S(2)}, u32[]{:S(2)}) collective-permute-start(bf16[5,128,256]{2,1,0:T(8,128)(2,1)S(1)} %get-tuple-element.59.pair), channel_id=1, source_target_pairs={{0,16},{4,20},{8,24},{12,28},{1,17},{5,21},{9,25},{13,29},{2,18},{... | collective-permute-start | bytes 983048 | tf_op jit(solution)/shard_map/ppermute | solution.py:490
  10.4 1.8 %edge.1 = (f32[5,128,256]{2,1,0:T(8,128)S(1)}, f32[5,128,256]{2,1,0:T(8,128)S(1)}, bf16[5,128,256]{2,1,0:T(8,128)(2,1)S(1)}, f32[32,128]{1,0:T(8,128)S(1)}) custom-call(bf16[32,128,256]{2,1,0:T(8,128)(2,1)S(1)} %get-tuple-element.46.frame.refs_4_.own, bf16[32,128,256]{2,1,0:T(8,128)(2,1)S(1)} %collective-permute-done.oth.refs_5_, ...), custom_call_target="tpu_custom_call" | custom-call | flops 1 | bytes 1 | tf_op jit(solution)/shard_map/edge/pallas_call | solution.py:251
  12.2 1.4 %collective-permute-start.4 = (bf16[5,128,256]{2,1,0:T(8,128)(2,1)S(1)}, bf16[5,128,256]{2,1,0:T(8,128)(2,1)S(1)}, u32[]{:S(2)}, u32[]{:S(2)}) collective-permute-start(bf16[5,128,256]{2,1,0:T(8,128)(2,1)S(1)} %get-tuple-element.61.pair), channel_id=1, source_target_pairs={{0,8},{4,12},{8,0},{12,4},{16,24},{20,28},{1,9},{5,13},{9,1},{13,5... | collective-permute-start | bytes 983048 | tf_op jit(solution)/shard_map/ppermute | solution.py:490
  13.6 6.1 %collective-permute-done.2.got.refs_2_ = bf16[7,128,256]{2,1,0:T(8,128)(2,1)S(1)} collective-permute-done((bf16[7,128,256]{2,1,0:T(8,128)(2,1)S(1)}, bf16[7,128,256]{2,1,0:T(8,128)(2,1)S(1)}, u32[]{:S(2)}, u32[]{:S(2)}) %collective-permute-start.2) | collective-permute-done | bytes 458784 | tf_op jit(solution)/shard_map/ppermute | solution.py:490
  20.0 1.3 %collective-permute-start.5 = (bf16[7,128,256]{2,1,0:T(8,128)(2,1)S(1)}, bf16[7,128,256]{2,1,0:T(8,128)(2,1)S(1)}, u32[]{:S(2)}, u32[]{:S(2)}) collective-permute-start(bf16[7,128,256]{2,1,0:T(8,128)(2,1)S(1)} %get-tuple-element.63), channel_id=1, source_target_pairs={{0,16},{4,20},{8,24},{12,28},{1,17},{5,21},{9,25},{13,29},{2,18},{... | collective-permute-start | bytes 1376264 | tf_op jit(solution)/shard_map/ppermute | solution.py:505
  21.5 1.9 %collective-permute-start.6 = (bf16[5,128,256]{2,1,0:T(8,128)(2,1)S(1)}, bf16[5,128,256]{2,1,0:T(8,128)(2,1)S(1)}, u32[]{:S(2)}, u32[]{:S(2)}) collective-permute-start(bf16[5,128,256]{2,1,0:T(8,128)(2,1)S(1)} %get-tuple-element.66), channel_id=1, source_target_pairs={{0,8},{4,12},{16,24},{20,28},{24,16},{28,20},{1,9},{5,13},{17,25},... | collective-permute-start | bytes 983048 | tf_op jit(solution)/shard_map/ppermute | solution.py:505
  23.4 2.1 %collective-permute-done.4.got.refs_2_ = bf16[5,128,256]{2,1,0:T(8,128)(2,1)S(1)} collective-permute-done((bf16[5,128,256]{2,1,0:T(8,128)(2,1)S(1)}, bf16[5,128,256]{2,1,0:T(8,128)(2,1)S(1)}, u32[]{:S(2)}, u32[]{:S(2)}) %collective-permute-start.4) | collective-permute-done | bytes 327712 | tf_op jit(solution)/shard_map/ppermute | solution.py:490
  25.7 1.5 %collective-permute-start.8 = (bf16[5,128,256]{2,1,0:T(8,128)(2,1)S(1)}, bf16[5,128,256]{2,1,0:T(8,128)(2,1)S(1)}, u32[]{:S(2)}, u32[]{:S(2)}) collective-permute-start(bf16[5,128,256]{2,1,0:T(8,128)(2,1)S(1)} %get-tuple-element.75), channel_id=1, source_target_pairs={{0,16},{4,20},{8,24},{12,28},{1,17},{5,21},{9,25},{13,29},{2,18},{... | collective-permute-start | bytes 983048 | tf_op jit(solution)/shard_map/ppermute | solution.py:505
  27.2 4.7 %collective-permute-done.5.refs_3_ = bf16[7,128,256]{2,1,0:T(8,128)(2,1)S(1)} collective-permute-done((bf16[7,128,256]{2,1,0:T(8,128)(2,1)S(1)}, bf16[7,128,256]{2,1,0:T(8,128)(2,1)S(1)}, u32[]{:S(2)}, u32[]{:S(2)}) %collective-permute-start.5) | collective-permute-done | bytes 458784 | tf_op jit(solution)/shard_map/ppermute | solution.py:505
  31.9 2.2 %output.4 = (bf16[5,128,256]{2,1,0:T(8,128)(2,1)S(1)}, bf16[5,128,256]{2,1,0:T(8,128)(2,1)S(1)}, bf16[2,2,128,256]{3,2,1,0:T(8,128)(2,1)S(1)}, bf16[2,2,128,256]...) custom-call(f32[32,128]{1,0:T(8,128)S(1)} %get-tuple-element.62.refs_0_, ...), custom_call_target="tpu_custom_call" | custom-call | flops 1 | bytes 1 | tf_op jit(solution)/shard_map/output/pallas_call | solution.py:402
  34.0 5.5 %collective-permute-start.7 = (bf16[2,128,256]{2,1,0:T(8,128)(2,1)S(1)}, bf16[2,128,256]{2,1,0:T(8,128)(2,1)S(1)}, u32[]{:S(2)}, u32[]{:S(2)}) collective-permute-start(bf16[2,128,256]{2,1,0:T(8,128)(2,1)S(1)} %get-tuple-element.73), channel_id=1, source_target_pairs={{0,4},{4,0},{8,12},{12,8},{16,20},{20,16},{24,28},{28,24},{1,5},{5... | collective-permute-start | bytes 393224 | tf_op jit(solution)/shard_map/ppermute | solution.py:543
  39.5 2.6 %output.5 = (bf16[10,128,256]{2,1,0:T(8,128)(2,1)S(1)}, bf16[5,128,256]{2,1,0:T(8,128)(2,1)S(1)}, bf16[32,128,256]{2,1,0:T(8,128)(2,1)}, bf16[2,2,128,256]{3,2,1,0:T(8,128)(2,1)S(1)}, f32[32,128]{1,0:T(8,128)S(1)}) custom-call(f32[32,128]{1,0:T(8,128)S(1)} %get-tuple-element.65.refs_0_, bf16[3,768,256]{2,1,0:T(8,128)(2,1)S(1)} %bitcast.7, ...), custom_call_target="tpu_custom_call" | custom-call | flops 1 | bytes 1 | tf_op jit(solution)/shard_map/output/pallas_call | solution.py:402
  42.2 0.5 %rim.1 = (bf16[2,128,256]{2,1,0:T(8,128)(2,1)S(1)}, f32[32,128]{1,0:T(8,128)S(1)}) custom-call(f32[32,128]{1,0:T(8,128)S(1)} %get-tuple-element.71.tab, bf16[3,768,256]{2,1,0:T(8,128)(2,1)S(1)} %bitcast.8, bf16[2,2,128,256]{3,2,1,0:T(8,128)(2,1)S(1)} %get-tuple-element.72.near, bf16[2,128,256]{2,1,0:T(8,128)(2,1)S(1)} %collective-permute-done.7.far, ...), custom_call_target="tpu_custom_call" | custom-call | flops 1 | bytes 1 | tf_op jit(solution)/shard_map/rim/pallas_call | solution.py:433
  42.8 1.2 %output.6 = (bf16[6,128,256]{2,1,0:T(8,128)(2,1)S(1)}, f32[32,128]{1,0:T(8,128)S(1)}) custom-call(f32[32,128]{1,0:T(8,128)S(1)} %get-tuple-element.74.refs_0_, bf16[3,768,256]{2,1,0:T(8,128)(2,1)S(1)} %bitcast.9, bf16[5,128,256]{2,1,0:T(8,128)(2,1)S(1)} %collective-permute-done.4.got.refs_2_, bf16[5,128,256]{2,1,0:T(8,128)(2,1)S(1)} %collective-permute-done.8.refs_3_, ...), custom_call_target="tpu_custom_call" | custom-call | flops 4000000000 | bytes 1 | tf_op jit(solution)/shard_map/output/pallas_call | solution.py:402
  44.0 0.5 %collective-permute-start.9 = (bf16[6,128,256]{2,1,0:T(8,128)(2,1)S(1)}, bf16[6,128,256]{2,1,0:T(8,128)(2,1)S(1)}, u32[]{:S(2)}, u32[]{:S(2)}) collective-permute-start(bf16[6,128,256]{2,1,0:T(8,128)(2,1)S(1)} %get-tuple-element.80), channel_id=1, source_target_pairs={{0,4},{4,0},{8,12},{12,8},{16,20},{20,16},{24,28},{28,24},{1,5},{5... | collective-permute-start | bytes 1179656 | tf_op jit(solution)/shard_map/ppermute | solution.py:556
  44.5 1.9 %output.7 = (bf16[5,128,256]{2,1,0:T(8,128)(2,1)S(1)}, bf16[32,128,256]{2,1,0:T(8,128)(2,1)}) custom-call(f32[32,128]{1,0:T(8,128)S(1)} %get-tuple-element.81.refs_0_, bf16[3,768,256]{2,1,0:T(8,128)(2,1)S(1)} %bitcast.10, bf16[5,128,256]{2,1,0:T(8,128)(2,1)S(1)} %collective-permute-done.4.got.refs_2_, ...), custom_call_target="tpu_custom_call", output_to_operand_aliasing={{1}: (12, {})} | custom-call | flops 1 | bytes 1 | tf_op jit(solution)/shard_map/output/pallas_call | solution.py:402
  46.5 0.9 %place.1 = bf16[32,128,256]{2,1,0:T(8,128)(2,1)} custom-call(bf16[6,128,256]{2,1,0:T(8,128)(2,1)S(1)} %collective-permute-done.9.parcel, bf16[5,128,256]{2,1,0:T(8,128)(2,1)S(1)} %get-tuple-element.85.block, bf16[2,128,256]{2,1,0:T(8,128)(2,1)S(1)} %get-tuple-element.79.refs_9_.rim, ...), custom_call_target="tpu_custom_call", output_to_operand_aliasing={{}: (3, {})} | custom-call | tf_op jit(solution)/shard_map/place/pallas_call | solution.py:460
  (14 shorter events, 0.8 us)
Async XLA Ops:
  0.0 4.7 %collective-permute-start = (bf16[32,128,256]{2,1,0:T(8,128)(2,1)}, bf16[32,128,256]{2,1,0:T(8,128)(2,1)S(1)}, u32[]{:S(2)}, u32[]{:S(2)}) collective-permute-start(bf16[32,128,256]{2,1,0:T(8,128)(2,1)} %bitcast.11), channel_id=1, source_target_pairs={{0,4},{4,0},{8,12},{12,8},{16,20},{20,16},{24,28},{28,24},{1,5},{5... | collective-permute-start | bytes 6291464 | tf_op jit(solution)/shard_map/ppermute | solution.py:516
  6.0 13.6 %collective-permute-start.2 = (bf16[7,128,256]{2,1,0:T(8,128)(2,1)S(1)}, bf16[7,128,256]{2,1,0:T(8,128)(2,1)S(1)}, u32[]{:S(2)}, u32[]{:S(2)}) collective-permute-start(bf16[7,128,256]{2,1,0:T(8,128)(2,1)S(1)} %get-tuple-element.57.pair), channel_id=1, source_target_pairs={{0,8},{4,12},{8,0},{12,4},{16,24},{20,28},{1,9},{5,13},{9,1},{13,5... | collective-permute-start | bytes 1376264 | tf_op jit(solution)/shard_map/ppermute | solution.py:490
  7.3 3.0 %collective-permute-start.1 = (bf16[2,2,128,256]{3,2,1,0:T(8,128)(2,1)S(1)}, bf16[2,2,128,256]{3,2,1,0:T(8,128)(2,1)S(1)}, u32[]{:S(2)}, u32[]{:S(2)}) collective-permute-start(bf16[2,2,128,256]{3,2,1,0:T(8,128)(2,1)S(1)} %get-tuple-element.55), channel_id=1, source_target_pairs={{4,1},{5,2},{6,3},{1,4},{2,5},{3,6},{12,9},{13,10},{14,11},{9,12},... | collective-permute-start | bytes 786440 | tf_op jit(solution)/shard_map/ppermute | solution.py:531
  9.1 12.2 %collective-permute-start.3 = (bf16[5,128,256]{2,1,0:T(8,128)(2,1)S(1)}, bf16[5,128,256]{2,1,0:T(8,128)(2,1)S(1)}, u32[]{:S(2)}, u32[]{:S(2)}) collective-permute-start(bf16[5,128,256]{2,1,0:T(8,128)(2,1)S(1)} %get-tuple-element.59.pair), channel_id=1, source_target_pairs={{0,16},{4,20},{8,24},{12,28},{1,17},{5,21},{9,25},{13,29},{2,18},{... | collective-permute-start | bytes 983048 | tf_op jit(solution)/shard_map/ppermute | solution.py:490
  12.2 19.7 %copy-start = (bf16[3,3,256,256]{3,2,1,0:T(8,128)(2,1)S(1)}, bf16[3,3,256,256]{3,2,1,0:T(8,128)(2,1)}, u32[]{:S(2)}) copy-start(bf16[3,3,256,256]{3,2,1,0:T(8,128)(2,1)} %param.9) | copy-start | bytes 3538948
  12.2 13.3 %collective-permute-start.4 = (bf16[5,128,256]{2,1,0:T(8,128)(2,1)S(1)}, bf16[5,128,256]{2,1,0:T(8,128)(2,1)S(1)}, u32[]{:S(2)}, u32[]{:S(2)}) collective-permute-start(bf16[5,128,256]{2,1,0:T(8,128)(2,1)S(1)} %get-tuple-element.61.pair), channel_id=1, source_target_pairs={{0,8},{4,12},{8,0},{12,4},{16,24},{20,28},{1,9},{5,13},{9,1},{13,5... | collective-permute-start | bytes 983048 | tf_op jit(solution)/shard_map/ppermute | solution.py:490
  20.0 11.9 %collective-permute-start.5 = (bf16[7,128,256]{2,1,0:T(8,128)(2,1)S(1)}, bf16[7,128,256]{2,1,0:T(8,128)(2,1)S(1)}, u32[]{:S(2)}, u32[]{:S(2)}) collective-permute-start(bf16[7,128,256]{2,1,0:T(8,128)(2,1)S(1)} %get-tuple-element.63), channel_id=1, source_target_pairs={{0,16},{4,20},{8,24},{12,28},{1,17},{5,21},{9,25},{13,29},{2,18},{... | collective-permute-start | bytes 1376264 | tf_op jit(solution)/shard_map/ppermute | solution.py:505
  21.5 18.1 %collective-permute-start.6 = (bf16[5,128,256]{2,1,0:T(8,128)(2,1)S(1)}, bf16[5,128,256]{2,1,0:T(8,128)(2,1)S(1)}, u32[]{:S(2)}, u32[]{:S(2)}) collective-permute-start(bf16[5,128,256]{2,1,0:T(8,128)(2,1)S(1)} %get-tuple-element.66), channel_id=1, source_target_pairs={{0,8},{4,12},{16,24},{20,28},{24,16},{28,20},{1,9},{5,13},{17,25},... | collective-permute-start | bytes 983048 | tf_op jit(solution)/shard_map/ppermute | solution.py:505
  25.7 17.1 %collective-permute-start.8 = (bf16[5,128,256]{2,1,0:T(8,128)(2,1)S(1)}, bf16[5,128,256]{2,1,0:T(8,128)(2,1)S(1)}, u32[]{:S(2)}, u32[]{:S(2)}) collective-permute-start(bf16[5,128,256]{2,1,0:T(8,128)(2,1)S(1)} %get-tuple-element.75), channel_id=1, source_target_pairs={{0,16},{4,20},{8,24},{12,28},{1,17},{5,21},{9,25},{13,29},{2,18},{... | collective-permute-start | bytes 983048 | tf_op jit(solution)/shard_map/ppermute | solution.py:505
  34.0 8.2 %collective-permute-start.7 = (bf16[2,128,256]{2,1,0:T(8,128)(2,1)S(1)}, bf16[2,128,256]{2,1,0:T(8,128)(2,1)S(1)}, u32[]{:S(2)}, u32[]{:S(2)}) collective-permute-start(bf16[2,128,256]{2,1,0:T(8,128)(2,1)S(1)} %get-tuple-element.73), channel_id=1, source_target_pairs={{0,4},{4,0},{8,12},{12,8},{16,20},{20,16},{24,28},{28,24},{1,5},{5... | collective-permute-start | bytes 393224 | tf_op jit(solution)/shard_map/ppermute | solution.py:543
  42.1 2.4 %collective-permute-start.10 = (bf16[10,128,256]{2,1,0:T(8,128)(2,1)S(1)}, bf16[10,128,256]{2,1,0:T(8,128)(2,1)S(1)}, u32[]{:S(2)}, u32[]{:S(2)}) collective-permute-start(bf16[10,128,256]{2,1,0:T(8,128)(2,1)S(1)} %get-tuple-element.83), channel_id=1, source_target_pairs={{0,4},{4,0},{8,12},{12,8},{16,20},{20,16},{24,28},{28,24},{1,5},{5... | collective-permute-start | bytes 1966088 | tf_op jit(solution)/shard_map/ppermute | solution.py:548
  44.0 2.5 %collective-permute-start.9 = (bf16[6,128,256]{2,1,0:T(8,128)(2,1)S(1)}, bf16[6,128,256]{2,1,0:T(8,128)(2,1)S(1)}, u32[]{:S(2)}, u32[]{:S(2)}) collective-permute-start(bf16[6,128,256]{2,1,0:T(8,128)(2,1)S(1)} %get-tuple-element.80), channel_id=1, source_target_pairs={{0,4},{4,0},{8,12},{12,8},{16,20},{20,16},{24,28},{28,24},{1,5},{5... | collective-permute-start | bytes 1179656 | tf_op jit(solution)/shard_map/ppermute | solution.py:556

commit v8 on v7

--- a/solution.py
+++ b/solution.py
@@ -442,7 +442,7 @@
     )(tab, weights, near, far, own, oth)
 
 
-def place_kernel(depth, parcel, block, rim, _, result, sem):
+def place_kernel(depth, above, parcel, block, rim, early, earlier, _, result, sem):
     core = my_core()
     inner = result.shape[0] // 2 - 1
     n = parcel.shape[0] - 1
@@ -451,22 +451,24 @@
         start_rows(parcel.at[pl.ds(n, 1)], result, 1 - core, inner, sem.at[1]),
         start_rows(block, result, core, depth, sem.at[2]),
         start_rows(rim.at[pl.ds(1, 1)], result, core, inner, sem.at[3]),
+        start_rows(early, result, 1 - core, above, sem.at[4]),
+        start_rows(earlier, result, core, above, sem.at[5]),
     ]
     for copy in copies:
         copy.wait()
 
 
-def place(parcel, block, rim, depth, result):
-    return pl.pallas_call(
-        functools.partial(place_kernel, depth),
+def place(parcel, block, rim, early, earlier, depth, above, result):
+    return pl.pallas_call(
+        functools.partial(place_kernel, depth, above),
         out_shape=jax.ShapeDtypeStruct(result.shape, result.dtype),
-        in_specs=[VMEM, VMEM, VMEM, HBM],
+        in_specs=[VMEM] * 5 + [HBM],
         out_specs=HBM,
-        input_output_aliases={3: 0},
-        scratch_shapes=[pltpu.SemaphoreType.DMA((4,))],
+        input_output_aliases={5: 0},
+        scratch_shapes=[pltpu.SemaphoreType.DMA((6,))],
         compiler_params=PARAMS,
         name="place",
-    )(parcel, block, rim, result)
+    )(parcel, block, rim, early, earlier, result)
 
 
 ALONG_X = [(0, 1), (1, 0), (2, 3)], [(0, 2), (1, 3)]
@@ -549,11 +551,8 @@
     rim, tab = rim_rows(tab, w_out, near, far, frame, oth)
     args = (w_out, (mine3, theirs3), (got3, also3), frame, oth, lo3, hi3, lo3 + 1, hi3 + 1, 0, 2)
     parcel, tab = output(tab, *args, (0,), kept=kept, seam=(rim,))
-    block3, result = output(
-        tab, *args, (1,), kept=kept, seam=(rim,), blocks=(block2, early), blocks_at=((lo2 + 1, 1), (lo2 + 1, 0)),
-        result=result,
-    )
-    return place(lax.ppermute(parcel, "tm", swap), block3, rim, lo3 + 1, result)[None]
+    (block3,) = output(tab, *args, (1,), kept=kept, seam=(rim,))
+    return place(lax.ppermute(parcel, "tm", swap), block3, rim, early, block2, lo3 + 1, lo2 + 1, result)[None]
 
 
 def solution(mesh):

time: 47.8 us -> 47.6 us (level)
    pallas_call x4, Pallas kernels: 7.87 us -> 7.11 us  [output(): pl.pallas_call(functools.partial(output_kernel, lo, hi, begin, end, slot,...]
  transfers between devices with their start and end apart: 11 -> 11, of which waited for: 4 -> 5; matrix products, arithmetic and copies ran while one was open for 0% -> 0% of each run, Pallas kernels for 33% -> 31%
where the time goes in v8:
time: 47.6 us; the launch traced here: 47.3 us
  Pallas kernels  17.4 us (37%)
  starting transfers between devices  16.2 us (34%)
  waiting for transfers between devices  13.4 us (28%)
    ppermute x3, waiting for transfers between devices, first_stage(): lax.ppermute(pair, 'tm', both_cores((ALONG_X if slot == 0 else ALONG_Y)[0]))  8.15 us
    pallas_call x4, Pallas kernels, output(): pl.pallas_call(functools.partial(output_kernel, lo, hi, begin, end, slot,...  7.11 us
    ppermute x1, starting transfers between devices, on_device(): far = lax.ppermute(send, 'tm', swap)  5.51 us
    ppermute x3, waiting for transfers between devices, second_stage(): lax.ppermute(pay, 'tm', both_cores((ALONG_X if slot == 0 else ALONG_Y)[1]))  4.69 us
    ppermute x3, starting transfers between devices, second_stage(): lax.ppermute(pay, 'tm', both_cores((ALONG_X if slot == 0 else ALONG_Y)[1]))  4.69 us
    ppermute x3, starting transfers between devices, first_stage(): lax.ppermute(pair, 'tm', both_cores((ALONG_X if slot == 0 else ALONG_Y)[0]))  4.01 us
    pallas_call x1, Pallas kernels, lead(): pl.pallas_call(functools.partial(lead_kernel, entries, lo, mid, hi, step)...  3.64 us
    pallas_call x2, Pallas kernels, pair_up(): pl.pallas_call(functools.partial(pair_kernel, lo, hi, step), out_shape=[j...  2.37 us
  transfers between devices with their start and end apart: 11, of which 5 were waited for; matrix products, arithmetic and copies ran while one was open for 0% of the time, Pallas kernels for 31%

profile of v8, /device:TPU:31, one launch (start us, length us, event | category | flops | bytes accessed | tf_op | source)
XLA Modules:
  0.0 47.3 jit_solution(1141669375231007988)
XLA Ops:
  0.0 0.7 %collective-permute-start = (bf16[32,128,256]{2,1,0:T(8,128)(2,1)}, bf16[32,128,256]{2,1,0:T(8,128)(2,1)S(1)}, u32[]{:S(2)}, u32[]{:S(2)}) collective-permute-start(bf16[32,128,256]{2,1,0:T(8,128)(2,1)} %bitcast.11), channel_id=1, source_target_pairs={{0,4},{4,0},{8,12},{12,8},{16,20},{20,16},{24,28},{28,24},{1,5},{5... | collective-permute-start | bytes 6291464 | tf_op jit(solution)/shard_map/ppermute | solution.py:518
  0.7 3.6 %lead.1 = (f32[7,128,256]{2,1,0:T(8,128)S(1)}, f32[5,128,256]{2,1,0:T(8,128)S(1)}, bf16[32,128,256]{2,1,0:T(8,128)(2,1)S(1)}, bf16[3,768,256]{2,1,0:T(8,128)(2,1...) custom-call(bf16[32,128,256]{2,1,0:T(8,128)(2,1)} %bitcast.12, bf16[3,768,256]{2,1,0:T(8,128)(2,1)} %bitcast.13, ...), custom_call_target="tpu_custom_call" | custom-call | flops 1 | bytes 1 | tf_op jit(solution)/shard_map/lead/pallas_call | solution.py:132
  4.3 0.3 collective-permute-done.oth.refs_5_
  4.7 1.3 %pair.2 = (f32[7,128,256]{2,1,0:T(8,128)S(1)}, bf16[7,128,256]{2,1,0:T(8,128)(2,1)S(1)}, f32[32,128]{1,0:T(8,128)S(1)}) custom-call(bf16[32,128,256]{2,1,0:T(8,128)(2,1)S(1)} %collective-permute-done.oth.refs_5_, bf16[3,768,256]{2,1,0:T(8,128)(2,1)S(1)} %get-tuple-element.45.weights, f32[32,128]{1,0:T(8,128)S(1)} %get-tuple-element.47.tab, ...), custom_call_target="tpu_custom_call" | custom-call | flops 1 | bytes 1 | tf_op jit(solution)/shard_map/pair/pallas_call | solution.py:178
  6.0 1.3 %collective-permute-start.2 = (bf16[7,128,256]{2,1,0:T(8,128)(2,1)S(1)}, bf16[7,128,256]{2,1,0:T(8,128)(2,1)S(1)}, u32[]{:S(2)}, u32[]{:S(2)}) collective-permute-start(bf16[7,128,256]{2,1,0:T(8,128)(2,1)S(1)} %get-tuple-element.55.pair), channel_id=1, source_target_pairs={{0,8},{4,12},{8,0},{12,4},{16,24},{20,28},{1,9},{5,13},{9,1},{13,5... | collective-permute-start | bytes 1376264 | tf_op jit(solution)/shard_map/ppermute | solution.py:492
  7.3 0.7 %collective-permute-start.1 = (bf16[2,2,128,256]{3,2,1,0:T(8,128)(2,1)S(1)}, bf16[2,2,128,256]{3,2,1,0:T(8,128)(2,1)S(1)}, u32[]{:S(2)}, u32[]{:S(2)}) collective-permute-start(bf16[2,2,128,256]{3,2,1,0:T(8,128)(2,1)S(1)} %get-tuple-element.53), channel_id=1, source_target_pairs={{4,1},{5,2},{6,3},{1,4},{2,5},{3,6},{12,9},{13,10},{14,11},{9,12},... | collective-permute-start | bytes 786440 | tf_op jit(solution)/shard_map/ppermute | solution.py:533
  8.0 1.0 %pair.3 = (f32[5,128,256]{2,1,0:T(8,128)S(1)}, bf16[5,128,256]{2,1,0:T(8,128)(2,1)S(1)}, f32[32,128]{1,0:T(8,128)S(1)}) custom-call(bf16[32,128,256]{2,1,0:T(8,128)(2,1)S(1)} %collective-permute-done.oth.refs_5_, bf16[3,768,256]{2,1,0:T(8,128)(2,1)S(1)} %get-tuple-element.45.weights, f32[32,128]{1,0:T(8,128)S(1)} %get-tuple-element.50.tab, ...), custom_call_target="tpu_custom_call" | custom-call | flops 1 | bytes 1 | tf_op jit(solution)/shard_map/pair/pallas_call | solution.py:178
  9.1 1.3 %collective-permute-start.3 = (bf16[5,128,256]{2,1,0:T(8,128)(2,1)S(1)}, bf16[5,128,256]{2,1,0:T(8,128)(2,1)S(1)}, u32[]{:S(2)}, u32[]{:S(2)}) collective-permute-start(bf16[5,128,256]{2,1,0:T(8,128)(2,1)S(1)} %get-tuple-element.57.pair), channel_id=1, source_target_pairs={{0,16},{4,20},{8,24},{12,28},{1,17},{5,21},{9,25},{13,29},{2,18},{... | collective-permute-start | bytes 983048 | tf_op jit(solution)/shard_map/ppermute | solution.py:492
  10.4 1.8 %edge.1 = (f32[5,128,256]{2,1,0:T(8,128)S(1)}, f32[5,128,256]{2,1,0:T(8,128)S(1)}, bf16[5,128,256]{2,1,0:T(8,128)(2,1)S(1)}, f32[32,128]{1,0:T(8,128)S(1)}) custom-call(bf16[32,128,256]{2,1,0:T(8,128)(2,1)S(1)} %get-tuple-element.44.frame.refs_4_.own, bf16[32,128,256]{2,1,0:T(8,128)(2,1)S(1)} %collective-permute-done.oth.refs_5_, ...), custom_call_target="tpu_custom_call" | custom-call | flops 1 | bytes 1 | tf_op jit(solution)/shard_map/edge/pallas_call | solution.py:251
  12.2 1.4 %collective-permute-start.4 = (bf16[5,128,256]{2,1,0:T(8,128)(2,1)S(1)}, bf16[5,128,256]{2,1,0:T(8,128)(2,1)S(1)}, u32[]{:S(2)}, u32[]{:S(2)}) collective-permute-start(bf16[5,128,256]{2,1,0:T(8,128)(2,1)S(1)} %get-tuple-element.59.pair), channel_id=1, source_target_pairs={{0,8},{4,12},{8,0},{12,4},{16,24},{20,28},{1,9},{5,13},{9,1},{13,5... | collective-permute-start | bytes 983048 | tf_op jit(solution)/shard_map/ppermute | solution.py:492
  13.6 6.1 %collective-permute-done.2.got.refs_2_ = bf16[7,128,256]{2,1,0:T(8,128)(2,1)S(1)} collective-permute-done((bf16[7,128,256]{2,1,0:T(8,128)(2,1)S(1)}, bf16[7,128,256]{2,1,0:T(8,128)(2,1)S(1)}, u32[]{:S(2)}, u32[]{:S(2)}) %collective-permute-start.2) | collective-permute-done | bytes 458784 | tf_op jit(solution)/shard_map/ppermute | solution.py:492
  20.0 1.3 %collective-permute-start.5 = (bf16[7,128,256]{2,1,0:T(8,128)(2,1)S(1)}, bf16[7,128,256]{2,1,0:T(8,128)(2,1)S(1)}, u32[]{:S(2)}, u32[]{:S(2)}) collective-permute-start(bf16[7,128,256]{2,1,0:T(8,128)(2,1)S(1)} %get-tuple-element.61), channel_id=1, source_target_pairs={{0,16},{4,20},{8,24},{12,28},{1,17},{5,21},{9,25},{13,29},{2,18},{... | collective-permute-start | bytes 1376264 | tf_op jit(solution)/shard_map/ppermute | solution.py:507
  21.5 1.9 %collective-permute-start.6 = (bf16[5,128,256]{2,1,0:T(8,128)(2,1)S(1)}, bf16[5,128,256]{2,1,0:T(8,128)(2,1)S(1)}, u32[]{:S(2)}, u32[]{:S(2)}) collective-permute-start(bf16[5,128,256]{2,1,0:T(8,128)(2,1)S(1)} %get-tuple-element.64), channel_id=1, source_target_pairs={{0,8},{4,12},{16,24},{20,28},{24,16},{28,20},{1,9},{5,13},{17,25},... | collective-permute-start | bytes 983048 | tf_op jit(solution)/shard_map/ppermute | solution.py:507
  23.4 2.1 %collective-permute-done.4.got.refs_2_ = bf16[5,128,256]{2,1,0:T(8,128)(2,1)S(1)} collective-permute-done((bf16[5,128,256]{2,1,0:T(8,128)(2,1)S(1)}, bf16[5,128,256]{2,1,0:T(8,128)(2,1)S(1)}, u32[]{:S(2)}, u32[]{:S(2)}) %collective-permute-start.4) | collective-permute-done | bytes 327712 | tf_op jit(solution)/shard_map/ppermute | solution.py:492
  25.7 1.5 %collective-permute-start.8 = (bf16[5,128,256]{2,1,0:T(8,128)(2,1)S(1)}, bf16[5,128,256]{2,1,0:T(8,128)(2,1)S(1)}, u32[]{:S(2)}, u32[]{:S(2)}) collective-permute-start(bf16[5,128,256]{2,1,0:T(8,128)(2,1)S(1)} %get-tuple-element.73), channel_id=1, source_target_pairs={{0,16},{4,20},{8,24},{12,28},{1,17},{5,21},{9,25},{13,29},{2,18},{... | collective-permute-start | bytes 983048 | tf_op jit(solution)/shard_map/ppermute | solution.py:507
  27.2 4.7 %collective-permute-done.5.refs_3_ = bf16[7,128,256]{2,1,0:T(8,128)(2,1)S(1)} collective-permute-done((bf16[7,128,256]{2,1,0:T(8,128)(2,1)S(1)}, bf16[7,128,256]{2,1,0:T(8,128)(2,1)S(1)}, u32[]{:S(2)}, u32[]{:S(2)}) %collective-permute-start.5) | collective-permute-done | bytes 458784 | tf_op jit(solution)/shard_map/ppermute | solution.py:507
  31.9 2.2 %output.4 = (bf16[5,128,256]{2,1,0:T(8,128)(2,1)S(1)}, bf16[5,128,256]{2,1,0:T(8,128)(2,1)S(1)}, bf16[2,2,128,256]{3,2,1,0:T(8,128)(2,1)S(1)}, bf16[2,2,128,256]...) custom-call(f32[32,128]{1,0:T(8,128)S(1)} %get-tuple-element.60.refs_0_, ...), custom_call_target="tpu_custom_call" | custom-call | flops 1 | bytes 1 | tf_op jit(solution)/shard_map/output/pallas_call | solution.py:402
  34.0 5.5 %collective-permute-start.7 = (bf16[2,128,256]{2,1,0:T(8,128)(2,1)S(1)}, bf16[2,128,256]{2,1,0:T(8,128)(2,1)S(1)}, u32[]{:S(2)}, u32[]{:S(2)}) collective-permute-start(bf16[2,128,256]{2,1,0:T(8,128)(2,1)S(1)} %get-tuple-element.71), channel_id=1, source_target_pairs={{0,4},{4,0},{8,12},{12,8},{16,20},{20,16},{24,28},{28,24},{1,5},{5... | collective-permute-start | bytes 393224 | tf_op jit(solution)/shard_map/ppermute | solution.py:545
  39.5 2.6 %output.5 = (bf16[10,128,256]{2,1,0:T(8,128)(2,1)S(1)}, bf16[5,128,256]{2,1,0:T(8,128)(2,1)S(1)}, bf16[32,128,256]{2,1,0:T(8,128)(2,1)}, bf16[2,2,128,256]{3,2,1,0:T(8,128)(2,1)S(1)}, f32[32,128]{1,0:T(8,128)S(1)}) custom-call(f32[32,128]{1,0:T(8,128)S(1)} %get-tuple-element.63.refs_0_, bf16[3,768,256]{2,1,0:T(8,128)(2,1)S(1)} %bitcast.7, ...), custom_call_target="tpu_custom_call" | custom-call | flops 1 | bytes 1 | tf_op jit(solution)/shard_map/output/pallas_call | solution.py:402
  42.2 0.5 %rim.1 = (bf16[2,128,256]{2,1,0:T(8,128)(2,1)S(1)}, f32[32,128]{1,0:T(8,128)S(1)}) custom-call(f32[32,128]{1,0:T(8,128)S(1)} %get-tuple-element.69.tab, bf16[3,768,256]{2,1,0:T(8,128)(2,1)S(1)} %bitcast.8, bf16[2,2,128,256]{3,2,1,0:T(8,128)(2,1)S(1)} %get-tuple-element.70.near, bf16[2,128,256]{2,1,0:T(8,128)(2,1)S(1)} %collective-permute-done.7.far, ...), custom_call_target="tpu_custom_call" | custom-call | flops 1 | bytes 1 | tf_op jit(solution)/shard_map/rim/pallas_call | solution.py:433
  42.8 1.2 %output.6 = (bf16[6,128,256]{2,1,0:T(8,128)(2,1)S(1)}, f32[32,128]{1,0:T(8,128)S(1)}) custom-call(f32[32,128]{1,0:T(8,128)S(1)} %get-tuple-element.72.refs_0_, bf16[3,768,256]{2,1,0:T(8,128)(2,1)S(1)} %bitcast.9, bf16[5,128,256]{2,1,0:T(8,128)(2,1)S(1)} %collective-permute-done.4.got.refs_2_, bf16[5,128,256]{2,1,0:T(8,128)(2,1)S(1)} %collective-permute-done.8.refs_3_, ...), custom_call_target="tpu_custom_call" | custom-call | flops 4000000000 | bytes 1 | tf_op jit(solution)/shard_map/output/pallas_call | solution.py:402
  44.0 0.5 %collective-permute-start.9 = (bf16[6,128,256]{2,1,0:T(8,128)(2,1)S(1)}, bf16[6,128,256]{2,1,0:T(8,128)(2,1)S(1)}, u32[]{:S(2)}, u32[]{:S(2)}) collective-permute-start(bf16[6,128,256]{2,1,0:T(8,128)(2,1)S(1)} %get-tuple-element.78), channel_id=1, source_target_pairs={{0,4},{4,0},{8,12},{12,8},{16,20},{20,16},{24,28},{28,24},{1,5},{5... | collective-permute-start | bytes 1179656 | tf_op jit(solution)/shard_map/ppermute | solution.py:555
  44.5 1.2 %output.7.block = bf16[5,128,256]{2,1,0:T(8,128)(2,1)S(1)} custom-call(f32[32,128]{1,0:T(8,128)S(1)} %get-tuple-element.79.refs_0_, bf16[3,768,256]{2,1,0:T(8,128)(2,1)S(1)} %bitcast.10, bf16[5,128,256]{2,1,0:T(8,128)(2,1)S(1)} %collective-permute-done.4.got.refs_2_, bf16[5,128,256]{2,1,0:T(8,128)(2,1)S(1)} %collective-permute-done.8.refs_3_, ...), custom_call_target="tpu_custom_call" | custom-call | flops 1 | bytes 1 | tf_op jit(solution)/shard_map/output/pallas_call | solution.py:402
  45.9 1.2 %place.1 = bf16[32,128,256]{2,1,0:T(8,128)(2,1)} custom-call(bf16[6,128,256]{2,1,0:T(8,128)(2,1)S(1)} %collective-permute-done.9.parcel, bf16[5,128,256]{2,1,0:T(8,128)(2,1)S(1)} %output.7.block, bf16[2,128,256]{2,1,0:T(8,128)(2,1)S(1)} %get-tuple-element.77.refs_9_.rim, ...), custom_call_target="tpu_custom_call", output_to_operand_aliasing={{}: (5, {})} | custom-call | tf_op jit(solution)/shard_map/place/pallas_call | solution.py:462
  (14 shorter events, 1.0 us)
Async XLA Ops:
  0.0 4.7 %collective-permute-start = (bf16[32,128,256]{2,1,0:T(8,128)(2,1)}, bf16[32,128,256]{2,1,0:T(8,128)(2,1)S(1)}, u32[]{:S(2)}, u32[]{:S(2)}) collective-permute-start(bf16[32,128,256]{2,1,0:T(8,128)(2,1)} %bitcast.11), channel_id=1, source_target_pairs={{0,4},{4,0},{8,12},{12,8},{16,20},{20,16},{24,28},{28,24},{1,5},{5... | collective-permute-start | bytes 6291464 | tf_op jit(solution)/shard_map/ppermute | solution.py:518
  6.0 13.6 %collective-permute-start.2 = (bf16[7,128,256]{2,1,0:T(8,128)(2,1)S(1)}, bf16[7,128,256]{2,1,0:T(8,128)(2,1)S(1)}, u32[]{:S(2)}, u32[]{:S(2)}) collective-permute-start(bf16[7,128,256]{2,1,0:T(8,128)(2,1)S(1)} %get-tuple-element.55.pair), channel_id=1, source_target_pairs={{0,8},{4,12},{8,0},{12,4},{16,24},{20,28},{1,9},{5,13},{9,1},{13,5... | collective-permute-start | bytes 1376264 | tf_op jit(solution)/shard_map/ppermute | solution.py:492
  7.3 3.0 %collective-permute-start.1 = (bf16[2,2,128,256]{3,2,1,0:T(8,128)(2,1)S(1)}, bf16[2,2,128,256]{3,2,1,0:T(8,128)(2,1)S(1)}, u32[]{:S(2)}, u32[]{:S(2)}) collective-permute-start(bf16[2,2,128,256]{3,2,1,0:T(8,128)(2,1)S(1)} %get-tuple-element.53), channel_id=1, source_target_pairs={{4,1},{5,2},{6,3},{1,4},{2,5},{3,6},{12,9},{13,10},{14,11},{9,12},... | collective-permute-start | bytes 786440 | tf_op jit(solution)/shard_map/ppermute | solution.py:533
  9.1 12.2 %collective-permute-start.3 = (bf16[5,128,256]{2,1,0:T(8,128)(2,1)S(1)}, bf16[5,128,256]{2,1,0:T(8,128)(2,1)S(1)}, u32[]{:S(2)}, u32[]{:S(2)}) collective-permute-start(bf16[5,128,256]{2,1,0:T(8,128)(2,1)S(1)} %get-tuple-element.57.pair), channel_id=1, source_target_pairs={{0,16},{4,20},{8,24},{12,28},{1,17},{5,21},{9,25},{13,29},{2,18},{... | collective-permute-start | bytes 983048 | tf_op jit(solution)/shard_map/ppermute | solution.py:492
  12.2 19.7 %copy-start = (bf16[3,3,256,256]{3,2,1,0:T(8,128)(2,1)S(1)}, bf16[3,3,256,256]{3,2,1,0:T(8,128)(2,1)}, u32[]{:S(2)}) copy-start(bf16[3,3,256,256]{3,2,1,0:T(8,128)(2,1)} %param.9) | copy-start | bytes 3538948
  12.2 13.3 %collective-permute-start.4 = (bf16[5,128,256]{2,1,0:T(8,128)(2,1)S(1)}, bf16[5,128,256]{2,1,0:T(8,128)(2,1)S(1)}, u32[]{:S(2)}, u32[]{:S(2)}) collective-permute-start(bf16[5,128,256]{2,1,0:T(8,128)(2,1)S(1)} %get-tuple-element.59.pair), channel_id=1, source_target_pairs={{0,8},{4,12},{8,0},{12,4},{16,24},{20,28},{1,9},{5,13},{9,1},{13,5... | collective-permute-start | bytes 983048 | tf_op jit(solution)/shard_map/ppermute | solution.py:492
  20.0 11.9 %collective-permute-start.5 = (bf16[7,128,256]{2,1,0:T(8,128)(2,1)S(1)}, bf16[7,128,256]{2,1,0:T(8,128)(2,1)S(1)}, u32[]{:S(2)}, u32[]{:S(2)}) collective-permute-start(bf16[7,128,256]{2,1,0:T(8,128)(2,1)S(1)} %get-tuple-element.61), channel_id=1, source_target_pairs={{0,16},{4,20},{8,24},{12,28},{1,17},{5,21},{9,25},{13,29},{2,18},{... | collective-permute-start | bytes 1376264 | tf_op jit(solution)/shard_map/ppermute | solution.py:507
  21.5 18.1 %collective-permute-start.6 = (bf16[5,128,256]{2,1,0:T(8,128)(2,1)S(1)}, bf16[5,128,256]{2,1,0:T(8,128)(2,1)S(1)}, u32[]{:S(2)}, u32[]{:S(2)}) collective-permute-start(bf16[5,128,256]{2,1,0:T(8,128)(2,1)S(1)} %get-tuple-element.64), channel_id=1, source_target_pairs={{0,8},{4,12},{16,24},{20,28},{24,16},{28,20},{1,9},{5,13},{17,25},... | collective-permute-start | bytes 983048 | tf_op jit(solution)/shard_map/ppermute | solution.py:507
  25.7 17.1 %collective-permute-start.8 = (bf16[5,128,256]{2,1,0:T(8,128)(2,1)S(1)}, bf16[5,128,256]{2,1,0:T(8,128)(2,1)S(1)}, u32[]{:S(2)}, u32[]{:S(2)}) collective-permute-start(bf16[5,128,256]{2,1,0:T(8,128)(2,1)S(1)} %get-tuple-element.73), channel_id=1, source_target_pairs={{0,16},{4,20},{8,24},{12,28},{1,17},{5,21},{9,25},{13,29},{2,18},{... | collective-permute-start | bytes 983048 | tf_op jit(solution)/shard_map/ppermute | solution.py:507
  34.0 8.2 %collective-permute-start.7 = (bf16[2,128,256]{2,1,0:T(8,128)(2,1)S(1)}, bf16[2,128,256]{2,1,0:T(8,128)(2,1)S(1)}, u32[]{:S(2)}, u32[]{:S(2)}) collective-permute-start(bf16[2,128,256]{2,1,0:T(8,128)(2,1)S(1)} %get-tuple-element.71), channel_id=1, source_target_pairs={{0,4},{4,0},{8,12},{12,8},{16,20},{20,16},{24,28},{28,24},{1,5},{5... | collective-permute-start | bytes 393224 | tf_op jit(solution)/shard_map/ppermute | solution.py:545
  42.1 3.7 %collective-permute-start.10 = (bf16[10,128,256]{2,1,0:T(8,128)(2,1)S(1)}, bf16[10,128,256]{2,1,0:T(8,128)(2,1)S(1)}, u32[]{:S(2)}, u32[]{:S(2)}) collective-permute-start(bf16[10,128,256]{2,1,0:T(8,128)(2,1)S(1)} %get-tuple-element.80), channel_id=1, source_target_pairs={{0,4},{4,0},{8,12},{12,8},{16,20},{20,16},{24,28},{28,24},{1,5},{5... | collective-permute-start | bytes 1966088 | tf_op jit(solution)/shard_map/ppermute | solution.py:550
  44.0 1.9 %collective-permute-start.9 = (bf16[6,128,256]{2,1,0:T(8,128)(2,1)S(1)}, bf16[6,128,256]{2,1,0:T(8,128)(2,1)S(1)}, u32[]{:S(2)}, u32[]{:S(2)}) collective-permute-start(bf16[6,128,256]{2,1,0:T(8,128)(2,1)S(1)} %get-tuple-element.78), channel_id=1, source_target_pairs={{0,4},{4,0},{8,12},{12,8},{16,20},{20,16},{24,28},{28,24},{1,5},{5... | collective-permute-start | bytes 1179656 | tf_op jit(solution)/shard_map/ppermute | solution.py:555

commit v9 on v8

--- a/solution.py
+++ b/solution.py
@@ -442,7 +442,7 @@
     )(tab, weights, near, far, own, oth)
 
 
-def place_kernel(depth, above, parcel, block, rim, early, earlier, _, result, sem):
+def place_kernel(depth, above, parcel, block, rim, early, _, result, sem):
     core = my_core()
     inner = result.shape[0] // 2 - 1
     n = parcel.shape[0] - 1
@@ -452,23 +452,22 @@
         start_rows(block, result, core, depth, sem.at[2]),
         start_rows(rim.at[pl.ds(1, 1)], result, core, inner, sem.at[3]),
         start_rows(early, result, 1 - core, above, sem.at[4]),
-        start_rows(earlier, result, core, above, sem.at[5]),
     ]
     for copy in copies:
         copy.wait()
 
 
-def place(parcel, block, rim, early, earlier, depth, above, result):
+def place(parcel, block, rim, early, depth, above, result):
     return pl.pallas_call(
         functools.partial(place_kernel, depth, above),
         out_shape=jax.ShapeDtypeStruct(result.shape, result.dtype),
-        in_specs=[VMEM] * 5 + [HBM],
+        in_specs=[VMEM] * 4 + [HBM],
         out_specs=HBM,
-        input_output_aliases={5: 0},
-        scratch_shapes=[pltpu.SemaphoreType.DMA((6,))],
+        input_output_aliases={4: 0},
+        scratch_shapes=[pltpu.SemaphoreType.DMA((5,))],
         compiler_params=PARAMS,
         name="place",
-    )(parcel, block, rim, early, earlier, result)
+    )(parcel, block, rim, early, result)
 
 
 ALONG_X = [(0, 1), (1, 0), (2, 3)], [(0, 2), (1, 3)]
@@ -551,8 +550,10 @@
     rim, tab = rim_rows(tab, w_out, near, far, frame, oth)
     args = (w_out, (mine3, theirs3), (got3, also3), frame, oth, lo3, hi3, lo3 + 1, hi3 + 1, 0, 2)
     parcel, tab = output(tab, *args, (0,), kept=kept, seam=(rim,))
-    (block3,) = output(tab, *args, (1,), kept=kept, seam=(rim,))
-    return place(lax.ppermute(parcel, "tm", swap), block3, rim, early, block2, lo3 + 1, lo2 + 1, result)[None]
+    block3, result = output(
+        tab, *args, (1,), kept=kept, seam=(rim,), blocks=(block2,), blocks_at=((lo2 + 1, 1),), result=result
+    )
+    return place(lax.ppermute(parcel, "tm", swap), block3, rim, early, lo3 + 1, lo2 + 1, result)[None]
 
 
 def solution(mesh):

time: 47.6 us -> 47.8 us (level)
  transfers between devices with their start and end apart: 11 -> 11, of which waited for: 5 -> 4; matrix products, arithmetic and copies ran while one was open for 0% -> 0% of each run, Pallas kernels for 31% -> 32%
where the time goes in v9:
time: 47.8 us; the launch traced here: 47.5 us
  Pallas kernels  17.8 us (37%)
  starting transfers between devices  16.2 us (34%)
  waiting for transfers between devices  13.2 us (28%)
    ppermute x3, waiting for transfers between devices, first_stage(): lax.ppermute(pair, 'tm', both_cores((ALONG_X if slot == 0 else ALONG_Y)[0]))  8.15 us
    pallas_call x4, Pallas kernels, output(): pl.pallas_call(functools.partial(output_kernel, lo, hi, begin, end, slot,...  7.57 us
    ppermute x1, starting transfers between devices, on_device(): far = lax.ppermute(send, 'tm', swap)  5.51 us
    ppermute x3, waiting for transfers between devices, second_stage(): lax.ppermute(pay, 'tm', both_cores((ALONG_X if slot == 0 else ALONG_Y)[1]))  4.69 us
    ppermute x3, starting transfers between devices, second_stage(): lax.ppermute(pay, 'tm', both_cores((ALONG_X if slot == 0 else ALONG_Y)[1]))  4.69 us
    ppermute x3, starting transfers between devices, first_stage(): lax.ppermute(pair, 'tm', both_cores((ALONG_X if slot == 0 else ALONG_Y)[0]))  4.01 us
    pallas_call x1, Pallas kernels, lead(): pl.pallas_call(functools.partial(lead_kernel, entries, lo, mid, hi, step)...  3.64 us
    pallas_call x2, Pallas kernels, pair_up(): pl.pallas_call(functools.partial(pair_kernel, lo, hi, step), out_shape=[j...  2.37 us
  transfers between devices with their start and end apart: 11, of which 4 were waited for; matrix products, arithmetic and copies ran while one was open for 0% of the time, Pallas kernels for 32%

profile of v9, /device:TPU:31, one launch (start us, length us, event | category | flops | bytes accessed | tf_op | source)
XLA Modules:
  0.0 47.5 jit_solution(8071777769048408158)
XLA Ops:
  0.0 0.7 %collective-permute-start = (bf16[32,128,256]{2,1,0:T(8,128)(2,1)}, bf16[32,128,256]{2,1,0:T(8,128)(2,1)S(1)}, u32[]{:S(2)}, u32[]{:S(2)}) collective-permute-start(bf16[32,128,256]{2,1,0:T(8,128)(2,1)} %bitcast.11), channel_id=1, source_target_pairs={{0,4},{4,0},{8,12},{12,8},{16,20},{20,16},{24,28},{28,24},{1,5},{5... | collective-permute-start | bytes 6291464 | tf_op jit(solution)/shard_map/ppermute | solution.py:517
  0.7 3.6 %lead.1 = (f32[7,128,256]{2,1,0:T(8,128)S(1)}, f32[5,128,256]{2,1,0:T(8,128)S(1)}, bf16[32,128,256]{2,1,0:T(8,128)(2,1)S(1)}, bf16[3,768,256]{2,1,0:T(8,128)(2,1...) custom-call(bf16[32,128,256]{2,1,0:T(8,128)(2,1)} %bitcast.12, bf16[3,768,256]{2,1,0:T(8,128)(2,1)} %bitcast.13, ...), custom_call_target="tpu_custom_call" | custom-call | flops 1 | bytes 1 | tf_op jit(solution)/shard_map/lead/pallas_call | solution.py:132
  4.3 0.3 collective-permute-done.oth.refs_5_
  4.7 1.3 %pair.2 = (f32[7,128,256]{2,1,0:T(8,128)S(1)}, bf16[7,128,256]{2,1,0:T(8,128)(2,1)S(1)}, f32[32,128]{1,0:T(8,128)S(1)}) custom-call(bf16[32,128,256]{2,1,0:T(8,128)(2,1)S(1)} %collective-permute-done.oth.refs_5_, bf16[3,768,256]{2,1,0:T(8,128)(2,1)S(1)} %get-tuple-element.47.weights, f32[32,128]{1,0:T(8,128)S(1)} %get-tuple-element.49.tab, ...), custom_call_target="tpu_custom_call" | custom-call | flops 1 | bytes 1 | tf_op jit(solution)/shard_map/pair/pallas_call | solution.py:178
  6.0 1.3 %collective-permute-start.2 = (bf16[7,128,256]{2,1,0:T(8,128)(2,1)S(1)}, bf16[7,128,256]{2,1,0:T(8,128)(2,1)S(1)}, u32[]{:S(2)}, u32[]{:S(2)}) collective-permute-start(bf16[7,128,256]{2,1,0:T(8,128)(2,1)S(1)} %get-tuple-element.57.pair), channel_id=1, source_target_pairs={{0,8},{4,12},{8,0},{12,4},{16,24},{20,28},{1,9},{5,13},{9,1},{13,5... | collective-permute-start | bytes 1376264 | tf_op jit(solution)/shard_map/ppermute | solution.py:491
  7.3 0.7 %collective-permute-start.1 = (bf16[2,2,128,256]{3,2,1,0:T(8,128)(2,1)S(1)}, bf16[2,2,128,256]{3,2,1,0:T(8,128)(2,1)S(1)}, u32[]{:S(2)}, u32[]{:S(2)}) collective-permute-start(bf16[2,2,128,256]{3,2,1,0:T(8,128)(2,1)S(1)} %get-tuple-element.55), channel_id=1, source_target_pairs={{4,1},{5,2},{6,3},{1,4},{2,5},{3,6},{12,9},{13,10},{14,11},{9,12},... | collective-permute-start | bytes 786440 | tf_op jit(solution)/shard_map/ppermute | solution.py:532
  8.0 1.0 %pair.3 = (f32[5,128,256]{2,1,0:T(8,128)S(1)}, bf16[5,128,256]{2,1,0:T(8,128)(2,1)S(1)}, f32[32,128]{1,0:T(8,128)S(1)}) custom-call(bf16[32,128,256]{2,1,0:T(8,128)(2,1)S(1)} %collective-permute-done.oth.refs_5_, bf16[3,768,256]{2,1,0:T(8,128)(2,1)S(1)} %get-tuple-element.47.weights, f32[32,128]{1,0:T(8,128)S(1)} %get-tuple-element.52.tab, ...), custom_call_target="tpu_custom_call" | custom-call | flops 1 | bytes 1 | tf_op jit(solution)/shard_map/pair/pallas_call | solution.py:178
  9.1 1.3 %collective-permute-start.3 = (bf16[5,128,256]{2,1,0:T(8,128)(2,1)S(1)}, bf16[5,128,256]{2,1,0:T(8,128)(2,1)S(1)}, u32[]{:S(2)}, u32[]{:S(2)}) collective-permute-start(bf16[5,128,256]{2,1,0:T(8,128)(2,1)S(1)} %get-tuple-element.59.pair), channel_id=1, source_target_pairs={{0,16},{4,20},{8,24},{12,28},{1,17},{5,21},{9,25},{13,29},{2,18},{... | collective-permute-start | bytes 983048 | tf_op jit(solution)/shard_map/ppermute | solution.py:491
  10.4 1.8 %edge.1 = (f32[5,128,256]{2,1,0:T(8,128)S(1)}, f32[5,128,256]{2,1,0:T(8,128)S(1)}, bf16[5,128,256]{2,1,0:T(8,128)(2,1)S(1)}, f32[32,128]{1,0:T(8,128)S(1)}) custom-call(bf16[32,128,256]{2,1,0:T(8,128)(2,1)S(1)} %get-tuple-element.46.frame.refs_4_.own, bf16[32,128,256]{2,1,0:T(8,128)(2,1)S(1)} %collective-permute-done.oth.refs_5_, ...), custom_call_target="tpu_custom_call" | custom-call | flops 1 | bytes 1 | tf_op jit(solution)/shard_map/edge/pallas_call | solution.py:251
  12.2 1.4 %collective-permute-start.4 = (bf16[5,128,256]{2,1,0:T(8,128)(2,1)S(1)}, bf16[5,128,256]{2,1,0:T(8,128)(2,1)S(1)}, u32[]{:S(2)}, u32[]{:S(2)}) collective-permute-start(bf16[5,128,256]{2,1,0:T(8,128)(2,1)S(1)} %get-tuple-element.61.pair), channel_id=1, source_target_pairs={{0,8},{4,12},{8,0},{12,4},{16,24},{20,28},{1,9},{5,13},{9,1},{13,5... | collective-permute-start | bytes 983048 | tf_op jit(solution)/shard_map/ppermute | solution.py:491
  13.6 6.1 %collective-permute-done.2.got.refs_2_ = bf16[7,128,256]{2,1,0:T(8,128)(2,1)S(1)} collective-permute-done((bf16[7,128,256]{2,1,0:T(8,128)(2,1)S(1)}, bf16[7,128,256]{2,1,0:T(8,128)(2,1)S(1)}, u32[]{:S(2)}, u32[]{:S(2)}) %collective-permute-start.2) | collective-permute-done | bytes 458784 | tf_op jit(solution)/shard_map/ppermute | solution.py:491
  20.0 1.3 %collective-permute-start.5 = (bf16[7,128,256]{2,1,0:T(8,128)(2,1)S(1)}, bf16[7,128,256]{2,1,0:T(8,128)(2,1)S(1)}, u32[]{:S(2)}, u32[]{:S(2)}) collective-permute-start(bf16[7,128,256]{2,1,0:T(8,128)(2,1)S(1)} %get-tuple-element.63), channel_id=1, source_target_pairs={{0,16},{4,20},{8,24},{12,28},{1,17},{5,21},{9,25},{13,29},{2,18},{... | collective-permute-start | bytes 1376264 | tf_op jit(solution)/shard_map/ppermute | solution.py:506
  21.5 1.9 %collective-permute-start.6 = (bf16[5,128,256]{2,1,0:T(8,128)(2,1)S(1)}, bf16[5,128,256]{2,1,0:T(8,128)(2,1)S(1)}, u32[]{:S(2)}, u32[]{:S(2)}) collective-permute-start(bf16[5,128,256]{2,1,0:T(8,128)(2,1)S(1)} %get-tuple-element.66), channel_id=1, source_target_pairs={{0,8},{4,12},{16,24},{20,28},{24,16},{28,20},{1,9},{5,13},{17,25},... | collective-permute-start | bytes 983048 | tf_op jit(solution)/shard_map/ppermute | solution.py:506
  23.4 2.1 %collective-permute-done.4.got.refs_2_ = bf16[5,128,256]{2,1,0:T(8,128)(2,1)S(1)} collective-permute-done((bf16[5,128,256]{2,1,0:T(8,128)(2,1)S(1)}, bf16[5,128,256]{2,1,0:T(8,128)(2,1)S(1)}, u32[]{:S(2)}, u32[]{:S(2)}) %collective-permute-start.4) | collective-permute-done | bytes 327712 | tf_op jit(solution)/shard_map/ppermute | solution.py:491
  25.7 1.5 %collective-permute-start.8 = (bf16[5,128,256]{2,1,0:T(8,128)(2,1)S(1)}, bf16[5,128,256]{2,1,0:T(8,128)(2,1)S(1)}, u32[]{:S(2)}, u32[]{:S(2)}) collective-permute-start(bf16[5,128,256]{2,1,0:T(8,128)(2,1)S(1)} %get-tuple-element.75), channel_id=1, source_target_pairs={{0,16},{4,20},{8,24},{12,28},{1,17},{5,21},{9,25},{13,29},{2,18},{... | collective-permute-start | bytes 983048 | tf_op jit(solution)/shard_map/ppermute | solution.py:506
  27.2 4.7 %collective-permute-done.5.refs_3_ = bf16[7,128,256]{2,1,0:T(8,128)(2,1)S(1)} collective-permute-done((bf16[7,128,256]{2,1,0:T(8,128)(2,1)S(1)}, bf16[7,128,256]{2,1,0:T(8,128)(2,1)S(1)}, u32[]{:S(2)}, u32[]{:S(2)}) %collective-permute-start.5) | collective-permute-done | bytes 458784 | tf_op jit(solution)/shard_map/ppermute | solution.py:506
  31.9 2.2 %output.4 = (bf16[5,128,256]{2,1,0:T(8,128)(2,1)S(1)}, bf16[5,128,256]{2,1,0:T(8,128)(2,1)S(1)}, bf16[2,2,128,256]{3,2,1,0:T(8,128)(2,1)S(1)}, bf16[2,2,128,256]...) custom-call(f32[32,128]{1,0:T(8,128)S(1)} %get-tuple-element.62.refs_0_, ...), custom_call_target="tpu_custom_call" | custom-call | flops 1 | bytes 1 | tf_op jit(solution)/shard_map/output/pallas_call | solution.py:402
  34.0 5.5 %collective-permute-start.7 = (bf16[2,128,256]{2,1,0:T(8,128)(2,1)S(1)}, bf16[2,128,256]{2,1,0:T(8,128)(2,1)S(1)}, u32[]{:S(2)}, u32[]{:S(2)}) collective-permute-start(bf16[2,128,256]{2,1,0:T(8,128)(2,1)S(1)} %get-tuple-element.73), channel_id=1, source_target_pairs={{0,4},{4,0},{8,12},{12,8},{16,20},{20,16},{24,28},{28,24},{1,5},{5... | collective-permute-start | bytes 393224 | tf_op jit(solution)/shard_map/ppermute | solution.py:544
  39.5 2.6 %output.5 = (bf16[10,128,256]{2,1,0:T(8,128)(2,1)S(1)}, bf16[5,128,256]{2,1,0:T(8,128)(2,1)S(1)}, bf16[32,128,256]{2,1,0:T(8,128)(2,1)}, bf16[2,2,128,256]{3,2,1,0:T(8,128)(2,1)S(1)}, f32[32,128]{1,0:T(8,128)S(1)}) custom-call(f32[32,128]{1,0:T(8,128)S(1)} %get-tuple-element.65.refs_0_, bf16[3,768,256]{2,1,0:T(8,128)(2,1)S(1)} %bitcast.7, ...), custom_call_target="tpu_custom_call" | custom-call | flops 1 | bytes 1 | tf_op jit(solution)/shard_map/output/pallas_call | solution.py:402
  42.2 0.5 %rim.1 = (bf16[2,128,256]{2,1,0:T(8,128)(2,1)S(1)}, f32[32,128]{1,0:T(8,128)S(1)}) custom-call(f32[32,128]{1,0:T(8,128)S(1)} %get-tuple-element.71.tab, bf16[3,768,256]{2,1,0:T(8,128)(2,1)S(1)} %bitcast.8, bf16[2,2,128,256]{3,2,1,0:T(8,128)(2,1)S(1)} %get-tuple-element.72.near, bf16[2,128,256]{2,1,0:T(8,128)(2,1)S(1)} %collective-permute-done.7.far, ...), custom_call_target="tpu_custom_call" | custom-call | flops 1 | bytes 1 | tf_op jit(solution)/shard_map/rim/pallas_call | solution.py:433
  42.8 1.2 %output.6 = (bf16[6,128,256]{2,1,0:T(8,128)(2,1)S(1)}, f32[32,128]{1,0:T(8,128)S(1)}) custom-call(f32[32,128]{1,0:T(8,128)S(1)} %get-tuple-element.74.refs_0_, bf16[3,768,256]{2,1,0:T(8,128)(2,1)S(1)} %bitcast.9, bf16[5,128,256]{2,1,0:T(8,128)(2,1)S(1)} %collective-permute-done.4.got.refs_2_, bf16[5,128,256]{2,1,0:T(8,128)(2,1)S(1)} %collective-permute-done.8.refs_3_, ...), custom_call_target="tpu_custom_call" | custom-call | flops 4000000000 | bytes 1 | tf_op jit(solution)/shard_map/output/pallas_call | solution.py:402
  44.0 0.5 %collective-permute-start.9 = (bf16[6,128,256]{2,1,0:T(8,128)(2,1)S(1)}, bf16[6,128,256]{2,1,0:T(8,128)(2,1)S(1)}, u32[]{:S(2)}, u32[]{:S(2)}) collective-permute-start(bf16[6,128,256]{2,1,0:T(8,128)(2,1)S(1)} %get-tuple-element.80), channel_id=1, source_target_pairs={{0,4},{4,0},{8,12},{12,8},{16,20},{20,16},{24,28},{28,24},{1,5},{5... | collective-permute-start | bytes 1179656 | tf_op jit(solution)/shard_map/ppermute | solution.py:556
  44.5 1.6 %output.7 = (bf16[5,128,256]{2,1,0:T(8,128)(2,1)S(1)}, bf16[32,128,256]{2,1,0:T(8,128)(2,1)}) custom-call(f32[32,128]{1,0:T(8,128)S(1)} %get-tuple-element.81.refs_0_, bf16[3,768,256]{2,1,0:T(8,128)(2,1)S(1)} %bitcast.10, bf16[5,128,256]{2,1,0:T(8,128)(2,1)S(1)} %collective-permute-done.4.got.refs_2_, ...), custom_call_target="tpu_custom_call", output_to_operand_aliasing={{1}: (11, {})} | custom-call | flops 1 | bytes 1 | tf_op jit(solution)/shard_map/output/pallas_call | solution.py:402
  46.2 1.2 %place.1 = bf16[32,128,256]{2,1,0:T(8,128)(2,1)} custom-call(bf16[6,128,256]{2,1,0:T(8,128)(2,1)S(1)} %collective-permute-done.9.parcel, bf16[5,128,256]{2,1,0:T(8,128)(2,1)S(1)} %get-tuple-element.84.block, bf16[2,128,256]{2,1,0:T(8,128)(2,1)S(1)} %get-tuple-element.79.refs_9_.rim, ...), custom_call_target="tpu_custom_call", output_to_operand_aliasing={{}: (4, {})} | custom-call | tf_op jit(solution)/shard_map/place/pallas_call | solution.py:461
  (14 shorter events, 0.8 us)
Async XLA Ops:
  0.0 4.7 %collective-permute-start = (bf16[32,128,256]{2,1,0:T(8,128)(2,1)}, bf16[32,128,256]{2,1,0:T(8,128)(2,1)S(1)}, u32[]{:S(2)}, u32[]{:S(2)}) collective-permute-start(bf16[32,128,256]{2,1,0:T(8,128)(2,1)} %bitcast.11), channel_id=1, source_target_pairs={{0,4},{4,0},{8,12},{12,8},{16,20},{20,16},{24,28},{28,24},{1,5},{5... | collective-permute-start | bytes 6291464 | tf_op jit(solution)/shard_map/ppermute | solution.py:517
  6.0 13.6 %collective-permute-start.2 = (bf16[7,128,256]{2,1,0:T(8,128)(2,1)S(1)}, bf16[7,128,256]{2,1,0:T(8,128)(2,1)S(1)}, u32[]{:S(2)}, u32[]{:S(2)}) collective-permute-start(bf16[7,128,256]{2,1,0:T(8,128)(2,1)S(1)} %get-tuple-element.57.pair), channel_id=1, source_target_pairs={{0,8},{4,12},{8,0},{12,4},{16,24},{20,28},{1,9},{5,13},{9,1},{13,5... | collective-permute-start | bytes 1376264 | tf_op jit(solution)/shard_map/ppermute | solution.py:491
  7.3 3.0 %collective-permute-start.1 = (bf16[2,2,128,256]{3,2,1,0:T(8,128)(2,1)S(1)}, bf16[2,2,128,256]{3,2,1,0:T(8,128)(2,1)S(1)}, u32[]{:S(2)}, u32[]{:S(2)}) collective-permute-start(bf16[2,2,128,256]{3,2,1,0:T(8,128)(2,1)S(1)} %get-tuple-element.55), channel_id=1, source_target_pairs={{4,1},{5,2},{6,3},{1,4},{2,5},{3,6},{12,9},{13,10},{14,11},{9,12},... | collective-permute-start | bytes 786440 | tf_op jit(solution)/shard_map/ppermute | solution.py:532
  9.1 12.2 %collective-permute-start.3 = (bf16[5,128,256]{2,1,0:T(8,128)(2,1)S(1)}, bf16[5,128,256]{2,1,0:T(8,128)(2,1)S(1)}, u32[]{:S(2)}, u32[]{:S(2)}) collective-permute-start(bf16[5,128,256]{2,1,0:T(8,128)(2,1)S(1)} %get-tuple-element.59.pair), channel_id=1, source_target_pairs={{0,16},{4,20},{8,24},{12,28},{1,17},{5,21},{9,25},{13,29},{2,18},{... | collective-permute-start | bytes 983048 | tf_op jit(solution)/shard_map/ppermute | solution.py:491
  12.2 19.7 %copy-start = (bf16[3,3,256,256]{3,2,1,0:T(8,128)(2,1)S(1)}, bf16[3,3,256,256]{3,2,1,0:T(8,128)(2,1)}, u32[]{:S(2)}) copy-start(bf16[3,3,256,256]{3,2,1,0:T(8,128)(2,1)} %param.9) | copy-start | bytes 3538948
  12.2 13.3 %collective-permute-start.4 = (bf16[5,128,256]{2,1,0:T(8,128)(2,1)S(1)}, bf16[5,128,256]{2,1,0:T(8,128)(2,1)S(1)}, u32[]{:S(2)}, u32[]{:S(2)}) collective-permute-start(bf16[5,128,256]{2,1,0:T(8,128)(2,1)S(1)} %get-tuple-element.61.pair), channel_id=1, source_target_pairs={{0,8},{4,12},{8,0},{12,4},{16,24},{20,28},{1,9},{5,13},{9,1},{13,5... | collective-permute-start | bytes 983048 | tf_op jit(solution)/shard_map/ppermute | solution.py:491
  20.0 11.9 %collective-permute-start.5 = (bf16[7,128,256]{2,1,0:T(8,128)(2,1)S(1)}, bf16[7,128,256]{2,1,0:T(8,128)(2,1)S(1)}, u32[]{:S(2)}, u32[]{:S(2)}) collective-permute-start(bf16[7,128,256]{2,1,0:T(8,128)(2,1)S(1)} %get-tuple-element.63), channel_id=1, source_target_pairs={{0,16},{4,20},{8,24},{12,28},{1,17},{5,21},{9,25},{13,29},{2,18},{... | collective-permute-start | bytes 1376264 | tf_op jit(solution)/shard_map/ppermute | solution.py:506
  21.5 18.1 %collective-permute-start.6 = (bf16[5,128,256]{2,1,0:T(8,128)(2,1)S(1)}, bf16[5,128,256]{2,1,0:T(8,128)(2,1)S(1)}, u32[]{:S(2)}, u32[]{:S(2)}) collective-permute-start(bf16[5,128,256]{2,1,0:T(8,128)(2,1)S(1)} %get-tuple-element.66), channel_id=1, source_target_pairs={{0,8},{4,12},{16,24},{20,28},{24,16},{28,20},{1,9},{5,13},{17,25},... | collective-permute-start | bytes 983048 | tf_op jit(solution)/shard_map/ppermute | solution.py:506
  25.7 17.1 %collective-permute-start.8 = (bf16[5,128,256]{2,1,0:T(8,128)(2,1)S(1)}, bf16[5,128,256]{2,1,0:T(8,128)(2,1)S(1)}, u32[]{:S(2)}, u32[]{:S(2)}) collective-permute-start(bf16[5,128,256]{2,1,0:T(8,128)(2,1)S(1)} %get-tuple-element.75), channel_id=1, source_target_pairs={{0,16},{4,20},{8,24},{12,28},{1,17},{5,21},{9,25},{13,29},{2,18},{... | collective-permute-start | bytes 983048 | tf_op jit(solution)/shard_map/ppermute | solution.py:506
  34.0 8.2 %collective-permute-start.7 = (bf16[2,128,256]{2,1,0:T(8,128)(2,1)S(1)}, bf16[2,128,256]{2,1,0:T(8,128)(2,1)S(1)}, u32[]{:S(2)}, u32[]{:S(2)}) collective-permute-start(bf16[2,128,256]{2,1,0:T(8,128)(2,1)S(1)} %get-tuple-element.73), channel_id=1, source_target_pairs={{0,4},{4,0},{8,12},{12,8},{16,20},{20,16},{24,28},{28,24},{1,5},{5... | collective-permute-start | bytes 393224 | tf_op jit(solution)/shard_map/ppermute | solution.py:544
  42.1 4.0 %collective-permute-start.10 = (bf16[10,128,256]{2,1,0:T(8,128)(2,1)S(1)}, bf16[10,128,256]{2,1,0:T(8,128)(2,1)S(1)}, u32[]{:S(2)}, u32[]{:S(2)}) collective-permute-start(bf16[10,128,256]{2,1,0:T(8,128)(2,1)S(1)} %get-tuple-element.85), channel_id=1, source_target_pairs={{0,4},{4,0},{8,12},{12,8},{16,20},{20,16},{24,28},{28,24},{1,5},{5... | collective-permute-start | bytes 1966088 | tf_op jit(solution)/shard_map/ppermute | solution.py:549
  44.0 2.2 %collective-permute-start.9 = (bf16[6,128,256]{2,1,0:T(8,128)(2,1)S(1)}, bf16[6,128,256]{2,1,0:T(8,128)(2,1)S(1)}, u32[]{:S(2)}, u32[]{:S(2)}) collective-permute-start(bf16[6,128,256]{2,1,0:T(8,128)(2,1)S(1)} %get-tuple-element.80), channel_id=1, source_target_pairs={{0,4},{4,0},{8,12},{12,8},{16,20},{20,16},{24,28},{28,24},{1,5},{5... | collective-permute-start | bytes 1179656 | tf_op jit(solution)/shard_map/ppermute | solution.py:556
